TPU v7x, 32 devices: a whole 2x2x4 slice. The times are simulated.
32 devices in a mesh: sec: 2 (over y), gx: 2 (over x), gy: 8 (over z, core).
Axes of the slice: x: 2, y: 2, z: 4, core: 2. Of those that a mesh axis runs over, the one named last changes fastest.
Arguments:
- state: float32 [2, 3, 2, 8, 102400], P('sec', None, 'gx', 'gy'), may hold values from -6 to 6
- previous: float32 [2, 3, 2, 8, 102400], P('sec', None, 'gx', 'gy'), may hold values from -6 to 6
- coeff: float32 [2, 2, 2, 8, 102400], P('sec', None, 'gx', 'gy'), may hold values from 0.04 to 0.16
- wet_mask: int32 [2, 8, 102400], P('gx', 'gy'), may hold values 0 or 1
- link_dest: int32 [2, 2, 8, 32, 1], P('sec', 'gx', 'gy'), may hold values from 0 to 15; in each aligned block of 32 rows (0 to 31, 32 to 63, ..., all dimensions but the last counted through in order) at most 4 rows name the same one
- link_rows: int32 [2, 2, 8, 32, 2], P('sec', 'gx', 'gy'), may hold values from 0 to 79, as said below
- link_weight: float32 [2, 2, 8, 32], P('sec', 'gx', 'gy'), may hold values from 0.5 to 2
Outputs:
- final_state: float32 [2, 3, 2, 8, 102400], P('sec', None, 'gx', 'gy')
Inputs may be any that keep to these rules, and one draw needn't show every extreme that they name: `link_rows`: in section 0, [..., 0] lies below 8 and [..., 1] below 80; in section 1, [..., 0] lies below 80 and [..., 1] below 8. `link_dest`: among the 32 links of one device at most 4 name the same owner.
All inputs are finite; a program needn't handle non-finite values. No bound on the sum of `wet_mask` on one device may be relied on, other than what follows from the above.
Results may differ from a plain program's by a relative error of at most 0.0001.
Values sent between devices are 32-bit elements; how exact they have to be, the bound alone decides.
No kernel may reach another device: no remote copies, remote signals or barrier semaphores. Data moves between devices by JAX's collectives and lax.ppermute only.
A program may use at most 128 MiB of HBM per device.

v0:
```python
import functools

import jax
import jax.numpy as jnp
from jax import lax
from jax.experimental import pallas as pl
from jax.experimental.pallas import tpu as pltpu
from jax.sharding import PartitionSpec as P

CX = 8
CY = 128
REFINE = 10
NL = 100
STEPS = 4
CAP = 4
FINE = REFINE * CX
ROWS = CX * NL
FIRST = 104
TOTAL = FIRST + ROWS + FIRST
SLOTS = 8
GROUP = 200
BLOCKS = GROUP // 8
F32 = jnp.float32


def split(x):
    high = x.astype(jnp.bfloat16)
    rest = x - high.astype(F32)
    middle = rest.astype(jnp.bfloat16)
    low = (rest - middle.astype(F32)).astype(jnp.bfloat16)
    return high, middle, low


def pick(mask, x):
    parts = jnp.concatenate(split(x), axis=1)
    wide = jnp.dot(mask.astype(jnp.bfloat16), parts, preferred_element_type=F32)
    width = x.shape[1]
    return wide[:, 0:width] + (wide[:, width : 2 * width] + wide[:, 2 * width :])


def spread(x, mask):
    rows = x.shape[0]
    tall = jnp.dot(jnp.concatenate(split(x), axis=0), mask, preferred_element_type=F32)
    return tall[0:rows] + (tall[rows : 2 * rows] + tall[2 * rows :])


def iota(shape, dim):
    return lax.broadcasted_iota(jnp.int32, shape, dim)


def one(mask):
    return jnp.where(mask, 1.0, 0.0).astype(F32)


def place():
    return lax.axis_index("sec"), lax.axis_index("gx"), lax.axis_index("gy")


def average(rows_of):
    total = jnp.zeros((FINE, CY), F32)
    for m in range(REFINE):
        fine = iota((CY, CY), 0) + m * CY
        first = iota((CY, CY), 1) * REFINE
        mask = one((fine >= first) & (fine < first + REFINE)).astype(jnp.bfloat16)
        total = total + spread(rows_of(m), mask)
    return total / REFINE


def surface(section, elastic, sheet, surf):
    surf[...] = jnp.zeros_like(surf)

    @pl.when(section == 0)
    def _():
        surf[0:CX] = elastic[pl.ds(0, CX, stride=NL)]

    @pl.when(section != 0)
    def _():
        surf[0:FINE] = average(lambda m: sheet[pl.ds(m, FINE, stride=REFINE)])


def source_pick(cols):
    return one(cols[0] == iota((cols.shape[1], CY), 1).astype(F32))


def outgoing(section, tiles, cols, pcat, payload):
    half = payload.shape[0] // 2
    lanes = tiles.shape
    last = jnp.broadcast_to(tiles[:, CY - 1 : CY], lanes) * cols[1]
    first = jnp.broadcast_to(tiles[:, 0:1], lanes) * cols[1]
    packed = pick(pcat[...], jnp.concatenate([tiles, last, first, cols[3]], axis=0))
    payload[pl.ds(pl.multiple_of(section * half, 8), half)] = jnp.zeros((half, CY), F32)
    payload[pl.ds(pl.multiple_of((1 - section) * half, 8), half)] = packed


def link_tables(section, me, n_gy, dest, rows, weight, lines, cols, pcat):
    links = dest.shape[1]
    lines[...] = jnp.zeros_like(lines)
    lines[0:1, 0:links] = dest[...].astype(F32)
    lines[1:3, 0:links] = rows[...].astype(F32)
    lines[3:4, 0:links] = weight[...]
    x = lines[...]
    eye = one(iota((links, CY), 0) == iota((links, CY), 1))

    def column(i):
        return jnp.sum(eye * x[i : i + 1], axis=1, keepdims=True)

    target, source, landing, weights = [column(i) for i in range(4)]
    same = one(target == x[0:1])
    at = iota((links, CY), 0)
    other = iota((links, CY), 1)
    inside = one(other < links)
    slot_row = jnp.sum(same * one(at < other) * inside, axis=0, keepdims=True)
    slot = jnp.sum(same * one(other < at) * inside, axis=1, keepdims=True)
    lane = other.astype(F32)
    cols[0] = jnp.broadcast_to(source, (links, CY))
    cols[1] = one(landing == lane)
    cols[2] = jnp.broadcast_to(weights, (links, CY))
    cols[3] = landing * one(lane == slot + (me * SLOTS).astype(F32))
    y = jnp.concatenate([x[0:3], slot_row, jnp.zeros((4, CY), F32)], axis=0)
    y = y + pltpu.roll(y, links, 1) + pltpu.roll(y, 2 * links, 1) + pltpu.roll(y, 3 * links, 1)
    shape = (pcat.shape[0], CY)
    owner = iota(shape, 0) >> 3
    part = iota(shape, 0) & 7
    group = iota(shape, 1) >> (links.bit_length() - 1)
    to = y[0:1]
    row = y[2:3]
    order = y[3:4]
    beside = jnp.where(owner < n_gy, owner + n_gy, owner - n_gy).astype(F32)
    bottom = jnp.where(section == 0, FINE - 1, CX - 1).astype(F32)
    edge = jnp.where(owner < n_gy, 0.0, bottom)
    along = owner & (n_gy - 1)
    own = owner.astype(F32)
    chosen = one((group == 0) & (part == order.astype(jnp.int32)) & (part < CAP) & (to == own))
    chosen += one((group == 0) & (part == 4) & (to == beside) & (row == edge))
    chosen += one((group == 1) & (part == 6) & (to == own - 1.0) & (along > 0))
    chosen += one((group == 2) & (part == 7) & (to == own + 1.0) & (along < n_gy - 1))
    chosen += one((group == 3) & (part == 5) & (to == own))
    pcat[...] = chosen


def collect(acc, value, j, lane):
    return jnp.where(lane >> 1 == j, pltpu.roll(value, 2 * j + 1, 1), acc)


def merge(it, acc, sides):
    for c, value in acc.items():
        sides[c, it >> 1] += pltpu.roll(value, (it & 1) * 2 * BLOCKS, 1)


def take_edges(section, p, fields, wet, xs):
    start = pl.multiple_of(jnp.where(p == 0, ROWS - FIRST, 0), 8)
    for c in range(3):
        xs[c] = fields[c, pl.ds(start, FIRST)]

    @pl.when(section != 0)
    def _():
        xs[2] = wet[pl.ds(start, FIRST)].astype(F32)


def load_kernel(n_gy, state, previous, wet, dest, rows, weight, payload, cols, pcat, cur, prev, xs, sides, scale, wet_in, dest_in, rows_in, weight_in, lines, surf, sem):
    section, p, q = place()
    pairs = [(dest, dest_in), (rows, rows_in), (weight, weight_in)]
    pairs += [(state.at[c], cur.at[c]) for c in (2, 0, 1)]
    pairs += [(wet, wet_in), (previous, prev)]
    copies = [pltpu.make_async_copy(a, b, sem.at[i]) for i, (a, b) in enumerate(pairs)]
    for copy in copies:
        copy.start()
    sides[...] = jnp.zeros_like(sides)
    for copy in copies[0:3]:
        copy.wait()
    link_tables(section, p * n_gy + q, n_gy, dest_in, rows_in, weight_in, lines, cols, pcat)
    for copy in copies[3:7]:
        copy.wait()
    surface(section, cur.at[2], cur.at[0], surf)
    tiles = cols[2] * pick(source_pick(cols), surf[...])
    outgoing(section, tiles, cols, pcat, payload)
    lane = iota((8, CY), 1)

    def pack(it, carry):
        acc = {c: jnp.zeros((8, CY), F32) for c in range(3)}
        views = [cur.at[c, group_rows(it, GROUP)] for c in range(3)]
        wets = wet_in.at[group_rows(it, GROUP)]
        for j in range(BLOCKS):
            at = slice(8 * j, 8 * j + 8)
            for c in range(3):
                value = views[c][at]
                if c == 1:
                    value = jnp.where(section == 0, value, wets[at].astype(F32))
                acc[c] = collect(acc[c], value, j, lane)
        merge(it, acc, sides)
        return carry

    lax.fori_loop(0, ROWS // GROUP, pack, 0)
    take_edges(section, p, cur, wet_in, xs)
    scale[...] = cols[2]

    @pl.when(section != 0)
    def _():
        surf[0:FINE] = average(lambda m: wet_in[pl.ds(m, FINE, stride=REFINE)].astype(F32))
        scale[...] = cols[2] * pick(source_pick(cols), surf[...])

    copies[7].wait()


def group_rows(it, rows):
    return pl.ds(pl.multiple_of(it * GROUP, 8), rows)


def arrived_rows(section, received):
    half = received.shape[0] // 2
    return received[pl.ds(pl.multiple_of((1 - section) * half, 8), half)]


def arrived_sums(arrived):
    return jnp.sum(arrived.reshape(-1, SLOTS, CY), axis=0)


def landed(arrived, sums):
    mine = iota((CY, arrived.shape[0]), 1)
    return pick(one((iota(mine.shape, 0).astype(F32) == sums[5:6]) & ((mine & 7) < CAP)), arrived)


def route_kernel(received, base, scale, cols, pcat, payload):
    section, _, _ = place()
    arrived = arrived_rows(section, received)
    landing = arrived_sums(arrived)[5:6]
    lane = iota(cols.shape[1:], 1)
    gather = one((cols[0] == landing) & ((lane & 7) < CAP))
    tiles = base[...] + scale[...] * pick(gather, arrived)
    outgoing(section, tiles, cols, pcat, payload)


def edge_addends(sums, period, offset):
    masks, values = [], []
    lane = iota((CY, 2 * CY), 1)
    block = ((lane & (CY - 1)) >> 1) + jnp.where(lane >= CY, 2 * BLOCKS, 0)
    inside = (lane & (CY - 1)) < 4 * BLOCKS
    for side, shift in ((0, 0), (1, offset)):
        at = iota(lane.shape, 0) * period + shift - block * 8
        masks.append(one((at >= 0) & (at < 8) & ((lane & 1) == side) & inside).astype(jnp.bfloat16))
        sub = (iota((16, CY), 1) * period + shift) & 7
        row = jnp.broadcast_to(sums[6 + side : 7 + side], (16, CY))
        values.append(jnp.where(sub == iota((16, CY), 0), row, 0.0))
    wide = spread(values[0], masks[0]) + spread(values[1], masks[1])
    return wide[0:8, 0:CY], wide[0:8, CY:]


def align_sides(zs, c, lane, sub):
    first, second = zs[c, 0], zs[c, 1]
    top = 4 * BLOCKS
    low_first = jnp.where(lane == top - 2, pltpu.roll(second, top - 2, 1), pltpu.roll(first, CY - 2, 1))
    low_second = pltpu.roll(second, CY - 2, 1)
    high_first = pltpu.roll(first, 2, 1)
    high_second = jnp.where(lane == 1, pltpu.roll(first, CY + 2 - top, 1), pltpu.roll(second, 2, 1))
    for h, (low, high) in enumerate(((low_first, high_first), (low_second, high_second))):
        zs[c, h] = jnp.where(lane & 1 == 0, pltpu.roll(low, 7, 0), pltpu.roll(high, 1, 0))


def step_kernel(linked, last, *refs):
    cur_in, prev_in, coeff, wet, cols, xr, yra, yrb, mine, *refs = refs
    if linked:
        received, *refs = refs
    cur, prev, *refs = refs
    if last:
        out, zs, full, co, wet_in, sem = refs
    else:
        base, xs, sides, zs, full, co, wet_in, sem, surf = refs
    section, p, q = place()
    lane = iota((8, CY), 1)
    sub = iota((8, CY), 0)
    zero = jnp.zeros((8, CY), F32)
    even_lane = lane & 1 == 0
    loads = [pltpu.make_async_copy(coeff, co, sem.at[0]), pltpu.make_async_copy(wet, wet_in, sem.at[1])]
    for load in loads:
        load.start()

    @pl.when((q & 1) == 1)
    def _():
        for c in range(3):
            for h in range(2):
                zs[c, h] = jnp.where(even_lane, yra[c, h], yrb[c, h])

    @pl.when((q & 1) == 0)
    def _():
        for c in range(3):
            for h in range(2):
                zs[c, h] = jnp.where(even_lane, yrb[c, h], yra[c, h])

    there = pl.multiple_of(jnp.where(p == 0, FIRST + ROWS, 0), 8)
    nowhere = pl.multiple_of(jnp.where(p == 0, 0, FIRST + ROWS), 8)
    for c in range(3):
        full[c, pl.ds(there, FIRST)] = xr[c]
        full[c, pl.ds(nowhere, FIRST)] = jnp.zeros((FIRST, CY), F32)

    if linked:
        arrived = arrived_rows(section, received)
        sums = arrived_sums(arrived)
        addend = landed(arrived, sums)
    if not last:
        sides[...] = jnp.zeros_like(sides)

    def widen(it, carry):
        for c in range(3):
            view = full.at[c, group_rows(it, FIRST + GROUP)]
            view[FIRST : FIRST + GROUP] = cur[c, group_rows(it, GROUP)]
        return carry

    def views_of(it, ref):
        return [ref.at[c, group_rows(it, GROUP)] for c in range(ref.shape[0])]

    def padded_of(it):
        return [full.at[c, group_rows(it, GROUP + 2 * FIRST)] for c in range(3)]

    @pl.when(section == 0)
    def _():
        if linked:
            for x in range(CX):
                cur[2, NL * x : NL * x + 1] += addend[x : x + 1]

            @pl.when(p == 0)
            def _():
                full[2, FIRST + ROWS : FIRST + ROWS + 1] += sums[4:5]

            @pl.when(p != 0)
            def _():
                full[2, FIRST - NL : FIRST - NL + 1] += sums[4:5]

            for h, value in enumerate(edge_addends(sums, NL, 0)):
                zs[2, h] += value

        lax.fori_loop(0, ROWS // GROUP, widen, 0)
        for load in loads:
            load.wait()

        def group(it, carry):
            turn = (CY - (it & 1) * 2 * BLOCKS) & (CY - 1)
            halos = [pltpu.roll(zs[c, it >> 1], turn, 1) for c in range(3)]
            acc = {c: zero for c in range(3)}
            fields, old, new_fields, factors = padded_of(it), views_of(it, prev_in), views_of(it, prev), views_of(it, co)
            for j in range(BLOCKS):
                at = slice(8 * j, 8 * j + 8)
                mu = factors[0][at]
                stiff = factors[1][at] + 2.0 * mu
                for c in range(3):

                    def near(rows):
                        return fields[c][FIRST + 8 * j + rows : FIRST + 8 * j + rows + 8]

                    v = near(0)
                    twice = 2.0 * v
                    above = near(-1)
                    below = near(1)
                    for row in (0, NL):
                        if 8 * j <= row < 8 * j + 8:
                            above = jnp.where(sub == row - 8 * j, 0.0, above)
                    for row in (NL - 1, GROUP - 1):
                        if 8 * j <= row < 8 * j + 8:
                            below = jnp.where(sub == row - 8 * j, 0.0, below)
                    halo = pltpu.roll(halos[c], CY - 1 - 2 * j, 1)
                    low = jnp.where(lane == CY - 1, halo, v)
                    high = jnp.where(lane == 0, halo, v)
                    along_first = near(-NL) + near(NL) - twice
                    along_depth = above + below - twice
                    along_second = pltpu.roll(low, 1, 1) + pltpu.roll(high, CY - 1, 1) - twice
                    if c == 0:
                        force = stiff * along_first + mu * (along_depth + along_second)
                    elif c == 1:
                        force = stiff * along_second + mu * (along_first + along_depth)
                    else:
                        force = stiff * along_depth + mu * (along_first + along_second)
                    new = twice - old[c][at] + force
                    new_fields[c][at] = new
                    if not last:
                        acc[c] = collect(acc[c], new, j, lane)
            if not last:
                merge(it, acc, sides)
            return carry

        lax.fori_loop(0, ROWS // GROUP, group, 0)

    @pl.when(section != 0)
    def _():
        for c in range(3):
            align_sides(zs, c, lane, sub)
        if linked:
            for h, value in enumerate(edge_addends(sums, REFINE, REFINE - 1)):
                zs[0, h] += zs[1, h] * value
            beside = jnp.broadcast_to(sums[4:5], (8, CY))
            fine_row = jnp.concatenate(
                [
                    jnp.take_along_axis(beside, (((sub + m) * CY + lane) * 6554) >> 16, axis=1)
                    for m in (0, 2)
                ],
                axis=0,
            )

            def add_edge(first):
                for start, rows in ((0, fine_row[0:8]), (8, fine_row[14:16])):
                    at = slice(first + start, first + start + rows.shape[0])
                    full[0, at] += full[2, at] * rows

            @pl.when(p == 0)
            def _():
                add_edge(FIRST + ROWS)

            @pl.when(p != 0)
            def _():
                add_edge(FIRST - REFINE)

        for load in loads:
            load.wait()
        if linked:
            for start, fine in fine_addend(addend):
                at = pl.ds(start, 8, stride=REFINE)
                cur[0, at] += wet_in[at].astype(F32) * fine
        lax.fori_loop(0, ROWS // GROUP, widen, 0)

        def group(it, carry):
            turn = (CY - (it & 1) * 2 * BLOCKS) & (CY - 1)
            halos = {c: pltpu.roll(zs[c, it >> 1], turn, 1) for c in (0, 2)}
            acc = {0: zero, 2: zero}
            fields, old, new_fields, factors = padded_of(it), views_of(it, prev_in), views_of(it, prev), views_of(it, co)
            wets = wet_in.at[group_rows(it, GROUP)]
            for j in range(BLOCKS):
                at = slice(8 * j, 8 * j + 8)
                a = factors[0][at]
                b = factors[1][at]
                w = wets[at].astype(F32)

                def near(c, rows):
                    return fields[c][FIRST + 8 * j + rows : FIRST + 8 * j + rows + 8]

                def across(c):
                    v = near(c, 0)
                    low = jnp.where(lane == CY - 1, near(c, -1), v)
                    high = jnp.where(lane == 0, near(c, 1), v)
                    halo = pltpu.roll(halos[c], CY - 1 - 2 * j, 1)
                    for s in range(8):
                        if (8 * j + s) % REFINE == 0:
                            low = jnp.where((lane == CY - 1) & (sub == s), halo, low)
                        if (8 * j + s) % REFINE == REFINE - 1:
                            high = jnp.where((lane == 0) & (sub == s), halo, high)
                    return pltpu.roll(high, CY - 1, 1) - pltpu.roll(low, 1, 1)

                def down(c):
                    return near(c, REFINE) - near(c, -REFINE)

                first_flux = w * (old[1][at] - a * down(0))
                second_flux = w * (old[2][at] - a * across(0))
                height = w * (old[0][at] - b * (down(1) + across(2)))
                new_fields[0][at] = height
                new_fields[1][at] = first_flux
                new_fields[2][at] = second_flux
                if not last:
                    acc[0] = collect(acc[0], height, j, lane)
                    acc[2] = collect(acc[2], second_flux, j, lane)
            if not last:
                merge(it, acc, sides)
            return carry

        lax.fori_loop(0, ROWS // GROUP, group, 0)
        if not last:
            sides[1] = mine[1]

    if last:
        copy = pltpu.make_async_copy(prev, out, sem.at[0])
        copy.start()
        copy.wait()
    else:
        take_edges(section, p, prev, wet_in, xs)
        surface(section, prev.at[2], prev.at[0], surf)
        base[...] = cols[2] * pick(source_pick(cols), surf[...])


def fine_addend(addend):
    lane = iota((8, CY), 1)
    for m in range(FINE // 8):
        rows = addend[8 * m : 8 * m + 8]
        for k in range(REFINE):
            fine = jnp.take_along_axis(rows, ((lane + k * CY) * 6554) >> 16, axis=1)
            yield 8 * REFINE * m + k, fine


def last_kernel(final_in, fields, wet, received, final, height, wet_in, load_sem, sem):
    section, _, _ = place()
    load = pltpu.make_async_copy(wet, wet_in, load_sem)
    load.start()
    arrived = arrived_rows(section, received)
    addend = landed(arrived, arrived_sums(arrived))
    load.wait()

    @pl.when(section == 0)
    def _():
        copies = []
        for x in range(CX):
            row = NL * x
            first = row // 8 * 8
            height[8 * x : 8 * x + 8] = fields[2, first : first + 8]
            at = 8 * x + row - first
            height[at : at + 1] += addend[x : x + 1]
            copies.append(
                pltpu.make_async_copy(
                    height.at[8 * x : 8 * x + 8], final.at[2, pl.ds(first, 8)], sem.at[x]
                )
            )
        for copy in copies:
            copy.start()
        for copy in copies:
            copy.wait()

    @pl.when(section != 0)
    def _():
        for start, fine in fine_addend(addend):
            at = pl.ds(start, 8, stride=REFINE)
            height[at] = fields[0, at] + wet_in[at].astype(F32) * fine
        copy = pltpu.make_async_copy(height, final.at[0], sem.at[0])
        copy.start()
        copy.wait()


def call(kernel, operands, outs, scratch=(), aliases=None, any_inputs=(), any_outs=(), limit=12, cost=4):
    vmem = pl.BlockSpec(memory_space=pltpu.VMEM)
    anywhere = pl.BlockSpec(memory_space=pl.ANY)
    return pl.pallas_call(
        kernel,
        out_shape=[
            (pltpu.VMEM if kept else jax.ShapeDtypeStruct)(shape, kind[0] if kind else F32)
            for shape, kept, *kind in outs
        ],
        in_specs=[anywhere if i in any_inputs else vmem for i in range(len(operands))],
        out_specs=[anywhere if i in any_outs else vmem for i in range(len(outs))],
        scratch_shapes=list(scratch),
        input_output_aliases=aliases or {},
        compiler_params=pltpu.CompilerParams(vmem_limit_bytes=limit * 1024 * 1024),
        cost_estimate=pl.CostEstimate(flops=cost * 10**9, bytes_accessed=cost * 1024 * 1024, transcendentals=0),
    )(*operands)


def keep(value):
    return pltpu.with_memory_space_constraint(value, pltpu.VMEM)


def outside(value):
    return pltpu.with_memory_space_constraint(value, pltpu.HBM)


def on_device(n_gy, owners, state, previous, coeff, wet_mask, link_dest, link_rows, link_weight):
    links = link_weight.size
    pairs = 2 * owners * SLOTS
    vmem = pltpu.VMEM
    dma = pltpu.SemaphoreType.DMA
    field_shape = (3, ROWS, CY)
    sides_shape = (3, 2, 8, CY)
    fields = (field_shape, True)
    edges = ((3, FIRST, CY), False)
    sides_out = (sides_shape, False)
    tiles = ((links, CY), True)
    surf = vmem((CY, CY), F32)
    wet_in = vmem((ROWS, CY), jnp.int32)
    state, previous = state.reshape(field_shape), previous.reshape(field_shape)
    coeff, wet = outside(coeff.reshape(2, ROWS, CY)), outside(wet_mask.reshape(ROWS, CY))

    def exchange(payload):
        payload = payload.reshape(2 * owners, SLOTS, CY)
        payload = lax.all_to_all(payload, ("sec", "gx", "gy"), 0, 0, tiled=True)
        return payload.reshape(pairs, CY)

    dest, rows, weight = link_dest.reshape(1, links), link_rows.reshape(links, 2).T, link_weight.reshape(1, links)
    payload, cols, pcat, cur, prev, xs, sides, scale = call(
        functools.partial(load_kernel, n_gy),
        [outside(x) for x in (state, previous, wet, dest, rows, weight)],
        [
            ((pairs, CY), False), ((4, links, CY), True), ((owners * SLOTS, CY), True), fields, fields,
            edges, sides_out, tiles,
        ],
        [
            wet_in, vmem((1, links), jnp.int32), vmem((2, links), jnp.int32),
            vmem((1, links), F32), vmem((8, CY), F32), surf, dma((8,)),
        ],
        any_inputs=range(6),
    )
    received = exchange(payload)
    swap = [(0, 1), (1, 0)]
    inner = [(i, i ^ 1) for i in range(n_gy)]
    outer = [(i, j) for k in range(1, n_gy - 1, 2) for i, j in ((k, k + 1), (k + 1, k))]
    before = None
    for step in range(STEPS):
        last = step == STEPS - 1
        xr = lax.ppermute(xs, "gx", swap)
        yra = lax.ppermute(sides, "gy", inner)
        yrb = lax.ppermute(sides, "gy", outer)
        operands = [keep(cur), keep(prev), coeff, wet, keep(cols), xr, yra, yrb, sides]
        if before is not None:
            operands.append(before)
        kernel = functools.partial(step_kernel, before is not None, last)
        scratch = [vmem(sides_shape, F32), vmem((3, TOTAL, CY), F32), vmem((2, ROWS, CY), F32), wet_in, dma((2,))]
        more = dict(aliases={0: 0, 1: 1}, any_inputs=(2, 3), cost=64)
        if last:
            _, new, final = call(
                kernel, operands, [fields, fields, (field_shape, False)], scratch, any_outs=(2,), **more
            )
        else:
            cur, prev, base, xs, sides = call(
                kernel, operands, [fields, fields, tiles, edges, sides_out], scratch + [surf], **more
            )
            cur, prev = prev, cur
            payload = call(
                route_kernel, (received, keep(base), keep(scale), keep(cols), keep(pcat)),
                [((pairs, CY), False)], limit=4,
            )[0]
            before = received
            received = exchange(payload)
    final = call(
        last_kernel,
        (outside(final), keep(new), wet, received),
        [(field_shape, False)],
        [vmem((ROWS, CY), F32), wet_in, dma, dma((CX,))],
        aliases={0: 0}, any_inputs=(0, 2), any_outs=(0,),
    )[0]
    return final.reshape(1, 3, 1, 1, -1)


def from_partner(value, axis, stride):
    return lax.ppermute(value, axis, [(i, i ^ 1 << stride) for i in range(lax.axis_size(axis))])


def with_halo(block, sides, width):
    for axis, dim in sides:
        count = lax.axis_size(axis)
        forward = [(i, i + 1) for i in range(count - 1)]
        backward = [(target, source) for source, target in forward]
        low = lax.ppermute(
            lax.slice_in_dim(block, block.shape[dim] - width, None, axis=dim), axis, forward
        )
        high = lax.ppermute(lax.slice_in_dim(block, 0, width, axis=dim), axis, backward)
        block = jnp.concatenate([low, block, high], axis=dim)
    return block


def elastic_update(padded, current, previous_field, shear_modulus, lame_first, surface_force):
    own_axis = (0, 2, 1)
    stiffness = lame_first + 2.0 * shear_modulus
    updated_list = []
    for component in range(3):
        displaced = current[component]
        extended = padded[component]
        along_first = extended[2:, :, 1:-1] - 2.0 * displaced + extended[:-2, :, 1:-1]
        deeper = jnp.pad(displaced, ((0, 0), (1, 1), (0, 0)))
        along_depth = deeper[:, 2:, :] - 2.0 * displaced + deeper[:, :-2, :]
        along_second = extended[1:-1, :, 2:] - 2.0 * displaced + extended[1:-1, :, :-2]
        factors = [
            stiffness if own_axis[component] == axis_index else shear_modulus
            for axis_index in range(3)
        ]
        acceleration = (
            factors[0] * along_first + factors[1] * along_depth + factors[2] * along_second
        )
        updated = 2.0 * displaced - previous_field[component] + acceleration
        if component == 2:
            updated = updated.at[:, 0, :].add(surface_force)
        updated_list.append(updated)
    return jnp.stack(updated_list)


def shallow_update(padded, current, previous_field, wave_factor, area_factor, wetness, source):
    fine_rows = REFINE * CX
    fine_cols = REFINE * CY
    sheet = current.reshape(3, fine_rows, fine_cols)
    earlier_sheet = previous_field.reshape(3, fine_rows, fine_cols)
    above = padded[:, 0, (REFINE - 1) * REFINE :, 1:-1].reshape(3, 1, fine_cols)
    below = padded[:, -1, :REFINE, 1:-1].reshape(3, 1, fine_cols)
    left_side = padded[:, 1:-1, REFINE - 1 :: REFINE, 0].reshape(3, fine_rows, 1)
    right_side = padded[:, 1:-1, 0::REFINE, -1].reshape(3, fine_rows, 1)
    by_rows = jnp.concatenate([above, sheet, below], axis=1)
    by_columns = jnp.concatenate([left_side, sheet, right_side], axis=2)

    def rows_diff(channel):
        return by_rows[channel, 2:, :] - by_rows[channel, :-2, :]

    def columns_diff(channel):
        return by_columns[channel, :, 2:] - by_columns[channel, :, :-2]

    flux_first = wetness * (earlier_sheet[1] - wave_factor * rows_diff(0))
    flux_second = wetness * (earlier_sheet[2] - wave_factor * columns_diff(0))
    height = wetness * (earlier_sheet[0] - area_factor * (rows_diff(1) + columns_diff(2)) + source)
    return jnp.stack([height, flux_first, flux_second]).reshape(3, CX, NL, CY)


def route(payload):
    tile_data, tile_rows = payload
    width = tile_data.shape[-1]
    received_data, received_rows = (
        lax.all_to_all(tile_data, ("gx", "gy"), split_axis=0, concat_axis=0, tiled=True),
        lax.all_to_all(tile_rows, ("gx", "gy"), split_axis=0, concat_axis=0, tiled=True),
    )
    return (received_data.reshape(-1, width), received_rows.reshape(-1))


def deliver(outgoing, send_rows):
    crossed = from_partner((outgoing, send_rows), "sec", 0)
    return route(crossed)


def general_on_device(state, previous, coeff, wet_mask, link_dest, link_rows, link_weight):
    section = lax.axis_index("sec")
    owners = lax.axis_size("gx") * lax.axis_size("gy")
    fine_rows = REFINE * CX
    fine_cols = REFINE * CY
    current = state[0, :, 0, 0].reshape(3, CX, NL, CY)
    earlier = previous[0, :, 0, 0].reshape(3, CX, NL, CY)
    first_factor = coeff[0, 0, 0, 0]
    second_factor = coeff[0, 1, 0, 0]
    wetness = wet_mask[0, 0].reshape(fine_rows, fine_cols).astype(jnp.float32)
    targets = link_dest.reshape(-1)
    pairs = link_rows.reshape(-1, 2)
    source_rows = pairs[:, 0]
    landing = pairs[:, 1]
    weights = link_weight.reshape(-1)
    one_hot = (targets[:, None] == jnp.arange(owners, dtype=jnp.int32)[None, :]).astype(jnp.int32)
    before = jnp.cumsum(one_hot, axis=0) - one_hot
    slot_index = jnp.sum(before * one_hot, axis=1)
    position = targets * CAP + slot_index
    send_rows = jnp.zeros((owners * CAP,), jnp.int32).at[position].set(landing).reshape(owners, CAP)
    for step_index in range(STEPS):
        padded = with_halo(current, (("gx", 1), ("gy", 3)), 1)

        def elastic_rows():
            return current[2, :, 0, :][source_rows]

        def shallow_rows():
            picked_fine = current[0].reshape(fine_rows, fine_cols)[source_rows]
            return jnp.sum(picked_fine.reshape(-1, CY, REFINE), axis=-1) / REFINE

        picked = lax.cond(section == 0, elastic_rows, shallow_rows)
        outgoing = (
            jnp.zeros((owners * CAP, CY), jnp.float32).at[position].set(picked * weights[:, None])
        )
        outgoing = outgoing.reshape(owners, CAP, CY)
        arrived, arrived_rows = deliver(outgoing, send_rows)

        def elastic_branch():
            surface_force = jnp.zeros((CX, CY), jnp.float32).at[arrived_rows].add(arrived)
            return elastic_update(
                padded,
                current,
                earlier,
                first_factor.reshape(CX, NL, CY),
                second_factor.reshape(CX, NL, CY),
                surface_force,
            )

        def shallow_branch():
            coarse_source = jnp.zeros((fine_rows, CY), jnp.float32).at[arrived_rows].add(arrived)
            source = jnp.repeat(coarse_source, REFINE, axis=1)
            return shallow_update(
                padded,
                current,
                earlier,
                first_factor.reshape(fine_rows, fine_cols),
                second_factor.reshape(fine_rows, fine_cols),
                wetness,
                source,
            )

        updated = lax.cond(section == 0, elastic_branch, shallow_branch)
        earlier, current = (current, updated)
    return current.reshape(1, 3, 1, 1, -1)


def solution(mesh):
    placed = (
        P("sec", None, "gx", "gy", None),
        P("sec", None, "gx", "gy", None),
        P("sec", None, "gx", "gy", None),
        P("gx", "gy", None),
        P("sec", "gx", "gy", None, None),
        P("sec", "gx", "gy", None, None),
        P("sec", "gx", "gy", None),
    )
    n_gx, n_gy = mesh.shape["gx"], mesh.shape["gy"]
    owners = n_gx * n_gy
    device_program = general_on_device
    if n_gx == 2 and n_gy & (n_gy - 1) == 0 and owners * SLOTS == CY:
        device_program = functools.partial(on_device, n_gy, owners)
    return jax.shard_map(
        device_program,
        mesh=mesh,
        in_specs=placed,
        out_specs=P("sec", None, "gx", "gy", None),
        check_vma=False,
    )
```

profile of v0, /device:TPU:0, one launch (start us, length us, event | category | flops | bytes accessed | tf_op | source)
XLA Modules:
  0.0 71.9 jit_solution(5000491238988894622)
XLA Ops:
  0.0 3.4 %shard_map.73 = (f32[256,128]{1,0:T(8,128)}, f32[4,32,128]{2,1,0:T(8,128)S(1)}, f32[128,128]{1,0:T(8,128)S(1)}, f32[3,800,128]{2,1,0:T(8,128)S(1)}, f32[3,800,12...) custom-call(f32[3,800,128]{2,1,0:T(8,128)} %bitcast.25, ...), custom_call_target="tpu_custom_call" | custom-call | flops 4000000000 | bytes 4194304 | tf_op jit(solution)/shard_map/pallas_call | solution.py:524
  3.4 3.0 %collective-permute-start = (f32[3,104,128]{2,1,0:T(8,128)S(1)}, f32[3,104,128]{2,1,0:T(8,128)S(1)}, u32[]{:S(2)}, u32[]{:S(2)}) collective-permute-start(f32[3,104,128]{2,1,0:T(8,128)S(1)} %get-tuple-element.33), channel_id=1, source_target_pairs={{0,8},{8,0},{1,9},{9,1},{2,10},{10,2},{3,11},{11,3},{4,12},{12,4},... | collective-permute-start | bytes 479240 | tf_op jit(solution)/shard_map/ppermute | solution.py:589
  6.5 0.0 collective-permute-start.1
  6.5 0.7 collective-permute-start.2
  7.1 7.9 %all-to-all-start = ((f32[32,8,128]{2,1,0:T(8,128)}), f32[32,8,128]{2,1,0:T(8,128)S(1)}, u32[]{:S(2)}, u32[]{:S(2)}) async-start(f32[32,8,128]{2,1,0:T(8,128)} %bitcast.8), calls=%async_computation | async-start | bytes 262144 | tf_op jit(solution)/shard_map/all_to_all | solution.py:565
  15.0 0.0 collective-permute-done.1.refs_6_
  15.0 0.0 collective-permute-done.2.refs_7_
  15.0 0.0 collective-permute-done.refs_5_
  15.0 6.3 %shard_map.74 = (f32[3,800,128]{2,1,0:T(8,128)S(1)}, f32[3,800,128]{2,1,0:T(8,128)S(1)}, f32[32,128]{1,0:T(8,128)S(1)}, f32[3,104,128]{2,1,0:T(8,128)S(1)}, f32[3,2,8,128]{3,2,1,0:T(8,128)S(1)}) custom-call(f32[3,800,128]{2,1,0:T(8,128)S(1)} %get-tuple-element.30.refs_0_, ...), custom_call_target="tpu_custom_call", output_to_operand_aliasing={{0}: (0, {}), {1}: (1, {})} | custom-call | flops 64000000000 | bytes 67108864 | tf_op jit(solution)/shard_map/pallas_call | solution.py:524
  21.3 0.3 collective-permute-start.4
  21.6 0.7 collective-permute-start.5
  22.3 1.7 %collective-permute-start.3 = (f32[3,104,128]{2,1,0:T(8,128)S(1)}, f32[3,104,128]{2,1,0:T(8,128)S(1)}, u32[]{:S(2)}, u32[]{:S(2)}) collective-permute-start(f32[3,104,128]{2,1,0:T(8,128)S(1)} %get-tuple-element.37), channel_id=1, source_target_pairs={{0,8},{8,0},{1,9},{9,1},{2,10},{10,2},{3,11},{11,3},{4,12},{12,4},... | collective-permute-start | bytes 479240 | tf_op jit(solution)/shard_map/ppermute | solution.py:589
  24.0 0.0 all-to-all-done
  24.0 1.0 %shard_map.76 = f32[256,128]{1,0:T(8,128)} custom-call(f32[256,128]{1,0:T(8,128)S(1)} %bitcast.22, f32[32,128]{1,0:T(8,128)S(1)} %get-tuple-element.44.base, f32[32,128]{1,0:T(8,128)S(1)} %get-tuple-element.45.scale, f32[4,32,128]{2,1,0:T(8,128)S(1)} %get-tuple-element.32.refs_4_.cols, f32[128,128]{1,0:T(8,128)S(1)} %get-tuple-element.46.pcat), custom_call_target="tpu_custom_call" | custom-call | flops 4000000000 | bytes 4194304 | tf_op jit(solution)/shard_map/pallas_call | solution.py:524
  25.1 5.4 %all-to-all-start.1 = ((f32[32,8,128]{2,1,0:T(8,128)}), f32[32,8,128]{2,1,0:T(8,128)S(1)}, u32[]{:S(2)}, u32[]{:S(2)}) async-start(f32[32,8,128]{2,1,0:T(8,128)} %bitcast.10), calls=%async_computation.1 | async-start | bytes 262144 | tf_op jit(solution)/shard_map/all_to_all | solution.py:565
  30.5 0.0 collective-permute-done.4.refs_6_
  30.5 0.0 collective-permute-done.5.refs_7_
  30.5 0.0 collective-permute-done.3.refs_5_
  30.5 6.3 %shard_map.75 = (f32[3,800,128]{2,1,0:T(8,128)S(1)}, f32[3,800,128]{2,1,0:T(8,128)S(1)}, f32[32,128]{1,0:T(8,128)S(1)}, f32[3,104,128]{2,1,0:T(8,128)S(1)}, f32[3,2,8,128]{3,2,1,0:T(8,128)S(1)}) custom-call(f32[3,800,128]{2,1,0:T(8,128)S(1)} %get-tuple-element.35.refs_0_, ...), custom_call_target="tpu_custom_call", output_to_operand_aliasing={{0}: (0, {}), {1}: (1, {})} | custom-call | flops 64000000000 | bytes 67108864 | tf_op jit(solution)/shard_map/pallas_call | solution.py:524
  36.8 0.3 collective-permute-start.7
  37.1 0.7 collective-permute-start.8
  37.8 1.7 %collective-permute-start.6 = (f32[3,104,128]{2,1,0:T(8,128)S(1)}, f32[3,104,128]{2,1,0:T(8,128)S(1)}, u32[]{:S(2)}, u32[]{:S(2)}) collective-permute-start(f32[3,104,128]{2,1,0:T(8,128)S(1)} %get-tuple-element.42), channel_id=1, source_target_pairs={{0,8},{8,0},{1,9},{9,1},{2,10},{10,2},{3,11},{11,3},{4,12},{12,4},... | collective-permute-start | bytes 479240 | tf_op jit(solution)/shard_map/ppermute | solution.py:589
  39.5 0.0 all-to-all-done.1
  39.5 1.0 %shard_map.78 = f32[256,128]{1,0:T(8,128)} custom-call(f32[256,128]{1,0:T(8,128)S(1)} %bitcast.20, f32[32,128]{1,0:T(8,128)S(1)} %get-tuple-element.51.base, f32[32,128]{1,0:T(8,128)S(1)} %get-tuple-element.45.scale, f32[4,32,128]{2,1,0:T(8,128)S(1)} %get-tuple-element.32.refs_4_.cols, f32[128,128]{1,0:T(8,128)S(1)} %get-tuple-element.46.pcat), custom_call_target="tpu_custom_call" | custom-call | flops 4000000000 | bytes 4194304 | tf_op jit(solution)/shard_map/pallas_call | solution.py:524
  40.5 5.8 %all-to-all-start.2 = ((f32[32,8,128]{2,1,0:T(8,128)}), f32[32,8,128]{2,1,0:T(8,128)S(1)}, u32[]{:S(2)}, u32[]{:S(2)}) async-start(f32[32,8,128]{2,1,0:T(8,128)} %bitcast.12), calls=%async_computation.2 | async-start | bytes 262144 | tf_op jit(solution)/shard_map/all_to_all | solution.py:565
  46.3 0.0 collective-permute-done.7.refs_6_
  46.3 0.0 collective-permute-done.8.refs_7_
  46.3 0.0 collective-permute-done.6.refs_5_
  46.3 6.3 %shard_map.77 = (f32[3,800,128]{2,1,0:T(8,128)S(1)}, f32[3,800,128]{2,1,0:T(8,128)S(1)}, f32[32,128]{1,0:T(8,128)S(1)}, f32[3,104,128]{2,1,0:T(8,128)S(1)}, f32[3,2,8,128]{3,2,1,0:T(8,128)S(1)}) custom-call(f32[3,800,128]{2,1,0:T(8,128)S(1)} %get-tuple-element.40.refs_0_, ...), custom_call_target="tpu_custom_call", output_to_operand_aliasing={{0}: (0, {}), {1}: (1, {})} | custom-call | flops 64000000000 | bytes 67108864 | tf_op jit(solution)/shard_map/pallas_call | solution.py:524
  52.6 0.3 collective-permute-start.10
  52.9 0.7 collective-permute-start.11
  53.6 1.7 %collective-permute-start.9 = (f32[3,104,128]{2,1,0:T(8,128)S(1)}, f32[3,104,128]{2,1,0:T(8,128)S(1)}, u32[]{:S(2)}, u32[]{:S(2)}) collective-permute-start(f32[3,104,128]{2,1,0:T(8,128)S(1)} %get-tuple-element.49), channel_id=1, source_target_pairs={{0,8},{8,0},{1,9},{9,1},{2,10},{10,2},{3,11},{11,3},{4,12},{12,4},... | collective-permute-start | bytes 479240 | tf_op jit(solution)/shard_map/ppermute | solution.py:589
  55.3 0.0 all-to-all-done.2
  55.3 1.0 %shard_map.80 = f32[256,128]{1,0:T(8,128)} custom-call(f32[256,128]{1,0:T(8,128)S(1)} %bitcast.18, f32[32,128]{1,0:T(8,128)S(1)} %get-tuple-element.54.base, f32[32,128]{1,0:T(8,128)S(1)} %get-tuple-element.45.scale, f32[4,32,128]{2,1,0:T(8,128)S(1)} %get-tuple-element.32.refs_4_.cols, f32[128,128]{1,0:T(8,128)S(1)} %get-tuple-element.46.pcat), custom_call_target="tpu_custom_call" | custom-call | flops 4000000000 | bytes 4194304 | tf_op jit(solution)/shard_map/pallas_call | solution.py:524
  56.4 5.7 %all-to-all-start.3 = ((f32[32,8,128]{2,1,0:T(8,128)}), f32[32,8,128]{2,1,0:T(8,128)S(1)}, u32[]{:S(2)}, u32[]{:S(2)}) async-start(f32[32,8,128]{2,1,0:T(8,128)} %bitcast.14), calls=%async_computation.3 | async-start | bytes 262144 | tf_op jit(solution)/shard_map/all_to_all | solution.py:565
  62.0 0.0 collective-permute-done.10.refs_6_
  62.1 0.0 collective-permute-done.11.refs_7_
  62.1 0.0 collective-permute-done.9.refs_5_
  62.1 6.5 %shard_map.79 = (f32[3,800,128]{2,1,0:T(8,128)S(1)}, f32[3,800,128]{2,1,0:T(8,128)S(1)}, f32[3,800,128]{2,1,0:T(8,128)}) custom-call(f32[3,800,128]{2,1,0:T(8,128)S(1)} %get-tuple-element.47.refs_0_, f32[3,800,128]{2,1,0:T(8,128)S(1)} %get-tuple-element.48.refs_1_, f32[2,800,128]{2,1,0:T(8,128)} %bitcast.30, ...), custom_call_target="tpu_custom_call", output_to_operand_aliasing={{0}: (0, {}), {1}: (1, {})} | custom-call | flops 64000000000 | bytes 67108864 | tf_op jit(solution)/shard_map/pallas_call | solution.py:524
  68.6 1.6 %all-to-all-done.3 = f32[32,8,128]{2,1,0:T(8,128)S(1)} async-done(((f32[32,8,128]{2,1,0:T(8,128)}), f32[32,8,128]{2,1,0:T(8,128)S(1)}, u32[]{:S(2)}, u32[]{:S(2)}) %all-to-all-start.3) | async-done | bytes 131104 | tf_op jit(solution)/shard_map/all_to_all | solution.py:565
  70.2 1.7 %shard_map.81 = f32[3,800,128]{2,1,0:T(8,128)} custom-call(f32[3,800,128]{2,1,0:T(8,128)} %get-tuple-element.52.final_in, f32[3,800,128]{2,1,0:T(8,128)S(1)} %get-tuple-element.53.fields, s32[800,128]{1,0:T(8,128)} %bitcast.36, f32[256,128]{1,0:T(8,128)S(1)} %bitcast.24), custom_call_target="tpu_custom_call", output_to_operand_aliasing={{}: (0, {})} | custom-call | flops 4000000000 | bytes 4194304 | tf_op jit(solution)/shard_map/pallas_call | solution.py:524
Async XLA Ops:
  3.4 11.6 %collective-permute-start = (f32[3,104,128]{2,1,0:T(8,128)S(1)}, f32[3,104,128]{2,1,0:T(8,128)S(1)}, u32[]{:S(2)}, u32[]{:S(2)}) collective-permute-start(f32[3,104,128]{2,1,0:T(8,128)S(1)} %get-tuple-element.33), channel_id=1, source_target_pairs={{0,8},{8,0},{1,9},{9,1},{2,10},{10,2},{3,11},{11,3},{4,12},{12,4},... | collective-permute-start | bytes 479240 | tf_op jit(solution)/shard_map/ppermute | solution.py:589
  6.5 8.5 %collective-permute-start.1 = (f32[3,2,8,128]{3,2,1,0:T(8,128)S(1)}, f32[3,2,8,128]{3,2,1,0:T(8,128)S(1)}, u32[]{:S(2)}, u32[]{:S(2)}) collective-permute-start(f32[3,2,8,128]{3,2,1,0:T(8,128)S(1)} %get-tuple-element.34.refs_8_), channel_id=1, source_target_pairs={{0,1},{1,0},{2,3},{3,2},{4,5},{5,4},{6,7},{7,6},{8,9},{9,8},{10,11... | collective-permute-start | bytes 73736 | tf_op jit(solution)/shard_map/ppermute | solution.py:590
  6.5 8.6 %collective-permute-start.2 = (f32[3,2,8,128]{3,2,1,0:T(8,128)S(1)}, f32[3,2,8,128]{3,2,1,0:T(8,128)S(1)}, u32[]{:S(2)}, u32[]{:S(2)}) collective-permute-start(f32[3,2,8,128]{3,2,1,0:T(8,128)S(1)} %get-tuple-element.34.refs_8_), channel_id=1, source_target_pairs={{1,2},{2,1},{3,4},{4,3},{5,6},{6,5},{9,10},{10,9},{11,12},{12,11},... | collective-permute-start | bytes 73736 | tf_op jit(solution)/shard_map/ppermute | solution.py:591
  7.1 16.9 %all-to-all-start = ((f32[32,8,128]{2,1,0:T(8,128)}), f32[32,8,128]{2,1,0:T(8,128)S(1)}, u32[]{:S(2)}, u32[]{:S(2)}) async-start(f32[32,8,128]{2,1,0:T(8,128)} %bitcast.8), calls=%async_computation | async-start | bytes 262144 | tf_op jit(solution)/shard_map/all_to_all | solution.py:565
  21.3 9.2 %collective-permute-start.4 = (f32[3,2,8,128]{3,2,1,0:T(8,128)S(1)}, f32[3,2,8,128]{3,2,1,0:T(8,128)S(1)}, u32[]{:S(2)}, u32[]{:S(2)}) collective-permute-start(f32[3,2,8,128]{3,2,1,0:T(8,128)S(1)} %get-tuple-element.38.refs_8_), channel_id=1, source_target_pairs={{0,1},{1,0},{2,3},{3,2},{4,5},{5,4},{6,7},{7,6},{8,9},{9,8},{10,11... | collective-permute-start | bytes 73736 | tf_op jit(solution)/shard_map/ppermute | solution.py:590
  21.6 8.9 %collective-permute-start.5 = (f32[3,2,8,128]{3,2,1,0:T(8,128)S(1)}, f32[3,2,8,128]{3,2,1,0:T(8,128)S(1)}, u32[]{:S(2)}, u32[]{:S(2)}) collective-permute-start(f32[3,2,8,128]{3,2,1,0:T(8,128)S(1)} %get-tuple-element.38.refs_8_), channel_id=1, source_target_pairs={{1,2},{2,1},{3,4},{4,3},{5,6},{6,5},{9,10},{10,9},{11,12},{12,11},... | collective-permute-start | bytes 73736 | tf_op jit(solution)/shard_map/ppermute | solution.py:591
  22.3 8.2 %collective-permute-start.3 = (f32[3,104,128]{2,1,0:T(8,128)S(1)}, f32[3,104,128]{2,1,0:T(8,128)S(1)}, u32[]{:S(2)}, u32[]{:S(2)}) collective-permute-start(f32[3,104,128]{2,1,0:T(8,128)S(1)} %get-tuple-element.37), channel_id=1, source_target_pairs={{0,8},{8,0},{1,9},{9,1},{2,10},{10,2},{3,11},{11,3},{4,12},{12,4},... | collective-permute-start | bytes 479240 | tf_op jit(solution)/shard_map/ppermute | solution.py:589
  25.1 14.4 %all-to-all-start.1 = ((f32[32,8,128]{2,1,0:T(8,128)}), f32[32,8,128]{2,1,0:T(8,128)S(1)}, u32[]{:S(2)}, u32[]{:S(2)}) async-start(f32[32,8,128]{2,1,0:T(8,128)} %bitcast.10), calls=%async_computation.1 | async-start | bytes 262144 | tf_op jit(solution)/shard_map/all_to_all | solution.py:565
  36.8 9.5 %collective-permute-start.7 = (f32[3,2,8,128]{3,2,1,0:T(8,128)S(1)}, f32[3,2,8,128]{3,2,1,0:T(8,128)S(1)}, u32[]{:S(2)}, u32[]{:S(2)}) collective-permute-start(f32[3,2,8,128]{3,2,1,0:T(8,128)S(1)} %get-tuple-element.43.refs_8_), channel_id=1, source_target_pairs={{0,1},{1,0},{2,3},{3,2},{4,5},{5,4},{6,7},{7,6},{8,9},{9,8},{10,11... | collective-permute-start | bytes 73736 | tf_op jit(solution)/shard_map/ppermute | solution.py:590
  37.1 9.2 %collective-permute-start.8 = (f32[3,2,8,128]{3,2,1,0:T(8,128)S(1)}, f32[3,2,8,128]{3,2,1,0:T(8,128)S(1)}, u32[]{:S(2)}, u32[]{:S(2)}) collective-permute-start(f32[3,2,8,128]{3,2,1,0:T(8,128)S(1)} %get-tuple-element.43.refs_8_), channel_id=1, source_target_pairs={{1,2},{2,1},{3,4},{4,3},{5,6},{6,5},{9,10},{10,9},{11,12},{12,11},... | collective-permute-start | bytes 73736 | tf_op jit(solution)/shard_map/ppermute | solution.py:591
  37.8 8.6 %collective-permute-start.6 = (f32[3,104,128]{2,1,0:T(8,128)S(1)}, f32[3,104,128]{2,1,0:T(8,128)S(1)}, u32[]{:S(2)}, u32[]{:S(2)}) collective-permute-start(f32[3,104,128]{2,1,0:T(8,128)S(1)} %get-tuple-element.42), channel_id=1, source_target_pairs={{0,8},{8,0},{1,9},{9,1},{2,10},{10,2},{3,11},{11,3},{4,12},{12,4},... | collective-permute-start | bytes 479240 | tf_op jit(solution)/shard_map/ppermute | solution.py:589
  40.5 14.8 %all-to-all-start.2 = ((f32[32,8,128]{2,1,0:T(8,128)}), f32[32,8,128]{2,1,0:T(8,128)S(1)}, u32[]{:S(2)}, u32[]{:S(2)}) async-start(f32[32,8,128]{2,1,0:T(8,128)} %bitcast.12), calls=%async_computation.2 | async-start | bytes 262144 | tf_op jit(solution)/shard_map/all_to_all | solution.py:565
  52.6 9.4 %collective-permute-start.10 = (f32[3,2,8,128]{3,2,1,0:T(8,128)S(1)}, f32[3,2,8,128]{3,2,1,0:T(8,128)S(1)}, u32[]{:S(2)}, u32[]{:S(2)}) collective-permute-start(f32[3,2,8,128]{3,2,1,0:T(8,128)S(1)} %get-tuple-element.50.refs_8_), channel_id=1, source_target_pairs={{0,1},{1,0},{2,3},{3,2},{4,5},{5,4},{6,7},{7,6},{8,9},{9,8},{10,11... | collective-permute-start | bytes 73736 | tf_op jit(solution)/shard_map/ppermute | solution.py:590
  52.9 9.1 %collective-permute-start.11 = (f32[3,2,8,128]{3,2,1,0:T(8,128)S(1)}, f32[3,2,8,128]{3,2,1,0:T(8,128)S(1)}, u32[]{:S(2)}, u32[]{:S(2)}) collective-permute-start(f32[3,2,8,128]{3,2,1,0:T(8,128)S(1)} %get-tuple-element.50.refs_8_), channel_id=1, source_target_pairs={{1,2},{2,1},{3,4},{4,3},{5,6},{6,5},{9,10},{10,9},{11,12},{12,11},... | collective-permute-start | bytes 73736 | tf_op jit(solution)/shard_map/ppermute | solution.py:591
  53.6 8.5 %collective-permute-start.9 = (f32[3,104,128]{2,1,0:T(8,128)S(1)}, f32[3,104,128]{2,1,0:T(8,128)S(1)}, u32[]{:S(2)}, u32[]{:S(2)}) collective-permute-start(f32[3,104,128]{2,1,0:T(8,128)S(1)} %get-tuple-element.49), channel_id=1, source_target_pairs={{0,8},{8,0},{1,9},{9,1},{2,10},{10,2},{3,11},{11,3},{4,12},{12,4},... | collective-permute-start | bytes 479240 | tf_op jit(solution)/shard_map/ppermute | solution.py:589
  56.4 13.9 %all-to-all-start.3 = ((f32[32,8,128]{2,1,0:T(8,128)}), f32[32,8,128]{2,1,0:T(8,128)S(1)}, u32[]{:S(2)}, u32[]{:S(2)}) async-start(f32[32,8,128]{2,1,0:T(8,128)} %bitcast.14), calls=%async_computation.3 | async-start | bytes 262144 | tf_op jit(solution)/shard_map/all_to_all | solution.py:565
where the time goes:
time: 72.5 us; the launch traced here: 71.9 us
  starting transfers between devices  36.5 us (50%)
  Pallas kernels  33.6 us (46%)
  waiting for transfers between devices  1.63 us (2%)
    pallas_call x9, Pallas kernels, call(): pl.pallas_call(kernel, out_shape=[(pltpu.VMEM if kept else jax.ShapeDtype...  33.6 us
    all_to_all x4, starting transfers between devices, exchange(): payload = lax.all_to_all(payload, ('sec', 'gx', 'gy'), 0, 0, tiled=True)  24.7 us
    ppermute x4, starting transfers between devices, on_device(): xr = lax.ppermute(xs, 'gx', swap)  8.2 us
    ppermute x4, starting transfers between devices, on_device(): yrb = lax.ppermute(sides, 'gy', outer)  2.6 us
    all_to_all x4, waiting for transfers between devices, exchange(): payload = lax.all_to_all(payload, ('sec', 'gx', 'gy'), 0, 0, tiled=True)  1.6 us
  transfers between devices with their start and end apart: 16, of which 1 were waited for; matrix products, arithmetic and copies ran while one was open for 0% of the time, Pallas kernels for 40%

commit v1 on v0

--- a/solution.py
+++ b/solution.py
@@ -18,30 +18,27 @@
 FIRST = 104
 TOTAL = FIRST + ROWS + FIRST
 SLOTS = 8
-GROUP = 200
-BLOCKS = GROUP // 8
+BLOCKS = 20
+BATCH = 4
+GROUP = 8 * BLOCKS
+HALF = ROWS // 16
 F32 = jnp.float32
 
 
 def split(x):
     high = x.astype(jnp.bfloat16)
-    rest = x - high.astype(F32)
-    middle = rest.astype(jnp.bfloat16)
-    low = (rest - middle.astype(F32)).astype(jnp.bfloat16)
-    return high, middle, low
+    return high, (x - high.astype(F32)).astype(jnp.bfloat16)
 
 
 def pick(mask, x):
     parts = jnp.concatenate(split(x), axis=1)
     wide = jnp.dot(mask.astype(jnp.bfloat16), parts, preferred_element_type=F32)
-    width = x.shape[1]
-    return wide[:, 0:width] + (wide[:, width : 2 * width] + wide[:, 2 * width :])
+    return wide[:, 0 : x.shape[1]] + wide[:, x.shape[1] :]
 
 
 def spread(x, mask):
-    rows = x.shape[0]
     tall = jnp.dot(jnp.concatenate(split(x), axis=0), mask, preferred_element_type=F32)
-    return tall[0:rows] + (tall[rows : 2 * rows] + tall[2 * rows :])
+    return tall[0 : x.shape[0]] + tall[x.shape[0] :]
 
 
 def iota(shape, dim):
@@ -138,13 +135,33 @@
     pcat[...] = chosen
 
 
-def collect(acc, value, j, lane):
-    return jnp.where(lane >> 1 == j, pltpu.roll(value, 2 * j + 1, 1), acc)
-
-
-def merge(it, acc, sides):
-    for c, value in acc.items():
-        sides[c, it >> 1] += pltpu.roll(value, (it & 1) * 2 * BLOCKS, 1)
+def pack_sides(values_of, sides, channels):
+    lane = iota((8, CY), 1)
+
+    def half_of(h, carry):
+        acc = {c: jnp.zeros((8, CY), F32) for c in channels}
+        views = {c: values_of(c, pl.ds(pl.multiple_of(h * HALF * 8, 8), HALF * 8)) for c in channels}
+        for b in range(HALF):
+            for c in channels:
+                value = views[c][8 * b : 8 * b + 8].astype(F32)
+                acc[c] = jnp.where(lane >> 1 == b, pltpu.roll(value, 2 * b + 1, 1), acc[c])
+        for c in channels:
+            sides[c, h] = acc[c]
+        return carry
+
+    lax.fori_loop(0, 2, half_of, 0)
+
+
+def unpack_sides(zs, halos, channels):
+    def half_of(h, carry):
+        for i, c in enumerate(channels):
+            value = zs[c, h]
+            view = halos.at[i, pl.ds(pl.multiple_of(h * HALF * 8, 8), HALF * 8)]
+            for b in range(HALF):
+                view[8 * b : 8 * b + 8] = pltpu.roll(value, CY - 1 - 2 * b, 1)
+        return carry
+
+    lax.fori_loop(0, 2, half_of, 0)
 
 
 def take_edges(section, p, fields, wet, xs):
@@ -165,7 +182,6 @@
     copies = [pltpu.make_async_copy(a, b, sem.at[i]) for i, (a, b) in enumerate(pairs)]
     for copy in copies:
         copy.start()
-    sides[...] = jnp.zeros_like(sides)
     for copy in copies[0:3]:
         copy.wait()
     link_tables(section, p * n_gy + q, n_gy, dest_in, rows_in, weight_in, lines, cols, pcat)
@@ -174,23 +190,15 @@
     surface(section, cur.at[2], cur.at[0], surf)
     tiles = cols[2] * pick(source_pick(cols), surf[...])
     outgoing(section, tiles, cols, pcat, payload)
-    lane = iota((8, CY), 1)
-
-    def pack(it, carry):
-        acc = {c: jnp.zeros((8, CY), F32) for c in range(3)}
-        views = [cur.at[c, group_rows(it, GROUP)] for c in range(3)]
-        wets = wet_in.at[group_rows(it, GROUP)]
-        for j in range(BLOCKS):
-            at = slice(8 * j, 8 * j + 8)
-            for c in range(3):
-                value = views[c][at]
-                if c == 1:
-                    value = jnp.where(section == 0, value, wets[at].astype(F32))
-                acc[c] = collect(acc[c], value, j, lane)
-        merge(it, acc, sides)
-        return carry
-
-    lax.fori_loop(0, ROWS // GROUP, pack, 0)
+
+    @pl.when(section == 0)
+    def _():
+        pack_sides(lambda c, at: cur.at[c, at], sides, (0, 1, 2))
+
+    @pl.when(section != 0)
+    def _():
+        pack_sides(lambda c, at: wet_in.at[at] if c == 1 else cur.at[c, at], sides, (0, 1, 2))
+
     take_edges(section, p, cur, wet_in, xs)
     scale[...] = cols[2]
 
@@ -233,8 +241,8 @@
 def edge_addends(sums, period, offset):
     masks, values = [], []
     lane = iota((CY, 2 * CY), 1)
-    block = ((lane & (CY - 1)) >> 1) + jnp.where(lane >= CY, 2 * BLOCKS, 0)
-    inside = (lane & (CY - 1)) < 4 * BLOCKS
+    block = ((lane & (CY - 1)) >> 1) + jnp.where(lane >= CY, HALF, 0)
+    inside = (lane & (CY - 1)) < 2 * HALF
     for side, shift in ((0, 0), (1, offset)):
         at = iota(lane.shape, 0) * period + shift - block * 8
         masks.append(one((at >= 0) & (at < 8) & ((lane & 1) == side) & inside).astype(jnp.bfloat16))
@@ -247,7 +255,7 @@
 
 def align_sides(zs, c, lane, sub):
     first, second = zs[c, 0], zs[c, 1]
-    top = 4 * BLOCKS
+    top = 2 * HALF
     low_first = jnp.where(lane == top - 2, pltpu.roll(second, top - 2, 1), pltpu.roll(first, CY - 2, 1))
     low_second = pltpu.roll(second, CY - 2, 1)
     high_first = pltpu.roll(first, 2, 1)
@@ -256,23 +264,42 @@
         zs[c, h] = jnp.where(lane & 1 == 0, pltpu.roll(low, 7, 0), pltpu.roll(high, 1, 0))
 
 
+def read_batch(fields, j):
+    return [fields[c][8 * i : 8 * i + 8] for i in range(j, j + BATCH) for c in range(3)]
+
+
+def write_batch(fields, j, values):
+    for n, value in enumerate(values):
+        i = j + 1 - BATCH + n // 3
+        fields[n % 3][8 * i : 8 * i + 8] = value
+
+
 def step_kernel(linked, last, *refs):
     cur_in, prev_in, coeff, wet, cols, xr, yra, yrb, mine, *refs = refs
     if linked:
         received, *refs = refs
     cur, prev, *refs = refs
     if last:
-        out, zs, full, co, wet_in, sem = refs
+        out, zs, full, halos, co, wet_in, sem = refs
     else:
-        base, xs, sides, zs, full, co, wet_in, sem, surf = refs
+        base, xs, sides, zs, full, halos, co, wet_in, sem, surf = refs
     section, p, q = place()
     lane = iota((8, CY), 1)
     sub = iota((8, CY), 0)
-    zero = jnp.zeros((8, CY), F32)
     even_lane = lane & 1 == 0
-    loads = [pltpu.make_async_copy(coeff, co, sem.at[0]), pltpu.make_async_copy(wet, wet_in, sem.at[1])]
-    for load in loads:
-        load.start()
+    groups = ROWS // GROUP
+    wet_load = pltpu.make_async_copy(wet, wet_in, sem.at[groups])
+
+    def load(it):
+        at = group_rows(it, GROUP)
+        return pltpu.make_async_copy(coeff.at[:, at], co.at[:, at], sem.at[it])
+
+    @pl.when(section != 0)
+    def _():
+        wet_load.start()
+
+    for it in range(groups):
+        load(it).start()
 
     @pl.when((q & 1) == 1)
     def _():
@@ -296,9 +323,6 @@
         arrived = arrived_rows(section, received)
         sums = arrived_sums(arrived)
         addend = landed(arrived, sums)
-    if not last:
-        sides[...] = jnp.zeros_like(sides)
-
     def widen(it, carry):
         for c in range(3):
             view = full.at[c, group_rows(it, FIRST + GROUP)]
@@ -328,19 +352,23 @@
             for h, value in enumerate(edge_addends(sums, NL, 0)):
                 zs[2, h] += value
 
-        lax.fori_loop(0, ROWS // GROUP, widen, 0)
-        for load in loads:
-            load.wait()
+        lax.fori_loop(0, groups, widen, 0)
+        unpack_sides(zs, halos, (0, 1, 2))
 
         def group(it, carry):
-            turn = (CY - (it & 1) * 2 * BLOCKS) & (CY - 1)
-            halos = [pltpu.roll(zs[c, it >> 1], turn, 1) for c in range(3)]
-            acc = {c: zero for c in range(3)}
+            load(it).wait()
+            sides_of = views_of(it, halos)
+            depth = it * GROUP - NL * ((it * GROUP * 656) >> 16) + sub
             fields, old, new_fields, factors = padded_of(it), views_of(it, prev_in), views_of(it, prev), views_of(it, co)
             for j in range(BLOCKS):
+                if j % BATCH == 0:
+                    olds, news = read_batch(old, j), []
                 at = slice(8 * j, 8 * j + 8)
                 mu = factors[0][at]
                 stiff = factors[1][at] + 2.0 * mu
+                layer = depth + 8 * j
+                shallowest = (layer == 0) | (layer == NL) | (layer == 2 * NL)
+                deepest = (layer == NL - 1) | (layer == 2 * NL - 1)
                 for c in range(3):
 
                     def near(rows):
@@ -348,15 +376,9 @@
 
                     v = near(0)
                     twice = 2.0 * v
-                    above = near(-1)
-                    below = near(1)
-                    for row in (0, NL):
-                        if 8 * j <= row < 8 * j + 8:
-                            above = jnp.where(sub == row - 8 * j, 0.0, above)
-                    for row in (NL - 1, GROUP - 1):
-                        if 8 * j <= row < 8 * j + 8:
-                            below = jnp.where(sub == row - 8 * j, 0.0, below)
-                    halo = pltpu.roll(halos[c], CY - 1 - 2 * j, 1)
+                    above = jnp.where(shallowest, 0.0, near(-1))
+                    below = jnp.where(deepest, 0.0, near(1))
+                    halo = sides_of[c][at]
                     low = jnp.where(lane == CY - 1, halo, v)
                     high = jnp.where(lane == 0, halo, v)
                     along_first = near(-NL) + near(NL) - twice
@@ -368,15 +390,14 @@
                         force = stiff * along_second + mu * (along_first + along_depth)
                     else:
                         force = stiff * along_depth + mu * (along_first + along_second)
-                    new = twice - old[c][at] + force
-                    new_fields[c][at] = new
-                    if not last:
-                        acc[c] = collect(acc[c], new, j, lane)
-            if not last:
-                merge(it, acc, sides)
+                    news.append(twice - olds.pop(0) + force)
+                if j % BATCH == BATCH - 1:
+                    write_batch(new_fields, j, news)
             return carry
 
-        lax.fori_loop(0, ROWS // GROUP, group, 0)
+        lax.fori_loop(0, groups, group, 0)
+        if not last:
+            pack_sides(lambda c, at: prev.at[c, at], sides, (0, 1, 2))
 
     @pl.when(section != 0)
     def _():
@@ -407,21 +428,22 @@
             def _():
                 add_edge(FIRST - REFINE)
 
-        for load in loads:
-            load.wait()
+        wet_load.wait()
         if linked:
             for start, fine in fine_addend(addend):
                 at = pl.ds(start, 8, stride=REFINE)
                 cur[0, at] += wet_in[at].astype(F32) * fine
-        lax.fori_loop(0, ROWS // GROUP, widen, 0)
+        lax.fori_loop(0, groups, widen, 0)
+        unpack_sides(zs, halos, (0, 2))
 
         def group(it, carry):
-            turn = (CY - (it & 1) * 2 * BLOCKS) & (CY - 1)
-            halos = {c: pltpu.roll(zs[c, it >> 1], turn, 1) for c in (0, 2)}
-            acc = {0: zero, 2: zero}
+            load(it).wait()
+            sides_of = views_of(it, halos)
             fields, old, new_fields, factors = padded_of(it), views_of(it, prev_in), views_of(it, prev), views_of(it, co)
             wets = wet_in.at[group_rows(it, GROUP)]
             for j in range(BLOCKS):
+                if j % BATCH == 0:
+                    olds, news = read_batch(old, j), []
                 at = slice(8 * j, 8 * j + 8)
                 a = factors[0][at]
                 b = factors[1][at]
@@ -434,7 +456,7 @@
                     v = near(c, 0)
                     low = jnp.where(lane == CY - 1, near(c, -1), v)
                     high = jnp.where(lane == 0, near(c, 1), v)
-                    halo = pltpu.roll(halos[c], CY - 1 - 2 * j, 1)
+                    halo = sides_of[c // 2][at]
                     for s in range(8):
                         if (8 * j + s) % REFINE == 0:
                             low = jnp.where((lane == CY - 1) & (sub == s), halo, low)
@@ -445,21 +467,16 @@
                 def down(c):
                     return near(c, REFINE) - near(c, -REFINE)
 
-                first_flux = w * (old[1][at] - a * down(0))
-                second_flux = w * (old[2][at] - a * across(0))
-                height = w * (old[0][at] - b * (down(1) + across(2)))
-                new_fields[0][at] = height
-                new_fields[1][at] = first_flux
-                new_fields[2][at] = second_flux
-                if not last:
-                    acc[0] = collect(acc[0], height, j, lane)
-                    acc[2] = collect(acc[2], second_flux, j, lane)
-            if not last:
-                merge(it, acc, sides)
+                news.append(w * (olds.pop(0) - b * (down(1) + across(2))))
+                news.append(w * (olds.pop(0) - a * down(0)))
+                news.append(w * (olds.pop(0) - a * across(0)))
+                if j % BATCH == BATCH - 1:
+                    write_batch(new_fields, j, news)
             return carry
 
-        lax.fori_loop(0, ROWS // GROUP, group, 0)
+        lax.fori_loop(0, groups, group, 0)
         if not last:
+            pack_sides(lambda c, at: prev.at[c, at], sides, (0, 2))
             sides[1] = mine[1]
 
     if last:
@@ -593,7 +610,10 @@
         if before is not None:
             operands.append(before)
         kernel = functools.partial(step_kernel, before is not None, last)
-        scratch = [vmem(sides_shape, F32), vmem((3, TOTAL, CY), F32), vmem((2, ROWS, CY), F32), wet_in, dma((2,))]
+        scratch = [
+            vmem(sides_shape, F32), vmem((3, TOTAL, CY), F32), vmem(field_shape, F32), vmem((2, ROWS, CY), F32),
+            wet_in, dma((ROWS // GROUP + 1,)),
+        ]
         more = dict(aliases={0: 0, 1: 1}, any_inputs=(2, 3), cost=64)
         if last:
             _, new, final = call(

time: 72.5 us -> 65.3 us (0.901)
  Pallas kernels: 33.6 us -> 19.9 us
  waiting for transfers between devices: 1.63 us -> 12.4 us
  starting transfers between devices: 36.5 us -> 32.3 us
    pallas_call x9, Pallas kernels: 33.6 us -> 19.9 us  [call(): pl.pallas_call(kernel, out_shape=[(pltpu.VMEM if kept else jax.ShapeDtype...]
    all_to_all x4, waiting for transfers between devices: 1.6 us -> 12.3 us  [exchange(): payload = lax.all_to_all(payload, ('sec', 'gx', 'gy'), 0, 0, tiled=True)]
    all_to_all x4, starting transfers between devices: 24.7 us -> 20.6 us  [exchange(): payload = lax.all_to_all(payload, ('sec', 'gx', 'gy'), 0, 0, tiled=True)]
  transfers between devices with their start and end apart: 16 -> 16, of which waited for: 1 -> 4; matrix products, arithmetic and copies ran while one was open for 0% -> 0% of each run, Pallas kernels for 40% -> 23%
where the time goes in v1:
time: 65.3 us; the launch traced here: 64.8 us
  starting transfers between devices  32.3 us (49%)
  Pallas kernels  19.9 us (30%)
  waiting for transfers between devices  12.4 us (19%)
    all_to_all x4, starting transfers between devices, exchange(): payload = lax.all_to_all(payload, ('sec', 'gx', 'gy'), 0, 0, tiled=True)  20.6 us
    pallas_call x9, Pallas kernels, call(): pl.pallas_call(kernel, out_shape=[(pltpu.VMEM if kept else jax.ShapeDtype...  19.9 us
    all_to_all x4, waiting for transfers between devices, exchange(): payload = lax.all_to_all(payload, ('sec', 'gx', 'gy'), 0, 0, tiled=True)  12.3 us
    ppermute x4, starting transfers between devices, on_device(): xr = lax.ppermute(xs, 'gx', swap)  8.2 us
    ppermute x4, starting transfers between devices, on_device(): yrb = lax.ppermute(sides, 'gy', outer)  2.6 us
  transfers between devices with their start and end apart: 16, of which 4 were waited for; matrix products, arithmetic and copies ran while one was open for 0% of the time, Pallas kernels for 23%

profile of v1, /device:TPU:0, one launch (start us, length us, event | category | flops | bytes accessed | tf_op | source)
XLA Modules:
  0.0 64.8 jit_solution(8075511086702097610)
XLA Ops:
  0.0 3.0 %shard_map.73 = (f32[256,128]{1,0:T(8,128)}, f32[4,32,128]{2,1,0:T(8,128)S(1)}, f32[128,128]{1,0:T(8,128)S(1)}, f32[3,800,128]{2,1,0:T(8,128)S(1)}, f32[3,800,12...) custom-call(f32[3,800,128]{2,1,0:T(8,128)} %bitcast.25, ...), custom_call_target="tpu_custom_call" | custom-call | flops 4000000000 | bytes 4194304 | tf_op jit(solution)/shard_map/pallas_call | solution.py:541
  3.0 3.0 %collective-permute-start = (f32[3,104,128]{2,1,0:T(8,128)S(1)}, f32[3,104,128]{2,1,0:T(8,128)S(1)}, u32[]{:S(2)}, u32[]{:S(2)}) collective-permute-start(f32[3,104,128]{2,1,0:T(8,128)S(1)} %get-tuple-element.33), channel_id=1, source_target_pairs={{0,8},{8,0},{1,9},{9,1},{2,10},{10,2},{3,11},{11,3},{4,12},{12,4},... | collective-permute-start | bytes 479240 | tf_op jit(solution)/shard_map/ppermute | solution.py:606
  6.0 0.0 collective-permute-start.1
  6.0 0.7 %collective-permute-start.2 = (f32[3,2,8,128]{3,2,1,0:T(8,128)S(1)}, f32[3,2,8,128]{3,2,1,0:T(8,128)S(1)}, u32[]{:S(2)}, u32[]{:S(2)}) collective-permute-start(f32[3,2,8,128]{3,2,1,0:T(8,128)S(1)} %get-tuple-element.34.refs_8_), channel_id=1, source_target_pairs={{1,2},{2,1},{3,4},{4,3},{5,6},{6,5},{9,10},{10,9},{11,12},{12,11},... | collective-permute-start | bytes 73736 | tf_op jit(solution)/shard_map/ppermute | solution.py:608
  6.7 7.5 %all-to-all-start = ((f32[32,8,128]{2,1,0:T(8,128)}), f32[32,8,128]{2,1,0:T(8,128)S(1)}, u32[]{:S(2)}, u32[]{:S(2)}) async-start(f32[32,8,128]{2,1,0:T(8,128)} %bitcast.8), calls=%async_computation | async-start | bytes 262144 | tf_op jit(solution)/shard_map/all_to_all | solution.py:582
  14.2 0.0 collective-permute-done.1.refs_6_
  14.2 0.0 collective-permute-done.2.refs_7_
  14.2 0.0 collective-permute-done.refs_5_
  14.2 2.9 %shard_map.74 = (f32[3,800,128]{2,1,0:T(8,128)S(1)}, f32[3,800,128]{2,1,0:T(8,128)S(1)}, f32[32,128]{1,0:T(8,128)S(1)}, f32[3,104,128]{2,1,0:T(8,128)S(1)}, f32[3,2,8,128]{3,2,1,0:T(8,128)S(1)}) custom-call(f32[3,800,128]{2,1,0:T(8,128)S(1)} %get-tuple-element.30.refs_0_, ...), custom_call_target="tpu_custom_call", output_to_operand_aliasing={{0}: (0, {}), {1}: (1, {})} | custom-call | flops 64000000000 | bytes 67108864 | tf_op jit(solution)/shard_map/pallas_call | solution.py:541
  17.1 0.3 collective-permute-start.4
  17.5 0.7 %collective-permute-start.5 = (f32[3,2,8,128]{3,2,1,0:T(8,128)S(1)}, f32[3,2,8,128]{3,2,1,0:T(8,128)S(1)}, u32[]{:S(2)}, u32[]{:S(2)}) collective-permute-start(f32[3,2,8,128]{3,2,1,0:T(8,128)S(1)} %get-tuple-element.38.refs_8_), channel_id=1, source_target_pairs={{1,2},{2,1},{3,4},{4,3},{5,6},{6,5},{9,10},{10,9},{11,12},{12,11},... | collective-permute-start | bytes 73736 | tf_op jit(solution)/shard_map/ppermute | solution.py:608
  18.1 1.7 %collective-permute-start.3 = (f32[3,104,128]{2,1,0:T(8,128)S(1)}, f32[3,104,128]{2,1,0:T(8,128)S(1)}, u32[]{:S(2)}, u32[]{:S(2)}) collective-permute-start(f32[3,104,128]{2,1,0:T(8,128)S(1)} %get-tuple-element.37), channel_id=1, source_target_pairs={{0,8},{8,0},{1,9},{9,1},{2,10},{10,2},{3,11},{11,3},{4,12},{12,4},... | collective-permute-start | bytes 479240 | tf_op jit(solution)/shard_map/ppermute | solution.py:606
  19.9 2.5 %all-to-all-done = f32[32,8,128]{2,1,0:T(8,128)S(1)} async-done(((f32[32,8,128]{2,1,0:T(8,128)}), f32[32,8,128]{2,1,0:T(8,128)S(1)}, u32[]{:S(2)}, u32[]{:S(2)}) %all-to-all-start) | async-done | bytes 131104 | tf_op jit(solution)/shard_map/all_to_all | solution.py:582
  22.4 1.0 %shard_map.76 = f32[256,128]{1,0:T(8,128)} custom-call(f32[256,128]{1,0:T(8,128)S(1)} %bitcast.22, f32[32,128]{1,0:T(8,128)S(1)} %get-tuple-element.44.base, f32[32,128]{1,0:T(8,128)S(1)} %get-tuple-element.45.scale, f32[4,32,128]{2,1,0:T(8,128)S(1)} %get-tuple-element.32.refs_4_.cols, f32[128,128]{1,0:T(8,128)S(1)} %get-tuple-element.46.pcat), custom_call_target="tpu_custom_call" | custom-call | flops 4000000000 | bytes 4194304 | tf_op jit(solution)/shard_map/pallas_call | solution.py:541
  23.4 4.1 %all-to-all-start.1 = ((f32[32,8,128]{2,1,0:T(8,128)}), f32[32,8,128]{2,1,0:T(8,128)S(1)}, u32[]{:S(2)}, u32[]{:S(2)}) async-start(f32[32,8,128]{2,1,0:T(8,128)} %bitcast.10), calls=%async_computation.1 | async-start | bytes 262144 | tf_op jit(solution)/shard_map/all_to_all | solution.py:582
  27.5 0.0 collective-permute-done.4.refs_6_
  27.5 0.0 collective-permute-done.5.refs_7_
  27.5 0.0 collective-permute-done.3.refs_5_
  27.6 2.9 %shard_map.75 = (f32[3,800,128]{2,1,0:T(8,128)S(1)}, f32[3,800,128]{2,1,0:T(8,128)S(1)}, f32[32,128]{1,0:T(8,128)S(1)}, f32[3,104,128]{2,1,0:T(8,128)S(1)}, f32[3,2,8,128]{3,2,1,0:T(8,128)S(1)}) custom-call(f32[3,800,128]{2,1,0:T(8,128)S(1)} %get-tuple-element.35.refs_0_, ...), custom_call_target="tpu_custom_call", output_to_operand_aliasing={{0}: (0, {}), {1}: (1, {})} | custom-call | flops 64000000000 | bytes 67108864 | tf_op jit(solution)/shard_map/pallas_call | solution.py:541
  30.5 0.3 collective-permute-start.7
  30.8 0.7 %collective-permute-start.8 = (f32[3,2,8,128]{3,2,1,0:T(8,128)S(1)}, f32[3,2,8,128]{3,2,1,0:T(8,128)S(1)}, u32[]{:S(2)}, u32[]{:S(2)}) collective-permute-start(f32[3,2,8,128]{3,2,1,0:T(8,128)S(1)} %get-tuple-element.43.refs_8_), channel_id=1, source_target_pairs={{1,2},{2,1},{3,4},{4,3},{5,6},{6,5},{9,10},{10,9},{11,12},{12,11},... | collective-permute-start | bytes 73736 | tf_op jit(solution)/shard_map/ppermute | solution.py:608
  31.4 1.7 %collective-permute-start.6 = (f32[3,104,128]{2,1,0:T(8,128)S(1)}, f32[3,104,128]{2,1,0:T(8,128)S(1)}, u32[]{:S(2)}, u32[]{:S(2)}) collective-permute-start(f32[3,104,128]{2,1,0:T(8,128)S(1)} %get-tuple-element.42), channel_id=1, source_target_pairs={{0,8},{8,0},{1,9},{9,1},{2,10},{10,2},{3,11},{11,3},{4,12},{12,4},... | collective-permute-start | bytes 479240 | tf_op jit(solution)/shard_map/ppermute | solution.py:606
  33.2 2.5 %all-to-all-done.1 = f32[32,8,128]{2,1,0:T(8,128)S(1)} async-done(((f32[32,8,128]{2,1,0:T(8,128)}), f32[32,8,128]{2,1,0:T(8,128)S(1)}, u32[]{:S(2)}, u32[]{:S(2)}) %all-to-all-start.1) | async-done | bytes 131104 | tf_op jit(solution)/shard_map/all_to_all | solution.py:582
  35.7 1.0 %shard_map.78 = f32[256,128]{1,0:T(8,128)} custom-call(f32[256,128]{1,0:T(8,128)S(1)} %bitcast.20, f32[32,128]{1,0:T(8,128)S(1)} %get-tuple-element.51.base, f32[32,128]{1,0:T(8,128)S(1)} %get-tuple-element.45.scale, f32[4,32,128]{2,1,0:T(8,128)S(1)} %get-tuple-element.32.refs_4_.cols, f32[128,128]{1,0:T(8,128)S(1)} %get-tuple-element.46.pcat), custom_call_target="tpu_custom_call" | custom-call | flops 4000000000 | bytes 4194304 | tf_op jit(solution)/shard_map/pallas_call | solution.py:541
  36.7 4.5 %all-to-all-start.2 = ((f32[32,8,128]{2,1,0:T(8,128)}), f32[32,8,128]{2,1,0:T(8,128)S(1)}, u32[]{:S(2)}, u32[]{:S(2)}) async-start(f32[32,8,128]{2,1,0:T(8,128)} %bitcast.12), calls=%async_computation.2 | async-start | bytes 262144 | tf_op jit(solution)/shard_map/all_to_all | solution.py:582
  41.2 0.0 collective-permute-done.7.refs_6_
  41.2 0.0 collective-permute-done.8.refs_7_
  41.2 0.0 collective-permute-done.6.refs_5_
  41.2 2.9 %shard_map.77 = (f32[3,800,128]{2,1,0:T(8,128)S(1)}, f32[3,800,128]{2,1,0:T(8,128)S(1)}, f32[32,128]{1,0:T(8,128)S(1)}, f32[3,104,128]{2,1,0:T(8,128)S(1)}, f32[3,2,8,128]{3,2,1,0:T(8,128)S(1)}) custom-call(f32[3,800,128]{2,1,0:T(8,128)S(1)} %get-tuple-element.40.refs_0_, ...), custom_call_target="tpu_custom_call", output_to_operand_aliasing={{0}: (0, {}), {1}: (1, {})} | custom-call | flops 64000000000 | bytes 67108864 | tf_op jit(solution)/shard_map/pallas_call | solution.py:541
  44.2 0.3 collective-permute-start.10
  44.5 0.7 %collective-permute-start.11 = (f32[3,2,8,128]{3,2,1,0:T(8,128)S(1)}, f32[3,2,8,128]{3,2,1,0:T(8,128)S(1)}, u32[]{:S(2)}, u32[]{:S(2)}) collective-permute-start(f32[3,2,8,128]{3,2,1,0:T(8,128)S(1)} %get-tuple-element.50.refs_8_), channel_id=1, source_target_pairs={{1,2},{2,1},{3,4},{4,3},{5,6},{6,5},{9,10},{10,9},{11,12},{12,11},... | collective-permute-start | bytes 73736 | tf_op jit(solution)/shard_map/ppermute | solution.py:608
  45.1 1.7 %collective-permute-start.9 = (f32[3,104,128]{2,1,0:T(8,128)S(1)}, f32[3,104,128]{2,1,0:T(8,128)S(1)}, u32[]{:S(2)}, u32[]{:S(2)}) collective-permute-start(f32[3,104,128]{2,1,0:T(8,128)S(1)} %get-tuple-element.49), channel_id=1, source_target_pairs={{0,8},{8,0},{1,9},{9,1},{2,10},{10,2},{3,11},{11,3},{4,12},{12,4},... | collective-permute-start | bytes 479240 | tf_op jit(solution)/shard_map/ppermute | solution.py:606
  46.9 2.5 %all-to-all-done.2 = f32[32,8,128]{2,1,0:T(8,128)S(1)} async-done(((f32[32,8,128]{2,1,0:T(8,128)}), f32[32,8,128]{2,1,0:T(8,128)S(1)}, u32[]{:S(2)}, u32[]{:S(2)}) %all-to-all-start.2) | async-done | bytes 131104 | tf_op jit(solution)/shard_map/all_to_all | solution.py:582
  49.4 1.0 %shard_map.80 = f32[256,128]{1,0:T(8,128)} custom-call(f32[256,128]{1,0:T(8,128)S(1)} %bitcast.18, f32[32,128]{1,0:T(8,128)S(1)} %get-tuple-element.54.base, f32[32,128]{1,0:T(8,128)S(1)} %get-tuple-element.45.scale, f32[4,32,128]{2,1,0:T(8,128)S(1)} %get-tuple-element.32.refs_4_.cols, f32[128,128]{1,0:T(8,128)S(1)} %get-tuple-element.46.pcat), custom_call_target="tpu_custom_call" | custom-call | flops 4000000000 | bytes 4194304 | tf_op jit(solution)/shard_map/pallas_call | solution.py:541
  50.4 4.5 %all-to-all-start.3 = ((f32[32,8,128]{2,1,0:T(8,128)}), f32[32,8,128]{2,1,0:T(8,128)S(1)}, u32[]{:S(2)}, u32[]{:S(2)}) async-start(f32[32,8,128]{2,1,0:T(8,128)} %bitcast.14), calls=%async_computation.3 | async-start | bytes 262144 | tf_op jit(solution)/shard_map/all_to_all | solution.py:582
  54.9 0.0 collective-permute-done.10.refs_6_
  54.9 0.0 collective-permute-done.11.refs_7_
  54.9 0.0 collective-permute-done.9.refs_5_
  54.9 3.3 %shard_map.79 = (f32[3,800,128]{2,1,0:T(8,128)S(1)}, f32[3,800,128]{2,1,0:T(8,128)S(1)}, f32[3,800,128]{2,1,0:T(8,128)}) custom-call(f32[3,800,128]{2,1,0:T(8,128)S(1)} %get-tuple-element.47.refs_0_, f32[3,800,128]{2,1,0:T(8,128)S(1)} %get-tuple-element.48.refs_1_, f32[2,800,128]{2,1,0:T(8,128)} %bitcast.30, ...), custom_call_target="tpu_custom_call", output_to_operand_aliasing={{0}: (0, {}), {1}: (1, {})} | custom-call | flops 64000000000 | bytes 67108864 | tf_op jit(solution)/shard_map/pallas_call | solution.py:541
  58.3 4.8 %all-to-all-done.3 = f32[32,8,128]{2,1,0:T(8,128)S(1)} async-done(((f32[32,8,128]{2,1,0:T(8,128)}), f32[32,8,128]{2,1,0:T(8,128)S(1)}, u32[]{:S(2)}, u32[]{:S(2)}) %all-to-all-start.3) | async-done | bytes 131104 | tf_op jit(solution)/shard_map/all_to_all | solution.py:582
  63.1 1.7 %shard_map.81 = f32[3,800,128]{2,1,0:T(8,128)} custom-call(f32[3,800,128]{2,1,0:T(8,128)} %get-tuple-element.52.final_in, f32[3,800,128]{2,1,0:T(8,128)S(1)} %get-tuple-element.53.fields, s32[800,128]{1,0:T(8,128)} %bitcast.36, f32[256,128]{1,0:T(8,128)S(1)} %bitcast.24), custom_call_target="tpu_custom_call", output_to_operand_aliasing={{}: (0, {})} | custom-call | flops 4000000000 | bytes 4194304 | tf_op jit(solution)/shard_map/pallas_call | solution.py:541
Async XLA Ops:
  3.0 11.2 %collective-permute-start = (f32[3,104,128]{2,1,0:T(8,128)S(1)}, f32[3,104,128]{2,1,0:T(8,128)S(1)}, u32[]{:S(2)}, u32[]{:S(2)}) collective-permute-start(f32[3,104,128]{2,1,0:T(8,128)S(1)} %get-tuple-element.33), channel_id=1, source_target_pairs={{0,8},{8,0},{1,9},{9,1},{2,10},{10,2},{3,11},{11,3},{4,12},{12,4},... | collective-permute-start | bytes 479240 | tf_op jit(solution)/shard_map/ppermute | solution.py:606
  6.0 8.2 %collective-permute-start.1 = (f32[3,2,8,128]{3,2,1,0:T(8,128)S(1)}, f32[3,2,8,128]{3,2,1,0:T(8,128)S(1)}, u32[]{:S(2)}, u32[]{:S(2)}) collective-permute-start(f32[3,2,8,128]{3,2,1,0:T(8,128)S(1)} %get-tuple-element.34.refs_8_), channel_id=1, source_target_pairs={{0,1},{1,0},{2,3},{3,2},{4,5},{5,4},{6,7},{7,6},{8,9},{9,8},{10,11... | collective-permute-start | bytes 73736 | tf_op jit(solution)/shard_map/ppermute | solution.py:607
  6.0 8.2 %collective-permute-start.2 = (f32[3,2,8,128]{3,2,1,0:T(8,128)S(1)}, f32[3,2,8,128]{3,2,1,0:T(8,128)S(1)}, u32[]{:S(2)}, u32[]{:S(2)}) collective-permute-start(f32[3,2,8,128]{3,2,1,0:T(8,128)S(1)} %get-tuple-element.34.refs_8_), channel_id=1, source_target_pairs={{1,2},{2,1},{3,4},{4,3},{5,6},{6,5},{9,10},{10,9},{11,12},{12,11},... | collective-permute-start | bytes 73736 | tf_op jit(solution)/shard_map/ppermute | solution.py:608
  6.7 15.7 %all-to-all-start = ((f32[32,8,128]{2,1,0:T(8,128)}), f32[32,8,128]{2,1,0:T(8,128)S(1)}, u32[]{:S(2)}, u32[]{:S(2)}) async-start(f32[32,8,128]{2,1,0:T(8,128)} %bitcast.8), calls=%async_computation | async-start | bytes 262144 | tf_op jit(solution)/shard_map/all_to_all | solution.py:582
  17.1 10.4 %collective-permute-start.4 = (f32[3,2,8,128]{3,2,1,0:T(8,128)S(1)}, f32[3,2,8,128]{3,2,1,0:T(8,128)S(1)}, u32[]{:S(2)}, u32[]{:S(2)}) collective-permute-start(f32[3,2,8,128]{3,2,1,0:T(8,128)S(1)} %get-tuple-element.38.refs_8_), channel_id=1, source_target_pairs={{0,1},{1,0},{2,3},{3,2},{4,5},{5,4},{6,7},{7,6},{8,9},{9,8},{10,11... | collective-permute-start | bytes 73736 | tf_op jit(solution)/shard_map/ppermute | solution.py:607
  17.5 10.1 %collective-permute-start.5 = (f32[3,2,8,128]{3,2,1,0:T(8,128)S(1)}, f32[3,2,8,128]{3,2,1,0:T(8,128)S(1)}, u32[]{:S(2)}, u32[]{:S(2)}) collective-permute-start(f32[3,2,8,128]{3,2,1,0:T(8,128)S(1)} %get-tuple-element.38.refs_8_), channel_id=1, source_target_pairs={{1,2},{2,1},{3,4},{4,3},{5,6},{6,5},{9,10},{10,9},{11,12},{12,11},... | collective-permute-start | bytes 73736 | tf_op jit(solution)/shard_map/ppermute | solution.py:608
  18.1 9.4 %collective-permute-start.3 = (f32[3,104,128]{2,1,0:T(8,128)S(1)}, f32[3,104,128]{2,1,0:T(8,128)S(1)}, u32[]{:S(2)}, u32[]{:S(2)}) collective-permute-start(f32[3,104,128]{2,1,0:T(8,128)S(1)} %get-tuple-element.37), channel_id=1, source_target_pairs={{0,8},{8,0},{1,9},{9,1},{2,10},{10,2},{3,11},{11,3},{4,12},{12,4},... | collective-permute-start | bytes 479240 | tf_op jit(solution)/shard_map/ppermute | solution.py:606
  23.4 12.3 %all-to-all-start.1 = ((f32[32,8,128]{2,1,0:T(8,128)}), f32[32,8,128]{2,1,0:T(8,128)S(1)}, u32[]{:S(2)}, u32[]{:S(2)}) async-start(f32[32,8,128]{2,1,0:T(8,128)} %bitcast.10), calls=%async_computation.1 | async-start | bytes 262144 | tf_op jit(solution)/shard_map/all_to_all | solution.py:582
  30.5 10.7 %collective-permute-start.7 = (f32[3,2,8,128]{3,2,1,0:T(8,128)S(1)}, f32[3,2,8,128]{3,2,1,0:T(8,128)S(1)}, u32[]{:S(2)}, u32[]{:S(2)}) collective-permute-start(f32[3,2,8,128]{3,2,1,0:T(8,128)S(1)} %get-tuple-element.43.refs_8_), channel_id=1, source_target_pairs={{0,1},{1,0},{2,3},{3,2},{4,5},{5,4},{6,7},{7,6},{8,9},{9,8},{10,11... | collective-permute-start | bytes 73736 | tf_op jit(solution)/shard_map/ppermute | solution.py:607
  30.8 10.4 %collective-permute-start.8 = (f32[3,2,8,128]{3,2,1,0:T(8,128)S(1)}, f32[3,2,8,128]{3,2,1,0:T(8,128)S(1)}, u32[]{:S(2)}, u32[]{:S(2)}) collective-permute-start(f32[3,2,8,128]{3,2,1,0:T(8,128)S(1)} %get-tuple-element.43.refs_8_), channel_id=1, source_target_pairs={{1,2},{2,1},{3,4},{4,3},{5,6},{6,5},{9,10},{10,9},{11,12},{12,11},... | collective-permute-start | bytes 73736 | tf_op jit(solution)/shard_map/ppermute | solution.py:608
  31.4 9.8 %collective-permute-start.6 = (f32[3,104,128]{2,1,0:T(8,128)S(1)}, f32[3,104,128]{2,1,0:T(8,128)S(1)}, u32[]{:S(2)}, u32[]{:S(2)}) collective-permute-start(f32[3,104,128]{2,1,0:T(8,128)S(1)} %get-tuple-element.42), channel_id=1, source_target_pairs={{0,8},{8,0},{1,9},{9,1},{2,10},{10,2},{3,11},{11,3},{4,12},{12,4},... | collective-permute-start | bytes 479240 | tf_op jit(solution)/shard_map/ppermute | solution.py:606
  36.7 12.7 %all-to-all-start.2 = ((f32[32,8,128]{2,1,0:T(8,128)}), f32[32,8,128]{2,1,0:T(8,128)S(1)}, u32[]{:S(2)}, u32[]{:S(2)}) async-start(f32[32,8,128]{2,1,0:T(8,128)} %bitcast.12), calls=%async_computation.2 | async-start | bytes 262144 | tf_op jit(solution)/shard_map/all_to_all | solution.py:582
  44.2 10.7 %collective-permute-start.10 = (f32[3,2,8,128]{3,2,1,0:T(8,128)S(1)}, f32[3,2,8,128]{3,2,1,0:T(8,128)S(1)}, u32[]{:S(2)}, u32[]{:S(2)}) collective-permute-start(f32[3,2,8,128]{3,2,1,0:T(8,128)S(1)} %get-tuple-element.50.refs_8_), channel_id=1, source_target_pairs={{0,1},{1,0},{2,3},{3,2},{4,5},{5,4},{6,7},{7,6},{8,9},{9,8},{10,11... | collective-permute-start | bytes 73736 | tf_op jit(solution)/shard_map/ppermute | solution.py:607
  44.5 10.4 %collective-permute-start.11 = (f32[3,2,8,128]{3,2,1,0:T(8,128)S(1)}, f32[3,2,8,128]{3,2,1,0:T(8,128)S(1)}, u32[]{:S(2)}, u32[]{:S(2)}) collective-permute-start(f32[3,2,8,128]{3,2,1,0:T(8,128)S(1)} %get-tuple-element.50.refs_8_), channel_id=1, source_target_pairs={{1,2},{2,1},{3,4},{4,3},{5,6},{6,5},{9,10},{10,9},{11,12},{12,11},... | collective-permute-start | bytes 73736 | tf_op jit(solution)/shard_map/ppermute | solution.py:608
  45.1 9.8 %collective-permute-start.9 = (f32[3,104,128]{2,1,0:T(8,128)S(1)}, f32[3,104,128]{2,1,0:T(8,128)S(1)}, u32[]{:S(2)}, u32[]{:S(2)}) collective-permute-start(f32[3,104,128]{2,1,0:T(8,128)S(1)} %get-tuple-element.49), channel_id=1, source_target_pairs={{0,8},{8,0},{1,9},{9,1},{2,10},{10,2},{3,11},{11,3},{4,12},{12,4},... | collective-permute-start | bytes 479240 | tf_op jit(solution)/shard_map/ppermute | solution.py:606
  50.4 12.7 %all-to-all-start.3 = ((f32[32,8,128]{2,1,0:T(8,128)}), f32[32,8,128]{2,1,0:T(8,128)S(1)}, u32[]{:S(2)}, u32[]{:S(2)}) async-start(f32[32,8,128]{2,1,0:T(8,128)} %bitcast.14), calls=%async_computation.3 | async-start | bytes 262144 | tf_op jit(solution)/shard_map/all_to_all | solution.py:582

commit v2 on v1

--- a/solution.py
+++ b/solution.py
@@ -79,14 +79,16 @@
     return one(cols[0] == iota((cols.shape[1], CY), 1).astype(F32))
 
 
-def outgoing(section, tiles, cols, pcat, payload):
-    half = payload.shape[0] // 2
+def outgoing(section, tiles, cols, pcat, packed, payload, sem):
+    half = packed.shape[0]
     lanes = tiles.shape
     last = jnp.broadcast_to(tiles[:, CY - 1 : CY], lanes) * cols[1]
     first = jnp.broadcast_to(tiles[:, 0:1], lanes) * cols[1]
-    packed = pick(pcat[...], jnp.concatenate([tiles, last, first, cols[3]], axis=0))
-    payload[pl.ds(pl.multiple_of(section * half, 8), half)] = jnp.zeros((half, CY), F32)
-    payload[pl.ds(pl.multiple_of((1 - section) * half, 8), half)] = packed
+    packed[...] = pick(pcat[...], jnp.concatenate([tiles, last, first, cols[3]], axis=0))
+    there = payload.at[pl.ds(pl.multiple_of((1 - section) * half, 8), half)]
+    copy = pltpu.make_async_copy(packed, there, sem)
+    copy.start()
+    return copy
 
 
 def link_tables(section, me, n_gy, dest, rows, weight, lines, cols, pcat):
@@ -174,7 +176,7 @@
         xs[2] = wet[pl.ds(start, FIRST)].astype(F32)
 
 
-def load_kernel(n_gy, state, previous, wet, dest, rows, weight, payload, cols, pcat, cur, prev, xs, sides, scale, wet_in, dest_in, rows_in, weight_in, lines, surf, sem):
+def load_kernel(n_gy, state, previous, wet, dest, rows, weight, payload, cols, pcat, cur, prev, xs, sides, wet_in, dest_in, rows_in, weight_in, lines, surf, packed, sem):
     section, p, q = place()
     pairs = [(dest, dest_in), (rows, rows_in), (weight, weight_in)]
     pairs += [(state.at[c], cur.at[c]) for c in (2, 0, 1)]
@@ -189,7 +191,7 @@
         copy.wait()
     surface(section, cur.at[2], cur.at[0], surf)
     tiles = cols[2] * pick(source_pick(cols), surf[...])
-    outgoing(section, tiles, cols, pcat, payload)
+    copies.append(outgoing(section, tiles, cols, pcat, packed, payload, sem.at[8]))
 
     @pl.when(section == 0)
     def _():
@@ -200,14 +202,8 @@
         pack_sides(lambda c, at: wet_in.at[at] if c == 1 else cur.at[c, at], sides, (0, 1, 2))
 
     take_edges(section, p, cur, wet_in, xs)
-    scale[...] = cols[2]
-
-    @pl.when(section != 0)
-    def _():
-        surf[0:FINE] = average(lambda m: wet_in[pl.ds(m, FINE, stride=REFINE)].astype(F32))
-        scale[...] = cols[2] * pick(source_pick(cols), surf[...])
-
-    copies[7].wait()
+    for copy in copies[7:]:
+        copy.wait()
 
 
 def group_rows(it, rows):
@@ -228,14 +224,14 @@
     return pick(one((iota(mine.shape, 0).astype(F32) == sums[5:6]) & ((mine & 7) < CAP)), arrived)
 
 
-def route_kernel(received, base, scale, cols, pcat, payload):
+def route_kernel(received, base, scale, cols, pcat, payload, packed, sem):
     section, _, _ = place()
     arrived = arrived_rows(section, received)
     landing = arrived_sums(arrived)[5:6]
     lane = iota(cols.shape[1:], 1)
     gather = one((cols[0] == landing) & ((lane & 7) < CAP))
     tiles = base[...] + scale[...] * pick(gather, arrived)
-    outgoing(section, tiles, cols, pcat, payload)
+    outgoing(section, tiles, cols, pcat, packed, payload, sem).wait()
 
 
 def edge_addends(sums, period, offset):
@@ -280,9 +276,12 @@
         received, *refs = refs
     cur, prev, *refs = refs
     if last:
-        out, zs, full, halos, co, wet_in, sem = refs
+        out, wet_out, zs, full, halos, co, wet_in, sem = refs
     else:
-        base, xs, sides, zs, full, halos, co, wet_in, sem, surf = refs
+        base, xs, sides, *refs = refs
+        if not linked:
+            scale, *refs = refs
+        zs, full, halos, co, wet_in, sem, surf = refs
     section, p, q = place()
     lane = iota((8, CY), 1)
     sub = iota((8, CY), 0)
@@ -328,6 +327,12 @@
             view = full.at[c, group_rows(it, FIRST + GROUP)]
             view[FIRST : FIRST + GROUP] = cur[c, group_rows(it, GROUP)]
         return carry
+
+    if last:
+
+        @pl.when(section == 0)
+        def _():
+            wet_out[...] = jnp.zeros_like(wet_out)
 
     def views_of(it, ref):
         return [ref.at[c, group_rows(it, GROUP)] for c in range(ref.shape[0])]
@@ -428,13 +433,17 @@
             def _():
                 add_edge(FIRST - REFINE)
 
+        unpack_sides(zs, halos, (0, 2))
+        lax.fori_loop(0, groups, widen, 0)
         wet_load.wait()
         if linked:
             for start, fine in fine_addend(addend):
                 at = pl.ds(start, 8, stride=REFINE)
-                cur[0, at] += wet_in[at].astype(F32) * fine
-        lax.fori_loop(0, groups, widen, 0)
-        unpack_sides(zs, halos, (0, 2))
+                value = cur[0, at] + wet_in[at].astype(F32) * fine
+                cur[0, at] = value
+                full[0, pl.ds(FIRST + start, 8, stride=REFINE)] = value
+        if last:
+            wet_out[...] = wet_in[...]
 
         def group(it, carry):
             load(it).wait()
@@ -487,6 +496,13 @@
         take_edges(section, p, prev, wet_in, xs)
         surface(section, prev.at[2], prev.at[0], surf)
         base[...] = cols[2] * pick(source_pick(cols), surf[...])
+    if not linked:
+        scale[...] = cols[2]
+
+        @pl.when(section != 0)
+        def _():
+            surf[0:FINE] = average(lambda m: wet_in[pl.ds(m, FINE, stride=REFINE)].astype(F32))
+            scale[...] = cols[2] * pick(source_pick(cols), surf[...])
 
 
 def fine_addend(addend):
@@ -498,13 +514,10 @@
             yield 8 * REFINE * m + k, fine
 
 
-def last_kernel(final_in, fields, wet, received, final, height, wet_in, load_sem, sem):
+def last_kernel(final_in, fields, wet, received, final, height, sem):
     section, _, _ = place()
-    load = pltpu.make_async_copy(wet, wet_in, load_sem)
-    load.start()
     arrived = arrived_rows(section, received)
     addend = landed(arrived, arrived_sums(arrived))
-    load.wait()
 
     @pl.when(section == 0)
     def _():
@@ -527,12 +540,17 @@
 
     @pl.when(section != 0)
     def _():
+        part = 8 * REFINE
+        copies = []
         for start, fine in fine_addend(addend):
             at = pl.ds(start, 8, stride=REFINE)
-            height[at] = fields[0, at] + wet_in[at].astype(F32) * fine
-        copy = pltpu.make_async_copy(height, final.at[0], sem.at[0])
-        copy.start()
-        copy.wait()
+            height[at] = fields[0, at] + wet[at].astype(F32) * fine
+            if start % part == REFINE - 1:
+                rows = pl.ds(start // part * part, part)
+                copies.append(pltpu.make_async_copy(height.at[rows], final.at[0, rows], sem.at[len(copies)]))
+                copies[-1].start()
+        for copy in copies:
+            copy.wait()
 
 
 def call(kernel, operands, outs, scratch=(), aliases=None, any_inputs=(), any_outs=(), limit=12, cost=4):
@@ -583,18 +601,18 @@
         return payload.reshape(pairs, CY)
 
     dest, rows, weight = link_dest.reshape(1, links), link_rows.reshape(links, 2).T, link_weight.reshape(1, links)
-    payload, cols, pcat, cur, prev, xs, sides, scale = call(
+    payload, cols, pcat, cur, prev, xs, sides = call(
         functools.partial(load_kernel, n_gy),
         [outside(x) for x in (state, previous, wet, dest, rows, weight)],
         [
             ((pairs, CY), False), ((4, links, CY), True), ((owners * SLOTS, CY), True), fields, fields,
-            edges, sides_out, tiles,
+            edges, sides_out,
         ],
         [
             wet_in, vmem((1, links), jnp.int32), vmem((2, links), jnp.int32),
-            vmem((1, links), F32), vmem((8, CY), F32), surf, dma((8,)),
+            vmem((1, links), F32), vmem((8, CY), F32), surf, vmem((owners * SLOTS, CY), F32), dma((9,)),
         ],
-        any_inputs=range(6),
+        any_inputs=range(6), any_outs=(0,),
     )
     received = exchange(payload)
     swap = [(0, 1), (1, 0)]
@@ -616,26 +634,27 @@
         ]
         more = dict(aliases={0: 0, 1: 1}, any_inputs=(2, 3), cost=64)
         if last:
-            _, new, final = call(
-                kernel, operands, [fields, fields, (field_shape, False)], scratch, any_outs=(2,), **more
+            _, new, final, wet_kept = call(
+                kernel, operands, [fields, fields, (field_shape, False), ((ROWS, CY), True, jnp.int32)], scratch,
+                any_outs=(2,), **more
             )
         else:
-            cur, prev, base, xs, sides = call(
-                kernel, operands, [fields, fields, tiles, edges, sides_out], scratch + [surf], **more
-            )
-            cur, prev = prev, cur
+            outs = [fields, fields, tiles, edges, sides_out] + [tiles] * (before is None)
+            prev, cur, base, xs, sides, *first = call(kernel, operands, outs, scratch + [surf], **more)
+            if first:
+                scale = first[0]
             payload = call(
                 route_kernel, (received, keep(base), keep(scale), keep(cols), keep(pcat)),
-                [((pairs, CY), False)], limit=4,
+                [((pairs, CY), False)], [vmem((owners * SLOTS, CY), F32), dma], any_outs=(0,), limit=4,
             )[0]
             before = received
             received = exchange(payload)
     final = call(
         last_kernel,
-        (outside(final), keep(new), wet, received),
+        (outside(final), keep(new), keep(wet_kept), received),
         [(field_shape, False)],
-        [vmem((ROWS, CY), F32), wet_in, dma, dma((CX,))],
-        aliases={0: 0}, any_inputs=(0, 2), any_outs=(0,),
+        [vmem((ROWS, CY), F32), dma((FINE // 8,))],
+        aliases={0: 0}, any_inputs=(0,), any_outs=(0,),
     )[0]
     return final.reshape(1, 3, 1, 1, -1)
 

time: 65.3 us -> 62.6 us (0.959)
  Pallas kernels: 19.9 us -> 18.4 us
  starting transfers between devices: 32.3 us -> 31 us
  local copies, waits for them, and re-layouts: 0 us -> 0.84 us
  waiting for transfers between devices: 12.4 us -> 11.6 us
    pallas_call x9, Pallas kernels: 19.9 us -> 18.4 us  [call(): pl.pallas_call(kernel, out_shape=[(pltpu.VMEM if kept else jax.ShapeDtype...]
    all_to_all x4, starting transfers between devices: 20.6 us -> 19.3 us  [exchange(): payload = lax.all_to_all(payload, ('sec', 'gx', 'gy'), 0, 0, tiled=True)]
    unnamed x0 -> x4, local copies, waits for them, and re-layouts: none -> 0.84 us
    all_to_all x4, waiting for transfers between devices: 12.3 us -> 11.5 us  [exchange(): payload = lax.all_to_all(payload, ('sec', 'gx', 'gy'), 0, 0, tiled=True)]
  transfers between devices with their start and end apart: 16 -> 16, of which waited for: 4 -> 4; matrix products, arithmetic and copies ran while one was open for 0% -> 0% of each run, Pallas kernels for 23% -> 24%
where the time goes in v2:
time: 62.6 us; the launch traced here: 62.1 us
  starting transfers between devices  31 us (50%)
  Pallas kernels  18.4 us (29%)
  waiting for transfers between devices  11.6 us (19%)
  local copies, waits for them, and re-layouts  0.84 us (1%)
    all_to_all x4, starting transfers between devices, exchange(): payload = lax.all_to_all(payload, ('sec', 'gx', 'gy'), 0, 0, tiled=True)  19.3 us
    pallas_call x9, Pallas kernels, call(): pl.pallas_call(kernel, out_shape=[(pltpu.VMEM if kept else jax.ShapeDtype...  18.4 us
    all_to_all x4, waiting for transfers between devices, exchange(): payload = lax.all_to_all(payload, ('sec', 'gx', 'gy'), 0, 0, tiled=True)  11.5 us
    ppermute x4, starting transfers between devices, on_device(): xr = lax.ppermute(xs, 'gx', swap)  8.2 us
    ppermute x4, starting transfers between devices, on_device(): yrb = lax.ppermute(sides, 'gy', outer)  2.6 us
  transfers between devices with their start and end apart: 16, of which 4 were waited for; matrix products, arithmetic and copies ran while one was open for 0% of the time, Pallas kernels for 24%

profile of v2, /device:TPU:0, one launch (start us, length us, event | category | flops | bytes accessed | tf_op | source)
XLA Modules:
  0.0 62.1 jit_solution(8139655760205726260)
XLA Ops:
  0.0 2.5 %shard_map.73 = (f32[256,128]{1,0:T(8,128)}, f32[4,32,128]{2,1,0:T(8,128)S(1)}, f32[128,128]{1,0:T(8,128)S(1)}, f32[3,800,128]{2,1,0:T(8,128)S(1)}, f32[3,800,12...) custom-call(f32[3,800,128]{2,1,0:T(8,128)} %bitcast.25, f32[3,800,128]{2,1,0:T(8,128)} %bitcast.26, ...), custom_call_target="tpu_custom_call" | custom-call | flops 4000000000 | bytes 4194304 | tf_op jit(solution)/shard_map/pallas_call | solution.py:559
  2.5 0.0 copy-start
  2.5 3.0 %collective-permute-start = (f32[3,104,128]{2,1,0:T(8,128)S(1)}, f32[3,104,128]{2,1,0:T(8,128)S(1)}, u32[]{:S(2)}, u32[]{:S(2)}) collective-permute-start(f32[3,104,128]{2,1,0:T(8,128)S(1)} %get-tuple-element.34), channel_id=1, source_target_pairs={{0,8},{8,0},{1,9},{9,1},{2,10},{10,2},{3,11},{11,3},{4,12},{12,4},... | collective-permute-start | bytes 479240 | tf_op jit(solution)/shard_map/ppermute | solution.py:624
  5.5 0.0 collective-permute-start.1
  5.5 0.7 %collective-permute-start.2 = (f32[3,2,8,128]{3,2,1,0:T(8,128)S(1)}, f32[3,2,8,128]{3,2,1,0:T(8,128)S(1)}, u32[]{:S(2)}, u32[]{:S(2)}) collective-permute-start(f32[3,2,8,128]{3,2,1,0:T(8,128)S(1)} %get-tuple-element.35.refs_8_), channel_id=1, source_target_pairs={{1,2},{2,1},{3,4},{4,3},{5,6},{6,5},{9,10},{10,9},{11,12},{12,11},... | collective-permute-start | bytes 73736 | tf_op jit(solution)/shard_map/ppermute | solution.py:626
  6.2 7.0 %all-to-all-start = ((f32[32,8,128]{2,1,0:T(8,128)}), f32[32,8,128]{2,1,0:T(8,128)S(1)}, u32[]{:S(2)}, u32[]{:S(2)}) async-start(f32[32,8,128]{2,1,0:T(8,128)} %bitcast.8), calls=%async_computation | async-start | bytes 262144 | tf_op jit(solution)/shard_map/all_to_all | solution.py:600
  13.2 0.0 collective-permute-done.1.refs_6_
  13.3 0.0 collective-permute-done.2.refs_7_
  13.3 0.0 collective-permute-done.refs_5_
  13.3 2.9 %shard_map.74 = (f32[3,800,128]{2,1,0:T(8,128)S(1)}, f32[3,800,128]{2,1,0:T(8,128)S(1)}, f32[32,128]{1,0:T(8,128)S(1)}, f32[3,104,128]{2,1,0:T(8,128)S(1)}, f32[...) custom-call(f32[3,800,128]{2,1,0:T(8,128)S(1)} %get-tuple-element.31.refs_0_, ...), custom_call_target="tpu_custom_call", output_to_operand_aliasing={{0}: (0, {}), {1}: (1, {})} | custom-call | flops 64000000000 | bytes 67108864 | tf_op jit(solution)/shard_map/pallas_call | solution.py:559
  16.2 0.3 collective-permute-start.4
  16.5 0.7 %collective-permute-start.5 = (f32[3,2,8,128]{3,2,1,0:T(8,128)S(1)}, f32[3,2,8,128]{3,2,1,0:T(8,128)S(1)}, u32[]{:S(2)}, u32[]{:S(2)}) collective-permute-start(f32[3,2,8,128]{3,2,1,0:T(8,128)S(1)} %get-tuple-element.39.refs_8_), channel_id=1, source_target_pairs={{1,2},{2,1},{3,4},{4,3},{5,6},{6,5},{9,10},{10,9},{11,12},{12,11},... | collective-permute-start | bytes 73736 | tf_op jit(solution)/shard_map/ppermute | solution.py:626
  17.2 1.7 %collective-permute-start.3 = (f32[3,104,128]{2,1,0:T(8,128)S(1)}, f32[3,104,128]{2,1,0:T(8,128)S(1)}, u32[]{:S(2)}, u32[]{:S(2)}) collective-permute-start(f32[3,104,128]{2,1,0:T(8,128)S(1)} %get-tuple-element.38), channel_id=1, source_target_pairs={{0,8},{8,0},{1,9},{9,1},{2,10},{10,2},{3,11},{11,3},{4,12},{12,4},... | collective-permute-start | bytes 479240 | tf_op jit(solution)/shard_map/ppermute | solution.py:624
  18.9 2.5 %all-to-all-done = f32[32,8,128]{2,1,0:T(8,128)S(1)} async-done(((f32[32,8,128]{2,1,0:T(8,128)}), f32[32,8,128]{2,1,0:T(8,128)S(1)}, u32[]{:S(2)}, u32[]{:S(2)}) %all-to-all-start) | async-done | bytes 131104 | tf_op jit(solution)/shard_map/all_to_all | solution.py:600
  21.4 1.0 %shard_map.76 = f32[256,128]{1,0:T(8,128)} custom-call(f32[256,128]{1,0:T(8,128)S(1)} %bitcast.20, f32[32,128]{1,0:T(8,128)S(1)} %get-tuple-element.45.base, f32[32,128]{1,0:T(8,128)S(1)} %get-tuple-element.46.scale, f32[4,32,128]{2,1,0:T(8,128)S(1)} %get-tuple-element.33.refs_4_.cols, f32[128,128]{1,0:T(8,128)S(1)} %get-tuple-element.47.pcat), custom_call_target="tpu_custom_call" | custom-call | flops 4000000000 | bytes 4194304 | tf_op jit(solution)/shard_map/pallas_call | solution.py:559
  22.4 4.2 %all-to-all-start.1 = ((f32[32,8,128]{2,1,0:T(8,128)}), f32[32,8,128]{2,1,0:T(8,128)S(1)}, u32[]{:S(2)}, u32[]{:S(2)}) async-start(f32[32,8,128]{2,1,0:T(8,128)} %bitcast.10), calls=%async_computation.1 | async-start | bytes 262144 | tf_op jit(solution)/shard_map/all_to_all | solution.py:600
  26.6 0.0 collective-permute-done.4.refs_6_
  26.6 0.0 collective-permute-done.5.refs_7_
  26.6 0.0 collective-permute-done.3.refs_5_
  26.6 2.9 %shard_map.75 = (f32[3,800,128]{2,1,0:T(8,128)S(1)}, f32[3,800,128]{2,1,0:T(8,128)S(1)}, f32[32,128]{1,0:T(8,128)S(1)}, f32[3,104,128]{2,1,0:T(8,128)S(1)}, f32[3,2,8,128]{3,2,1,0:T(8,128)S(1)}) custom-call(f32[3,800,128]{2,1,0:T(8,128)S(1)} %get-tuple-element.36.refs_0_, ...), custom_call_target="tpu_custom_call", output_to_operand_aliasing={{0}: (0, {}), {1}: (1, {})} | custom-call | flops 64000000000 | bytes 67108864 | tf_op jit(solution)/shard_map/pallas_call | solution.py:559
  29.5 0.3 collective-permute-start.7
  29.9 0.7 %collective-permute-start.8 = (f32[3,2,8,128]{3,2,1,0:T(8,128)S(1)}, f32[3,2,8,128]{3,2,1,0:T(8,128)S(1)}, u32[]{:S(2)}, u32[]{:S(2)}) collective-permute-start(f32[3,2,8,128]{3,2,1,0:T(8,128)S(1)} %get-tuple-element.44.refs_8_), channel_id=1, source_target_pairs={{1,2},{2,1},{3,4},{4,3},{5,6},{6,5},{9,10},{10,9},{11,12},{12,11},... | collective-permute-start | bytes 73736 | tf_op jit(solution)/shard_map/ppermute | solution.py:626
  30.5 1.7 %collective-permute-start.6 = (f32[3,104,128]{2,1,0:T(8,128)S(1)}, f32[3,104,128]{2,1,0:T(8,128)S(1)}, u32[]{:S(2)}, u32[]{:S(2)}) collective-permute-start(f32[3,104,128]{2,1,0:T(8,128)S(1)} %get-tuple-element.43), channel_id=1, source_target_pairs={{0,8},{8,0},{1,9},{9,1},{2,10},{10,2},{3,11},{11,3},{4,12},{12,4},... | collective-permute-start | bytes 479240 | tf_op jit(solution)/shard_map/ppermute | solution.py:624
  32.3 2.5 %all-to-all-done.1 = f32[32,8,128]{2,1,0:T(8,128)S(1)} async-done(((f32[32,8,128]{2,1,0:T(8,128)}), f32[32,8,128]{2,1,0:T(8,128)S(1)}, u32[]{:S(2)}, u32[]{:S(2)}) %all-to-all-start.1) | async-done | bytes 131104 | tf_op jit(solution)/shard_map/all_to_all | solution.py:600
  34.8 1.0 %shard_map.78 = f32[256,128]{1,0:T(8,128)} custom-call(f32[256,128]{1,0:T(8,128)S(1)} %bitcast.22, f32[32,128]{1,0:T(8,128)S(1)} %get-tuple-element.52.base, f32[32,128]{1,0:T(8,128)S(1)} %get-tuple-element.46.scale, f32[4,32,128]{2,1,0:T(8,128)S(1)} %get-tuple-element.33.refs_4_.cols, f32[128,128]{1,0:T(8,128)S(1)} %get-tuple-element.47.pcat), custom_call_target="tpu_custom_call" | custom-call | flops 4000000000 | bytes 4194304 | tf_op jit(solution)/shard_map/pallas_call | solution.py:559
  35.8 4.0 %all-to-all-start.2 = ((f32[32,8,128]{2,1,0:T(8,128)}), f32[32,8,128]{2,1,0:T(8,128)S(1)}, u32[]{:S(2)}, u32[]{:S(2)}) async-start(f32[32,8,128]{2,1,0:T(8,128)} %bitcast.12), calls=%async_computation.2 | async-start | bytes 262144 | tf_op jit(solution)/shard_map/all_to_all | solution.py:600
  39.8 0.0 collective-permute-done.7.refs_6_
  39.9 0.0 collective-permute-done.8.refs_7_
  39.9 0.0 collective-permute-done.6.refs_5_
  39.9 2.9 %shard_map.77 = (f32[3,800,128]{2,1,0:T(8,128)S(1)}, f32[3,800,128]{2,1,0:T(8,128)S(1)}, f32[32,128]{1,0:T(8,128)S(1)}, f32[3,104,128]{2,1,0:T(8,128)S(1)}, f32[3,2,8,128]{3,2,1,0:T(8,128)S(1)}) custom-call(f32[3,800,128]{2,1,0:T(8,128)S(1)} %get-tuple-element.41.refs_0_, ...), custom_call_target="tpu_custom_call", output_to_operand_aliasing={{0}: (0, {}), {1}: (1, {})} | custom-call | flops 64000000000 | bytes 67108864 | tf_op jit(solution)/shard_map/pallas_call | solution.py:559
  42.8 0.3 collective-permute-start.10
  43.1 0.7 %collective-permute-start.11 = (f32[3,2,8,128]{3,2,1,0:T(8,128)S(1)}, f32[3,2,8,128]{3,2,1,0:T(8,128)S(1)}, u32[]{:S(2)}, u32[]{:S(2)}) collective-permute-start(f32[3,2,8,128]{3,2,1,0:T(8,128)S(1)} %get-tuple-element.51.refs_8_), channel_id=1, source_target_pairs={{1,2},{2,1},{3,4},{4,3},{5,6},{6,5},{9,10},{10,9},{11,12},{12,11},... | collective-permute-start | bytes 73736 | tf_op jit(solution)/shard_map/ppermute | solution.py:626
  43.8 1.7 %collective-permute-start.9 = (f32[3,104,128]{2,1,0:T(8,128)S(1)}, f32[3,104,128]{2,1,0:T(8,128)S(1)}, u32[]{:S(2)}, u32[]{:S(2)}) collective-permute-start(f32[3,104,128]{2,1,0:T(8,128)S(1)} %get-tuple-element.50), channel_id=1, source_target_pairs={{0,8},{8,0},{1,9},{9,1},{2,10},{10,2},{3,11},{11,3},{4,12},{12,4},... | collective-permute-start | bytes 479240 | tf_op jit(solution)/shard_map/ppermute | solution.py:624
  45.5 2.5 %all-to-all-done.2 = f32[32,8,128]{2,1,0:T(8,128)S(1)} async-done(((f32[32,8,128]{2,1,0:T(8,128)}), f32[32,8,128]{2,1,0:T(8,128)S(1)}, u32[]{:S(2)}, u32[]{:S(2)}) %all-to-all-start.2) | async-done | bytes 131104 | tf_op jit(solution)/shard_map/all_to_all | solution.py:600
  48.0 0.0 copy-done
  48.0 1.0 %shard_map.80 = f32[256,128]{1,0:T(8,128)} custom-call(f32[256,128]{1,0:T(8,128)S(1)} %bitcast.18, f32[32,128]{1,0:T(8,128)S(1)} %get-tuple-element.56.base, f32[32,128]{1,0:T(8,128)S(1)} %get-tuple-element.46.scale, f32[4,32,128]{2,1,0:T(8,128)S(1)} %get-tuple-element.33.refs_4_.cols, f32[128,128]{1,0:T(8,128)S(1)} %get-tuple-element.47.pcat), custom_call_target="tpu_custom_call" | custom-call | flops 4000000000 | bytes 4194304 | tf_op jit(solution)/shard_map/pallas_call | solution.py:559
  49.0 4.1 %all-to-all-start.3 = ((f32[32,8,128]{2,1,0:T(8,128)}), f32[32,8,128]{2,1,0:T(8,128)S(1)}, u32[]{:S(2)}, u32[]{:S(2)}) async-start(f32[32,8,128]{2,1,0:T(8,128)} %bitcast.14), calls=%async_computation.3 | async-start | bytes 262144 | tf_op jit(solution)/shard_map/all_to_all | solution.py:600
  53.1 0.0 collective-permute-done.10.refs_6_
  53.1 0.0 collective-permute-done.11.refs_7_
  53.1 0.0 collective-permute-done.9.refs_5_
  53.1 0.0 copy-start.1
  53.1 0.8 %copy-done.1 = f32[4,32,128]{2,1,0:T(8,128)S(1)} copy-done((f32[4,32,128]{2,1,0:T(8,128)S(1)}, f32[4,32,128]{2,1,0:T(8,128)}, u32[]{:S(2)}) %copy-start.1) | copy-done | bytes 65560
  54.0 3.3 %shard_map.79 = (f32[3,800,128]{2,1,0:T(8,128)S(1)}, f32[3,800,128]{2,1,0:T(8,128)S(1)}, f32[3,800,128]{2,1,0:T(8,128)}, s32[800,128]{1,0:T(8,128)S(1)}) custom-call(f32[3,800,128]{2,1,0:T(8,128)S(1)} %get-tuple-element.48.refs_0_, f32[3,800,128]{2,1,0:T(8,128)S(1)} %get-tuple-element.49.refs_1_, ...), custom_call_target="tpu_custom_call", output_to_operand_aliasing={{0}: (0, {}), {1}: (1, {})} | custom-call | flops 64000000000 | bytes 67108864 | tf_op jit(solution)/shard_map/pallas_call | solution.py:559
  57.3 4.0 %all-to-all-done.3 = f32[32,8,128]{2,1,0:T(8,128)S(1)} async-done(((f32[32,8,128]{2,1,0:T(8,128)}), f32[32,8,128]{2,1,0:T(8,128)S(1)}, u32[]{:S(2)}, u32[]{:S(2)}) %all-to-all-start.3) | async-done | bytes 131104 | tf_op jit(solution)/shard_map/all_to_all | solution.py:600
  61.3 0.8 %shard_map.81 = f32[3,800,128]{2,1,0:T(8,128)} custom-call(f32[3,800,128]{2,1,0:T(8,128)} %get-tuple-element.53.final_in, f32[3,800,128]{2,1,0:T(8,128)S(1)} %get-tuple-element.54.fields, s32[800,128]{1,0:T(8,128)S(1)} %get-tuple-element.55.wet, f32[256,128]{1,0:T(8,128)S(1)} %bitcast.24), custom_call_target="tpu_custom_call", output_to_operand_aliasing={{}: (0, {})} | custom-call | flops 4000000000 | bytes 4194304 | tf_op jit(solution)/shard_map/pallas_call | solution.py:559
Async XLA Ops:
  2.5 45.5 %copy-start = (f32[4,32,128]{2,1,0:T(8,128)}, f32[4,32,128]{2,1,0:T(8,128)S(1)}, u32[]{:S(2)}) copy-start(f32[4,32,128]{2,1,0:T(8,128)S(1)} %get-tuple-element.33.refs_4_.cols) | copy-start | bytes 196612
  2.5 10.7 %collective-permute-start = (f32[3,104,128]{2,1,0:T(8,128)S(1)}, f32[3,104,128]{2,1,0:T(8,128)S(1)}, u32[]{:S(2)}, u32[]{:S(2)}) collective-permute-start(f32[3,104,128]{2,1,0:T(8,128)S(1)} %get-tuple-element.34), channel_id=1, source_target_pairs={{0,8},{8,0},{1,9},{9,1},{2,10},{10,2},{3,11},{11,3},{4,12},{12,4},... | collective-permute-start | bytes 479240 | tf_op jit(solution)/shard_map/ppermute | solution.py:624
  5.5 7.7 %collective-permute-start.1 = (f32[3,2,8,128]{3,2,1,0:T(8,128)S(1)}, f32[3,2,8,128]{3,2,1,0:T(8,128)S(1)}, u32[]{:S(2)}, u32[]{:S(2)}) collective-permute-start(f32[3,2,8,128]{3,2,1,0:T(8,128)S(1)} %get-tuple-element.35.refs_8_), channel_id=1, source_target_pairs={{0,1},{1,0},{2,3},{3,2},{4,5},{5,4},{6,7},{7,6},{8,9},{9,8},{10,11... | collective-permute-start | bytes 73736 | tf_op jit(solution)/shard_map/ppermute | solution.py:625
  5.5 7.7 %collective-permute-start.2 = (f32[3,2,8,128]{3,2,1,0:T(8,128)S(1)}, f32[3,2,8,128]{3,2,1,0:T(8,128)S(1)}, u32[]{:S(2)}, u32[]{:S(2)}) collective-permute-start(f32[3,2,8,128]{3,2,1,0:T(8,128)S(1)} %get-tuple-element.35.refs_8_), channel_id=1, source_target_pairs={{1,2},{2,1},{3,4},{4,3},{5,6},{6,5},{9,10},{10,9},{11,12},{12,11},... | collective-permute-start | bytes 73736 | tf_op jit(solution)/shard_map/ppermute | solution.py:626
  6.2 15.2 %all-to-all-start = ((f32[32,8,128]{2,1,0:T(8,128)}), f32[32,8,128]{2,1,0:T(8,128)S(1)}, u32[]{:S(2)}, u32[]{:S(2)}) async-start(f32[32,8,128]{2,1,0:T(8,128)} %bitcast.8), calls=%async_computation | async-start | bytes 262144 | tf_op jit(solution)/shard_map/all_to_all | solution.py:600
  16.2 10.4 %collective-permute-start.4 = (f32[3,2,8,128]{3,2,1,0:T(8,128)S(1)}, f32[3,2,8,128]{3,2,1,0:T(8,128)S(1)}, u32[]{:S(2)}, u32[]{:S(2)}) collective-permute-start(f32[3,2,8,128]{3,2,1,0:T(8,128)S(1)} %get-tuple-element.39.refs_8_), channel_id=1, source_target_pairs={{0,1},{1,0},{2,3},{3,2},{4,5},{5,4},{6,7},{7,6},{8,9},{9,8},{10,11... | collective-permute-start | bytes 73736 | tf_op jit(solution)/shard_map/ppermute | solution.py:625
  16.5 10.1 %collective-permute-start.5 = (f32[3,2,8,128]{3,2,1,0:T(8,128)S(1)}, f32[3,2,8,128]{3,2,1,0:T(8,128)S(1)}, u32[]{:S(2)}, u32[]{:S(2)}) collective-permute-start(f32[3,2,8,128]{3,2,1,0:T(8,128)S(1)} %get-tuple-element.39.refs_8_), channel_id=1, source_target_pairs={{1,2},{2,1},{3,4},{4,3},{5,6},{6,5},{9,10},{10,9},{11,12},{12,11},... | collective-permute-start | bytes 73736 | tf_op jit(solution)/shard_map/ppermute | solution.py:626
  17.2 9.5 %collective-permute-start.3 = (f32[3,104,128]{2,1,0:T(8,128)S(1)}, f32[3,104,128]{2,1,0:T(8,128)S(1)}, u32[]{:S(2)}, u32[]{:S(2)}) collective-permute-start(f32[3,104,128]{2,1,0:T(8,128)S(1)} %get-tuple-element.38), channel_id=1, source_target_pairs={{0,8},{8,0},{1,9},{9,1},{2,10},{10,2},{3,11},{11,3},{4,12},{12,4},... | collective-permute-start | bytes 479240 | tf_op jit(solution)/shard_map/ppermute | solution.py:624
  22.4 12.3 %all-to-all-start.1 = ((f32[32,8,128]{2,1,0:T(8,128)}), f32[32,8,128]{2,1,0:T(8,128)S(1)}, u32[]{:S(2)}, u32[]{:S(2)}) async-start(f32[32,8,128]{2,1,0:T(8,128)} %bitcast.10), calls=%async_computation.1 | async-start | bytes 262144 | tf_op jit(solution)/shard_map/all_to_all | solution.py:600
  29.5 10.3 %collective-permute-start.7 = (f32[3,2,8,128]{3,2,1,0:T(8,128)S(1)}, f32[3,2,8,128]{3,2,1,0:T(8,128)S(1)}, u32[]{:S(2)}, u32[]{:S(2)}) collective-permute-start(f32[3,2,8,128]{3,2,1,0:T(8,128)S(1)} %get-tuple-element.44.refs_8_), channel_id=1, source_target_pairs={{0,1},{1,0},{2,3},{3,2},{4,5},{5,4},{6,7},{7,6},{8,9},{9,8},{10,11... | collective-permute-start | bytes 73736 | tf_op jit(solution)/shard_map/ppermute | solution.py:625
  29.9 10.0 %collective-permute-start.8 = (f32[3,2,8,128]{3,2,1,0:T(8,128)S(1)}, f32[3,2,8,128]{3,2,1,0:T(8,128)S(1)}, u32[]{:S(2)}, u32[]{:S(2)}) collective-permute-start(f32[3,2,8,128]{3,2,1,0:T(8,128)S(1)} %get-tuple-element.44.refs_8_), channel_id=1, source_target_pairs={{1,2},{2,1},{3,4},{4,3},{5,6},{6,5},{9,10},{10,9},{11,12},{12,11},... | collective-permute-start | bytes 73736 | tf_op jit(solution)/shard_map/ppermute | solution.py:626
  30.5 9.3 %collective-permute-start.6 = (f32[3,104,128]{2,1,0:T(8,128)S(1)}, f32[3,104,128]{2,1,0:T(8,128)S(1)}, u32[]{:S(2)}, u32[]{:S(2)}) collective-permute-start(f32[3,104,128]{2,1,0:T(8,128)S(1)} %get-tuple-element.43), channel_id=1, source_target_pairs={{0,8},{8,0},{1,9},{9,1},{2,10},{10,2},{3,11},{11,3},{4,12},{12,4},... | collective-permute-start | bytes 479240 | tf_op jit(solution)/shard_map/ppermute | solution.py:624
  35.8 12.2 %all-to-all-start.2 = ((f32[32,8,128]{2,1,0:T(8,128)}), f32[32,8,128]{2,1,0:T(8,128)S(1)}, u32[]{:S(2)}, u32[]{:S(2)}) async-start(f32[32,8,128]{2,1,0:T(8,128)} %bitcast.12), calls=%async_computation.2 | async-start | bytes 262144 | tf_op jit(solution)/shard_map/all_to_all | solution.py:600
  42.8 10.3 %collective-permute-start.10 = (f32[3,2,8,128]{3,2,1,0:T(8,128)S(1)}, f32[3,2,8,128]{3,2,1,0:T(8,128)S(1)}, u32[]{:S(2)}, u32[]{:S(2)}) collective-permute-start(f32[3,2,8,128]{3,2,1,0:T(8,128)S(1)} %get-tuple-element.51.refs_8_), channel_id=1, source_target_pairs={{0,1},{1,0},{2,3},{3,2},{4,5},{5,4},{6,7},{7,6},{8,9},{9,8},{10,11... | collective-permute-start | bytes 73736 | tf_op jit(solution)/shard_map/ppermute | solution.py:625
  43.1 10.0 %collective-permute-start.11 = (f32[3,2,8,128]{3,2,1,0:T(8,128)S(1)}, f32[3,2,8,128]{3,2,1,0:T(8,128)S(1)}, u32[]{:S(2)}, u32[]{:S(2)}) collective-permute-start(f32[3,2,8,128]{3,2,1,0:T(8,128)S(1)} %get-tuple-element.51.refs_8_), channel_id=1, source_target_pairs={{1,2},{2,1},{3,4},{4,3},{5,6},{6,5},{9,10},{10,9},{11,12},{12,11},... | collective-permute-start | bytes 73736 | tf_op jit(solution)/shard_map/ppermute | solution.py:626
  43.8 9.4 %collective-permute-start.9 = (f32[3,104,128]{2,1,0:T(8,128)S(1)}, f32[3,104,128]{2,1,0:T(8,128)S(1)}, u32[]{:S(2)}, u32[]{:S(2)}) collective-permute-start(f32[3,104,128]{2,1,0:T(8,128)S(1)} %get-tuple-element.50), channel_id=1, source_target_pairs={{0,8},{8,0},{1,9},{9,1},{2,10},{10,2},{3,11},{11,3},{4,12},{12,4},... | collective-permute-start | bytes 479240 | tf_op jit(solution)/shard_map/ppermute | solution.py:624
  49.0 12.2 %all-to-all-start.3 = ((f32[32,8,128]{2,1,0:T(8,128)}), f32[32,8,128]{2,1,0:T(8,128)S(1)}, u32[]{:S(2)}, u32[]{:S(2)}) async-start(f32[32,8,128]{2,1,0:T(8,128)} %bitcast.14), calls=%async_computation.3 | async-start | bytes 262144 | tf_op jit(solution)/shard_map/all_to_all | solution.py:600
  53.1 0.8 %copy-start.1 = (f32[4,32,128]{2,1,0:T(8,128)S(1)}, f32[4,32,128]{2,1,0:T(8,128)}, u32[]{:S(2)}) copy-start(f32[4,32,128]{2,1,0:T(8,128)} %copy-done) | copy-start | bytes 196612

commit v3 on v2

--- a/solution.py
+++ b/solution.py
@@ -178,20 +178,23 @@
 
 def load_kernel(n_gy, state, previous, wet, dest, rows, weight, payload, cols, pcat, cur, prev, xs, sides, wet_in, dest_in, rows_in, weight_in, lines, surf, packed, sem):
     section, p, q = place()
+    linked = 2 * (1 - section)
     pairs = [(dest, dest_in), (rows, rows_in), (weight, weight_in)]
-    pairs += [(state.at[c], cur.at[c]) for c in (2, 0, 1)]
+    pairs += [(state.at[c], cur.at[c]) for c in (linked, 1, 2 - linked)]
     pairs += [(wet, wet_in), (previous, prev)]
     copies = [pltpu.make_async_copy(a, b, sem.at[i]) for i, (a, b) in enumerate(pairs)]
-    for copy in copies:
+    for copy in copies[0:7]:
         copy.start()
     for copy in copies[0:3]:
         copy.wait()
     link_tables(section, p * n_gy + q, n_gy, dest_in, rows_in, weight_in, lines, cols, pcat)
-    for copy in copies[3:7]:
-        copy.wait()
+    copies[3].wait()
+    copies[7].start()
     surface(section, cur.at[2], cur.at[0], surf)
     tiles = cols[2] * pick(source_pick(cols), surf[...])
     copies.append(outgoing(section, tiles, cols, pcat, packed, payload, sem.at[8]))
+    for copy in copies[4:7]:
+        copy.wait()
 
     @pl.when(section == 0)
     def _():

time: 62.6 us -> 62.4 us (level)
  no operation moved by 1% of the time
where the time goes in v3:
time: 62.4 us; the launch traced here: 61.8 us
  starting transfers between devices  30.7 us (49%)
  Pallas kernels  18.4 us (29%)
  waiting for transfers between devices  11.6 us (19%)
  local copies, waits for them, and re-layouts  0.84 us (1%)
    all_to_all x4, starting transfers between devices, exchange(): payload = lax.all_to_all(payload, ('sec', 'gx', 'gy'), 0, 0, tiled=True)  19 us
    pallas_call x9, Pallas kernels, call(): pl.pallas_call(kernel, out_shape=[(pltpu.VMEM if kept else jax.ShapeDtype...  18.4 us
    all_to_all x4, waiting for transfers between devices, exchange(): payload = lax.all_to_all(payload, ('sec', 'gx', 'gy'), 0, 0, tiled=True)  11.5 us
    ppermute x4, starting transfers between devices, on_device(): xr = lax.ppermute(xs, 'gx', swap)  8.2 us
    ppermute x4, starting transfers between devices, on_device(): yrb = lax.ppermute(sides, 'gy', outer)  2.6 us
  transfers between devices with their start and end apart: 16, of which 4 were waited for; matrix products, arithmetic and copies ran while one was open for 0% of the time, Pallas kernels for 24%

profile of v3, /device:TPU:0, one launch (start us, length us, event | category | flops | bytes accessed | tf_op | source)
XLA Modules:
  0.0 61.8 jit_solution(12734815035155558689)
XLA Ops:
  0.0 2.5 %shard_map.73 = (f32[256,128]{1,0:T(8,128)}, f32[4,32,128]{2,1,0:T(8,128)S(1)}, f32[128,128]{1,0:T(8,128)S(1)}, f32[3,800,128]{2,1,0:T(8,128)S(1)}, f32[3,800,12...) custom-call(f32[3,800,128]{2,1,0:T(8,128)} %bitcast.25, f32[3,800,128]{2,1,0:T(8,128)} %bitcast.26, ...), custom_call_target="tpu_custom_call" | custom-call | flops 4000000000 | bytes 4194304 | tf_op jit(solution)/shard_map/pallas_call | solution.py:562
  2.5 0.0 copy-start
  2.5 3.0 %collective-permute-start = (f32[3,104,128]{2,1,0:T(8,128)S(1)}, f32[3,104,128]{2,1,0:T(8,128)S(1)}, u32[]{:S(2)}, u32[]{:S(2)}) collective-permute-start(f32[3,104,128]{2,1,0:T(8,128)S(1)} %get-tuple-element.34), channel_id=1, source_target_pairs={{0,8},{8,0},{1,9},{9,1},{2,10},{10,2},{3,11},{11,3},{4,12},{12,4},... | collective-permute-start | bytes 479240 | tf_op jit(solution)/shard_map/ppermute | solution.py:627
  5.5 0.0 collective-permute-start.1
  5.5 0.7 %collective-permute-start.2 = (f32[3,2,8,128]{3,2,1,0:T(8,128)S(1)}, f32[3,2,8,128]{3,2,1,0:T(8,128)S(1)}, u32[]{:S(2)}, u32[]{:S(2)}) collective-permute-start(f32[3,2,8,128]{3,2,1,0:T(8,128)S(1)} %get-tuple-element.35.refs_8_), channel_id=1, source_target_pairs={{1,2},{2,1},{3,4},{4,3},{5,6},{6,5},{9,10},{10,9},{11,12},{12,11},... | collective-permute-start | bytes 73736 | tf_op jit(solution)/shard_map/ppermute | solution.py:629
  6.2 6.7 %all-to-all-start = ((f32[32,8,128]{2,1,0:T(8,128)}), f32[32,8,128]{2,1,0:T(8,128)S(1)}, u32[]{:S(2)}, u32[]{:S(2)}) async-start(f32[32,8,128]{2,1,0:T(8,128)} %bitcast.8), calls=%async_computation | async-start | bytes 262144 | tf_op jit(solution)/shard_map/all_to_all | solution.py:603
  12.9 0.0 collective-permute-done.1.refs_6_
  12.9 0.0 collective-permute-done.2.refs_7_
  13.0 0.0 collective-permute-done.refs_5_
  13.0 2.9 %shard_map.74 = (f32[3,800,128]{2,1,0:T(8,128)S(1)}, f32[3,800,128]{2,1,0:T(8,128)S(1)}, f32[32,128]{1,0:T(8,128)S(1)}, f32[3,104,128]{2,1,0:T(8,128)S(1)}, f32[...) custom-call(f32[3,800,128]{2,1,0:T(8,128)S(1)} %get-tuple-element.31.refs_0_, ...), custom_call_target="tpu_custom_call", output_to_operand_aliasing={{0}: (0, {}), {1}: (1, {})} | custom-call | flops 64000000000 | bytes 67108864 | tf_op jit(solution)/shard_map/pallas_call | solution.py:562
  15.9 0.3 collective-permute-start.4
  16.2 0.7 %collective-permute-start.5 = (f32[3,2,8,128]{3,2,1,0:T(8,128)S(1)}, f32[3,2,8,128]{3,2,1,0:T(8,128)S(1)}, u32[]{:S(2)}, u32[]{:S(2)}) collective-permute-start(f32[3,2,8,128]{3,2,1,0:T(8,128)S(1)} %get-tuple-element.39.refs_8_), channel_id=1, source_target_pairs={{1,2},{2,1},{3,4},{4,3},{5,6},{6,5},{9,10},{10,9},{11,12},{12,11},... | collective-permute-start | bytes 73736 | tf_op jit(solution)/shard_map/ppermute | solution.py:629
  16.9 1.7 %collective-permute-start.3 = (f32[3,104,128]{2,1,0:T(8,128)S(1)}, f32[3,104,128]{2,1,0:T(8,128)S(1)}, u32[]{:S(2)}, u32[]{:S(2)}) collective-permute-start(f32[3,104,128]{2,1,0:T(8,128)S(1)} %get-tuple-element.38), channel_id=1, source_target_pairs={{0,8},{8,0},{1,9},{9,1},{2,10},{10,2},{3,11},{11,3},{4,12},{12,4},... | collective-permute-start | bytes 479240 | tf_op jit(solution)/shard_map/ppermute | solution.py:627
  18.6 2.5 %all-to-all-done = f32[32,8,128]{2,1,0:T(8,128)S(1)} async-done(((f32[32,8,128]{2,1,0:T(8,128)}), f32[32,8,128]{2,1,0:T(8,128)S(1)}, u32[]{:S(2)}, u32[]{:S(2)}) %all-to-all-start) | async-done | bytes 131104 | tf_op jit(solution)/shard_map/all_to_all | solution.py:603
  21.1 1.0 %shard_map.76 = f32[256,128]{1,0:T(8,128)} custom-call(f32[256,128]{1,0:T(8,128)S(1)} %bitcast.20, f32[32,128]{1,0:T(8,128)S(1)} %get-tuple-element.45.base, f32[32,128]{1,0:T(8,128)S(1)} %get-tuple-element.46.scale, f32[4,32,128]{2,1,0:T(8,128)S(1)} %get-tuple-element.33.refs_4_.cols, f32[128,128]{1,0:T(8,128)S(1)} %get-tuple-element.47.pcat), custom_call_target="tpu_custom_call" | custom-call | flops 4000000000 | bytes 4194304 | tf_op jit(solution)/shard_map/pallas_call | solution.py:562
  22.1 4.2 %all-to-all-start.1 = ((f32[32,8,128]{2,1,0:T(8,128)}), f32[32,8,128]{2,1,0:T(8,128)S(1)}, u32[]{:S(2)}, u32[]{:S(2)}) async-start(f32[32,8,128]{2,1,0:T(8,128)} %bitcast.10), calls=%async_computation.1 | async-start | bytes 262144 | tf_op jit(solution)/shard_map/all_to_all | solution.py:603
  26.3 0.0 collective-permute-done.4.refs_6_
  26.3 0.0 collective-permute-done.5.refs_7_
  26.3 0.0 collective-permute-done.3.refs_5_
  26.3 2.9 %shard_map.75 = (f32[3,800,128]{2,1,0:T(8,128)S(1)}, f32[3,800,128]{2,1,0:T(8,128)S(1)}, f32[32,128]{1,0:T(8,128)S(1)}, f32[3,104,128]{2,1,0:T(8,128)S(1)}, f32[3,2,8,128]{3,2,1,0:T(8,128)S(1)}) custom-call(f32[3,800,128]{2,1,0:T(8,128)S(1)} %get-tuple-element.36.refs_0_, ...), custom_call_target="tpu_custom_call", output_to_operand_aliasing={{0}: (0, {}), {1}: (1, {})} | custom-call | flops 64000000000 | bytes 67108864 | tf_op jit(solution)/shard_map/pallas_call | solution.py:562
  29.2 0.3 collective-permute-start.7
  29.6 0.7 %collective-permute-start.8 = (f32[3,2,8,128]{3,2,1,0:T(8,128)S(1)}, f32[3,2,8,128]{3,2,1,0:T(8,128)S(1)}, u32[]{:S(2)}, u32[]{:S(2)}) collective-permute-start(f32[3,2,8,128]{3,2,1,0:T(8,128)S(1)} %get-tuple-element.44.refs_8_), channel_id=1, source_target_pairs={{1,2},{2,1},{3,4},{4,3},{5,6},{6,5},{9,10},{10,9},{11,12},{12,11},... | collective-permute-start | bytes 73736 | tf_op jit(solution)/shard_map/ppermute | solution.py:629
  30.2 1.7 %collective-permute-start.6 = (f32[3,104,128]{2,1,0:T(8,128)S(1)}, f32[3,104,128]{2,1,0:T(8,128)S(1)}, u32[]{:S(2)}, u32[]{:S(2)}) collective-permute-start(f32[3,104,128]{2,1,0:T(8,128)S(1)} %get-tuple-element.43), channel_id=1, source_target_pairs={{0,8},{8,0},{1,9},{9,1},{2,10},{10,2},{3,11},{11,3},{4,12},{12,4},... | collective-permute-start | bytes 479240 | tf_op jit(solution)/shard_map/ppermute | solution.py:627
  31.9 2.5 %all-to-all-done.1 = f32[32,8,128]{2,1,0:T(8,128)S(1)} async-done(((f32[32,8,128]{2,1,0:T(8,128)}), f32[32,8,128]{2,1,0:T(8,128)S(1)}, u32[]{:S(2)}, u32[]{:S(2)}) %all-to-all-start.1) | async-done | bytes 131104 | tf_op jit(solution)/shard_map/all_to_all | solution.py:603
  34.5 1.0 %shard_map.78 = f32[256,128]{1,0:T(8,128)} custom-call(f32[256,128]{1,0:T(8,128)S(1)} %bitcast.22, f32[32,128]{1,0:T(8,128)S(1)} %get-tuple-element.52.base, f32[32,128]{1,0:T(8,128)S(1)} %get-tuple-element.46.scale, f32[4,32,128]{2,1,0:T(8,128)S(1)} %get-tuple-element.33.refs_4_.cols, f32[128,128]{1,0:T(8,128)S(1)} %get-tuple-element.47.pcat), custom_call_target="tpu_custom_call" | custom-call | flops 4000000000 | bytes 4194304 | tf_op jit(solution)/shard_map/pallas_call | solution.py:562
  35.5 4.0 %all-to-all-start.2 = ((f32[32,8,128]{2,1,0:T(8,128)}), f32[32,8,128]{2,1,0:T(8,128)S(1)}, u32[]{:S(2)}, u32[]{:S(2)}) async-start(f32[32,8,128]{2,1,0:T(8,128)} %bitcast.12), calls=%async_computation.2 | async-start | bytes 262144 | tf_op jit(solution)/shard_map/all_to_all | solution.py:603
  39.5 0.0 collective-permute-done.7.refs_6_
  39.5 0.0 collective-permute-done.8.refs_7_
  39.6 0.0 collective-permute-done.6.refs_5_
  39.6 2.9 %shard_map.77 = (f32[3,800,128]{2,1,0:T(8,128)S(1)}, f32[3,800,128]{2,1,0:T(8,128)S(1)}, f32[32,128]{1,0:T(8,128)S(1)}, f32[3,104,128]{2,1,0:T(8,128)S(1)}, f32[3,2,8,128]{3,2,1,0:T(8,128)S(1)}) custom-call(f32[3,800,128]{2,1,0:T(8,128)S(1)} %get-tuple-element.41.refs_0_, ...), custom_call_target="tpu_custom_call", output_to_operand_aliasing={{0}: (0, {}), {1}: (1, {})} | custom-call | flops 64000000000 | bytes 67108864 | tf_op jit(solution)/shard_map/pallas_call | solution.py:562
  42.5 0.3 collective-permute-start.10
  42.8 0.7 %collective-permute-start.11 = (f32[3,2,8,128]{3,2,1,0:T(8,128)S(1)}, f32[3,2,8,128]{3,2,1,0:T(8,128)S(1)}, u32[]{:S(2)}, u32[]{:S(2)}) collective-permute-start(f32[3,2,8,128]{3,2,1,0:T(8,128)S(1)} %get-tuple-element.51.refs_8_), channel_id=1, source_target_pairs={{1,2},{2,1},{3,4},{4,3},{5,6},{6,5},{9,10},{10,9},{11,12},{12,11},... | collective-permute-start | bytes 73736 | tf_op jit(solution)/shard_map/ppermute | solution.py:629
  43.5 1.7 %collective-permute-start.9 = (f32[3,104,128]{2,1,0:T(8,128)S(1)}, f32[3,104,128]{2,1,0:T(8,128)S(1)}, u32[]{:S(2)}, u32[]{:S(2)}) collective-permute-start(f32[3,104,128]{2,1,0:T(8,128)S(1)} %get-tuple-element.50), channel_id=1, source_target_pairs={{0,8},{8,0},{1,9},{9,1},{2,10},{10,2},{3,11},{11,3},{4,12},{12,4},... | collective-permute-start | bytes 479240 | tf_op jit(solution)/shard_map/ppermute | solution.py:627
  45.2 2.5 %all-to-all-done.2 = f32[32,8,128]{2,1,0:T(8,128)S(1)} async-done(((f32[32,8,128]{2,1,0:T(8,128)}), f32[32,8,128]{2,1,0:T(8,128)S(1)}, u32[]{:S(2)}, u32[]{:S(2)}) %all-to-all-start.2) | async-done | bytes 131104 | tf_op jit(solution)/shard_map/all_to_all | solution.py:603
  47.7 0.0 copy-done
  47.7 1.0 %shard_map.80 = f32[256,128]{1,0:T(8,128)} custom-call(f32[256,128]{1,0:T(8,128)S(1)} %bitcast.18, f32[32,128]{1,0:T(8,128)S(1)} %get-tuple-element.56.base, f32[32,128]{1,0:T(8,128)S(1)} %get-tuple-element.46.scale, f32[4,32,128]{2,1,0:T(8,128)S(1)} %get-tuple-element.33.refs_4_.cols, f32[128,128]{1,0:T(8,128)S(1)} %get-tuple-element.47.pcat), custom_call_target="tpu_custom_call" | custom-call | flops 4000000000 | bytes 4194304 | tf_op jit(solution)/shard_map/pallas_call | solution.py:562
  48.7 4.1 %all-to-all-start.3 = ((f32[32,8,128]{2,1,0:T(8,128)}), f32[32,8,128]{2,1,0:T(8,128)S(1)}, u32[]{:S(2)}, u32[]{:S(2)}) async-start(f32[32,8,128]{2,1,0:T(8,128)} %bitcast.14), calls=%async_computation.3 | async-start | bytes 262144 | tf_op jit(solution)/shard_map/all_to_all | solution.py:603
  52.8 0.0 collective-permute-done.10.refs_6_
  52.8 0.0 collective-permute-done.11.refs_7_
  52.8 0.0 collective-permute-done.9.refs_5_
  52.8 0.0 copy-start.1
  52.8 0.8 %copy-done.1 = f32[4,32,128]{2,1,0:T(8,128)S(1)} copy-done((f32[4,32,128]{2,1,0:T(8,128)S(1)}, f32[4,32,128]{2,1,0:T(8,128)}, u32[]{:S(2)}) %copy-start.1) | copy-done | bytes 65560
  53.7 3.3 %shard_map.79 = (f32[3,800,128]{2,1,0:T(8,128)S(1)}, f32[3,800,128]{2,1,0:T(8,128)S(1)}, f32[3,800,128]{2,1,0:T(8,128)}, s32[800,128]{1,0:T(8,128)S(1)}) custom-call(f32[3,800,128]{2,1,0:T(8,128)S(1)} %get-tuple-element.48.refs_0_, f32[3,800,128]{2,1,0:T(8,128)S(1)} %get-tuple-element.49.refs_1_, ...), custom_call_target="tpu_custom_call", output_to_operand_aliasing={{0}: (0, {}), {1}: (1, {})} | custom-call | flops 64000000000 | bytes 67108864 | tf_op jit(solution)/shard_map/pallas_call | solution.py:562
  57.0 4.0 %all-to-all-done.3 = f32[32,8,128]{2,1,0:T(8,128)S(1)} async-done(((f32[32,8,128]{2,1,0:T(8,128)}), f32[32,8,128]{2,1,0:T(8,128)S(1)}, u32[]{:S(2)}, u32[]{:S(2)}) %all-to-all-start.3) | async-done | bytes 131104 | tf_op jit(solution)/shard_map/all_to_all | solution.py:603
  61.0 0.8 %shard_map.81 = f32[3,800,128]{2,1,0:T(8,128)} custom-call(f32[3,800,128]{2,1,0:T(8,128)} %get-tuple-element.53.final_in, f32[3,800,128]{2,1,0:T(8,128)S(1)} %get-tuple-element.54.fields, s32[800,128]{1,0:T(8,128)S(1)} %get-tuple-element.55.wet, f32[256,128]{1,0:T(8,128)S(1)} %bitcast.24), custom_call_target="tpu_custom_call", output_to_operand_aliasing={{}: (0, {})} | custom-call | flops 4000000000 | bytes 4194304 | tf_op jit(solution)/shard_map/pallas_call | solution.py:562
Async XLA Ops:
  2.5 45.2 %copy-start = (f32[4,32,128]{2,1,0:T(8,128)}, f32[4,32,128]{2,1,0:T(8,128)S(1)}, u32[]{:S(2)}) copy-start(f32[4,32,128]{2,1,0:T(8,128)S(1)} %get-tuple-element.33.refs_4_.cols) | copy-start | bytes 196612
  2.5 10.4 %collective-permute-start = (f32[3,104,128]{2,1,0:T(8,128)S(1)}, f32[3,104,128]{2,1,0:T(8,128)S(1)}, u32[]{:S(2)}, u32[]{:S(2)}) collective-permute-start(f32[3,104,128]{2,1,0:T(8,128)S(1)} %get-tuple-element.34), channel_id=1, source_target_pairs={{0,8},{8,0},{1,9},{9,1},{2,10},{10,2},{3,11},{11,3},{4,12},{12,4},... | collective-permute-start | bytes 479240 | tf_op jit(solution)/shard_map/ppermute | solution.py:627
  5.5 7.4 %collective-permute-start.1 = (f32[3,2,8,128]{3,2,1,0:T(8,128)S(1)}, f32[3,2,8,128]{3,2,1,0:T(8,128)S(1)}, u32[]{:S(2)}, u32[]{:S(2)}) collective-permute-start(f32[3,2,8,128]{3,2,1,0:T(8,128)S(1)} %get-tuple-element.35.refs_8_), channel_id=1, source_target_pairs={{0,1},{1,0},{2,3},{3,2},{4,5},{5,4},{6,7},{7,6},{8,9},{9,8},{10,11... | collective-permute-start | bytes 73736 | tf_op jit(solution)/shard_map/ppermute | solution.py:628
  5.5 7.4 %collective-permute-start.2 = (f32[3,2,8,128]{3,2,1,0:T(8,128)S(1)}, f32[3,2,8,128]{3,2,1,0:T(8,128)S(1)}, u32[]{:S(2)}, u32[]{:S(2)}) collective-permute-start(f32[3,2,8,128]{3,2,1,0:T(8,128)S(1)} %get-tuple-element.35.refs_8_), channel_id=1, source_target_pairs={{1,2},{2,1},{3,4},{4,3},{5,6},{6,5},{9,10},{10,9},{11,12},{12,11},... | collective-permute-start | bytes 73736 | tf_op jit(solution)/shard_map/ppermute | solution.py:629
  6.2 14.9 %all-to-all-start = ((f32[32,8,128]{2,1,0:T(8,128)}), f32[32,8,128]{2,1,0:T(8,128)S(1)}, u32[]{:S(2)}, u32[]{:S(2)}) async-start(f32[32,8,128]{2,1,0:T(8,128)} %bitcast.8), calls=%async_computation | async-start | bytes 262144 | tf_op jit(solution)/shard_map/all_to_all | solution.py:603
  15.9 10.4 %collective-permute-start.4 = (f32[3,2,8,128]{3,2,1,0:T(8,128)S(1)}, f32[3,2,8,128]{3,2,1,0:T(8,128)S(1)}, u32[]{:S(2)}, u32[]{:S(2)}) collective-permute-start(f32[3,2,8,128]{3,2,1,0:T(8,128)S(1)} %get-tuple-element.39.refs_8_), channel_id=1, source_target_pairs={{0,1},{1,0},{2,3},{3,2},{4,5},{5,4},{6,7},{7,6},{8,9},{9,8},{10,11... | collective-permute-start | bytes 73736 | tf_op jit(solution)/shard_map/ppermute | solution.py:628
  16.2 10.1 %collective-permute-start.5 = (f32[3,2,8,128]{3,2,1,0:T(8,128)S(1)}, f32[3,2,8,128]{3,2,1,0:T(8,128)S(1)}, u32[]{:S(2)}, u32[]{:S(2)}) collective-permute-start(f32[3,2,8,128]{3,2,1,0:T(8,128)S(1)} %get-tuple-element.39.refs_8_), channel_id=1, source_target_pairs={{1,2},{2,1},{3,4},{4,3},{5,6},{6,5},{9,10},{10,9},{11,12},{12,11},... | collective-permute-start | bytes 73736 | tf_op jit(solution)/shard_map/ppermute | solution.py:629
  16.9 9.5 %collective-permute-start.3 = (f32[3,104,128]{2,1,0:T(8,128)S(1)}, f32[3,104,128]{2,1,0:T(8,128)S(1)}, u32[]{:S(2)}, u32[]{:S(2)}) collective-permute-start(f32[3,104,128]{2,1,0:T(8,128)S(1)} %get-tuple-element.38), channel_id=1, source_target_pairs={{0,8},{8,0},{1,9},{9,1},{2,10},{10,2},{3,11},{11,3},{4,12},{12,4},... | collective-permute-start | bytes 479240 | tf_op jit(solution)/shard_map/ppermute | solution.py:627
  22.1 12.3 %all-to-all-start.1 = ((f32[32,8,128]{2,1,0:T(8,128)}), f32[32,8,128]{2,1,0:T(8,128)S(1)}, u32[]{:S(2)}, u32[]{:S(2)}) async-start(f32[32,8,128]{2,1,0:T(8,128)} %bitcast.10), calls=%async_computation.1 | async-start | bytes 262144 | tf_op jit(solution)/shard_map/all_to_all | solution.py:603
  29.2 10.3 %collective-permute-start.7 = (f32[3,2,8,128]{3,2,1,0:T(8,128)S(1)}, f32[3,2,8,128]{3,2,1,0:T(8,128)S(1)}, u32[]{:S(2)}, u32[]{:S(2)}) collective-permute-start(f32[3,2,8,128]{3,2,1,0:T(8,128)S(1)} %get-tuple-element.44.refs_8_), channel_id=1, source_target_pairs={{0,1},{1,0},{2,3},{3,2},{4,5},{5,4},{6,7},{7,6},{8,9},{9,8},{10,11... | collective-permute-start | bytes 73736 | tf_op jit(solution)/shard_map/ppermute | solution.py:628
  29.6 10.0 %collective-permute-start.8 = (f32[3,2,8,128]{3,2,1,0:T(8,128)S(1)}, f32[3,2,8,128]{3,2,1,0:T(8,128)S(1)}, u32[]{:S(2)}, u32[]{:S(2)}) collective-permute-start(f32[3,2,8,128]{3,2,1,0:T(8,128)S(1)} %get-tuple-element.44.refs_8_), channel_id=1, source_target_pairs={{1,2},{2,1},{3,4},{4,3},{5,6},{6,5},{9,10},{10,9},{11,12},{12,11},... | collective-permute-start | bytes 73736 | tf_op jit(solution)/shard_map/ppermute | solution.py:629
  30.2 9.3 %collective-permute-start.6 = (f32[3,104,128]{2,1,0:T(8,128)S(1)}, f32[3,104,128]{2,1,0:T(8,128)S(1)}, u32[]{:S(2)}, u32[]{:S(2)}) collective-permute-start(f32[3,104,128]{2,1,0:T(8,128)S(1)} %get-tuple-element.43), channel_id=1, source_target_pairs={{0,8},{8,0},{1,9},{9,1},{2,10},{10,2},{3,11},{11,3},{4,12},{12,4},... | collective-permute-start | bytes 479240 | tf_op jit(solution)/shard_map/ppermute | solution.py:627
  35.5 12.2 %all-to-all-start.2 = ((f32[32,8,128]{2,1,0:T(8,128)}), f32[32,8,128]{2,1,0:T(8,128)S(1)}, u32[]{:S(2)}, u32[]{:S(2)}) async-start(f32[32,8,128]{2,1,0:T(8,128)} %bitcast.12), calls=%async_computation.2 | async-start | bytes 262144 | tf_op jit(solution)/shard_map/all_to_all | solution.py:603
  42.5 10.3 %collective-permute-start.10 = (f32[3,2,8,128]{3,2,1,0:T(8,128)S(1)}, f32[3,2,8,128]{3,2,1,0:T(8,128)S(1)}, u32[]{:S(2)}, u32[]{:S(2)}) collective-permute-start(f32[3,2,8,128]{3,2,1,0:T(8,128)S(1)} %get-tuple-element.51.refs_8_), channel_id=1, source_target_pairs={{0,1},{1,0},{2,3},{3,2},{4,5},{5,4},{6,7},{7,6},{8,9},{9,8},{10,11... | collective-permute-start | bytes 73736 | tf_op jit(solution)/shard_map/ppermute | solution.py:628
  42.8 10.0 %collective-permute-start.11 = (f32[3,2,8,128]{3,2,1,0:T(8,128)S(1)}, f32[3,2,8,128]{3,2,1,0:T(8,128)S(1)}, u32[]{:S(2)}, u32[]{:S(2)}) collective-permute-start(f32[3,2,8,128]{3,2,1,0:T(8,128)S(1)} %get-tuple-element.51.refs_8_), channel_id=1, source_target_pairs={{1,2},{2,1},{3,4},{4,3},{5,6},{6,5},{9,10},{10,9},{11,12},{12,11},... | collective-permute-start | bytes 73736 | tf_op jit(solution)/shard_map/ppermute | solution.py:629
  43.5 9.4 %collective-permute-start.9 = (f32[3,104,128]{2,1,0:T(8,128)S(1)}, f32[3,104,128]{2,1,0:T(8,128)S(1)}, u32[]{:S(2)}, u32[]{:S(2)}) collective-permute-start(f32[3,104,128]{2,1,0:T(8,128)S(1)} %get-tuple-element.50), channel_id=1, source_target_pairs={{0,8},{8,0},{1,9},{9,1},{2,10},{10,2},{3,11},{11,3},{4,12},{12,4},... | collective-permute-start | bytes 479240 | tf_op jit(solution)/shard_map/ppermute | solution.py:627
  48.7 12.2 %all-to-all-start.3 = ((f32[32,8,128]{2,1,0:T(8,128)}), f32[32,8,128]{2,1,0:T(8,128)S(1)}, u32[]{:S(2)}, u32[]{:S(2)}) async-start(f32[32,8,128]{2,1,0:T(8,128)} %bitcast.14), calls=%async_computation.3 | async-start | bytes 262144 | tf_op jit(solution)/shard_map/all_to_all | solution.py:603
  52.8 0.8 %copy-start.1 = (f32[4,32,128]{2,1,0:T(8,128)S(1)}, f32[4,32,128]{2,1,0:T(8,128)}, u32[]{:S(2)}) copy-start(f32[4,32,128]{2,1,0:T(8,128)} %copy-done) | copy-start | bytes 196612

commit v4 on v3

--- a/solution.py
+++ b/solution.py
@@ -273,7 +273,7 @@
         fields[n % 3][8 * i : 8 * i + 8] = value
 
 
-def step_kernel(linked, last, *refs):
+def step_kernel(n_gy, linked, last, *refs):
     cur_in, prev_in, coeff, wet, cols, xr, yra, yrb, mine, *refs = refs
     if linked:
         received, *refs = refs
@@ -303,17 +303,19 @@
     for it in range(groups):
         load(it).start()
 
+    within = (q > 0) & (q < n_gy - 1)
+
     @pl.when((q & 1) == 1)
     def _():
         for c in range(3):
             for h in range(2):
-                zs[c, h] = jnp.where(even_lane, yra[c, h], yrb[c, h])
+                zs[c, h] = jnp.where(even_lane, yra[c, h], jnp.where(within, yrb[c, h], 0.0))
 
     @pl.when((q & 1) == 0)
     def _():
         for c in range(3):
             for h in range(2):
-                zs[c, h] = jnp.where(even_lane, yrb[c, h], yra[c, h])
+                zs[c, h] = jnp.where(even_lane, jnp.where(within, yrb[c, h], 0.0), yra[c, h])
 
     there = pl.multiple_of(jnp.where(p == 0, FIRST + ROWS, 0), 8)
     nowhere = pl.multiple_of(jnp.where(p == 0, 0, FIRST + ROWS), 8)
@@ -620,7 +622,7 @@
     received = exchange(payload)
     swap = [(0, 1), (1, 0)]
     inner = [(i, i ^ 1) for i in range(n_gy)]
-    outer = [(i, j) for k in range(1, n_gy - 1, 2) for i, j in ((k, k + 1), (k + 1, k))]
+    outer = [(i, (i + 1 if i % 2 else i - 1) % n_gy) for i in range(n_gy)]
     before = None
     for step in range(STEPS):
         last = step == STEPS - 1
@@ -630,7 +632,7 @@
         operands = [keep(cur), keep(prev), coeff, wet, keep(cols), xr, yra, yrb, sides]
         if before is not None:
             operands.append(before)
-        kernel = functools.partial(step_kernel, before is not None, last)
+        kernel = functools.partial(step_kernel, n_gy, before is not None, last)
         scratch = [
             vmem(sides_shape, F32), vmem((3, TOTAL, CY), F32), vmem(field_shape, F32), vmem((2, ROWS, CY), F32),
             wet_in, dma((ROWS // GROUP + 1,)),

time: 62.4 us -> 56.9 us (0.912)
  waiting for transfers between devices: 11.6 us -> 4.31 us
  starting transfers between devices: 30.7 us -> 32.6 us
    ppermute x4, starting transfers between devices: 2.6 us -> 14.5 us  [on_device(): yrb = lax.ppermute(sides, 'gy', outer)]
    all_to_all x4, starting transfers between devices: 19 us -> 10.3 us  [exchange(): payload = lax.all_to_all(payload, ('sec', 'gx', 'gy'), 0, 0, tiled=True)]
    all_to_all x4, waiting for transfers between devices: 11.5 us -> 3.82 us  [exchange(): payload = lax.all_to_all(payload, ('sec', 'gx', 'gy'), 0, 0, tiled=True)]
    ppermute x4, starting transfers between devices: 8.2 us -> 7.44 us  [on_device(): xr = lax.ppermute(xs, 'gx', swap)]
    ppermute x4, starting transfers between devices: 0.95 us -> 0.32 us  [on_device(): yra = lax.ppermute(sides, 'gy', inner)]
  transfers between devices with their start and end apart: 16 -> 16, of which waited for: 4 -> 4; matrix products, arithmetic and copies ran while one was open for 0% -> 0% of each run, Pallas kernels for 24% -> 27%
where the time goes in v4:
time: 56.9 us; the launch traced here: 56.4 us
  starting transfers between devices  32.6 us (57%)
  Pallas kernels  18.4 us (32%)
  waiting for transfers between devices  4.31 us (8%)
  local copies, waits for them, and re-layouts  0.84 us (1%)
    pallas_call x9, Pallas kernels, call(): pl.pallas_call(kernel, out_shape=[(pltpu.VMEM if kept else jax.ShapeDtype...  18.4 us
    ppermute x4, starting transfers between devices, on_device(): yrb = lax.ppermute(sides, 'gy', outer)  14.5 us
    all_to_all x4, starting transfers between devices, exchange(): payload = lax.all_to_all(payload, ('sec', 'gx', 'gy'), 0, 0, tiled=True)  10.3 us
    ppermute x4, starting transfers between devices, on_device(): xr = lax.ppermute(xs, 'gx', swap)  7.44 us
    all_to_all x4, waiting for transfers between devices, exchange(): payload = lax.all_to_all(payload, ('sec', 'gx', 'gy'), 0, 0, tiled=True)  3.82 us
  transfers between devices with their start and end apart: 16, of which 4 were waited for; matrix products, arithmetic and copies ran while one was open for 0% of the time, Pallas kernels for 27%

profile of v4, /device:TPU:0, one launch (start us, length us, event | category | flops | bytes accessed | tf_op | source)
XLA Modules:
  0.0 56.4 jit_solution(17388855948015428553)
XLA Ops:
  0.0 2.5 %shard_map.73 = (f32[256,128]{1,0:T(8,128)}, f32[4,32,128]{2,1,0:T(8,128)S(1)}, f32[128,128]{1,0:T(8,128)S(1)}, f32[3,800,128]{2,1,0:T(8,128)S(1)}, f32[3,800,12...) custom-call(f32[3,800,128]{2,1,0:T(8,128)} %bitcast.25, f32[3,800,128]{2,1,0:T(8,128)} %bitcast.26, ...), custom_call_target="tpu_custom_call" | custom-call | flops 4000000000 | bytes 4194304 | tf_op jit(solution)/shard_map/pallas_call | solution.py:564
  2.5 0.0 copy-start
  2.5 3.0 %collective-permute-start = (f32[3,104,128]{2,1,0:T(8,128)S(1)}, f32[3,104,128]{2,1,0:T(8,128)S(1)}, u32[]{:S(2)}, u32[]{:S(2)}) collective-permute-start(f32[3,104,128]{2,1,0:T(8,128)S(1)} %get-tuple-element.34), channel_id=1, source_target_pairs={{0,8},{8,0},{1,9},{9,1},{2,10},{10,2},{3,11},{11,3},{4,12},{12,4},... | collective-permute-start | bytes 479240 | tf_op jit(solution)/shard_map/ppermute | solution.py:629
  5.5 0.0 collective-permute-start.1
  5.5 3.7 %collective-permute-start.2 = (f32[3,2,8,128]{3,2,1,0:T(8,128)S(1)}, f32[3,2,8,128]{3,2,1,0:T(8,128)S(1)}, u32[]{:S(2)}, u32[]{:S(2)}) collective-permute-start(f32[3,2,8,128]{3,2,1,0:T(8,128)S(1)} %get-tuple-element.35.refs_8_), channel_id=1, source_target_pairs={{0,7},{1,2},{2,1},{3,4},{4,3},{5,6},{6,5},{7,0},{8,15},{9,10},{10,... | collective-permute-start | bytes 73736 | tf_op jit(solution)/shard_map/ppermute | solution.py:631
  9.2 2.6 %all-to-all-start = ((f32[32,8,128]{2,1,0:T(8,128)}), f32[32,8,128]{2,1,0:T(8,128)S(1)}, u32[]{:S(2)}, u32[]{:S(2)}) async-start(f32[32,8,128]{2,1,0:T(8,128)} %bitcast.8), calls=%async_computation | async-start | bytes 262144 | tf_op jit(solution)/shard_map/all_to_all | solution.py:605
  11.8 0.0 collective-permute-done.1.refs_6_
  11.8 0.0 collective-permute-done.2.refs_7_
  11.9 0.0 collective-permute-done.refs_5_
  11.9 2.9 %shard_map.74 = (f32[3,800,128]{2,1,0:T(8,128)S(1)}, f32[3,800,128]{2,1,0:T(8,128)S(1)}, f32[32,128]{1,0:T(8,128)S(1)}, f32[3,104,128]{2,1,0:T(8,128)S(1)}, f32[...) custom-call(f32[3,800,128]{2,1,0:T(8,128)S(1)} %get-tuple-element.31.refs_0_, ...), custom_call_target="tpu_custom_call", output_to_operand_aliasing={{0}: (0, {}), {1}: (1, {})} | custom-call | flops 64000000000 | bytes 67108864 | tf_op jit(solution)/shard_map/pallas_call | solution.py:564
  14.8 0.2 collective-permute-start.4
  15.0 3.6 %collective-permute-start.5 = (f32[3,2,8,128]{3,2,1,0:T(8,128)S(1)}, f32[3,2,8,128]{3,2,1,0:T(8,128)S(1)}, u32[]{:S(2)}, u32[]{:S(2)}) collective-permute-start(f32[3,2,8,128]{3,2,1,0:T(8,128)S(1)} %get-tuple-element.39.refs_8_), channel_id=1, source_target_pairs={{0,7},{1,2},{2,1},{3,4},{4,3},{5,6},{6,5},{7,0},{8,15},{9,10},{10,... | collective-permute-start | bytes 73736 | tf_op jit(solution)/shard_map/ppermute | solution.py:631
  18.6 1.5 %collective-permute-start.3 = (f32[3,104,128]{2,1,0:T(8,128)S(1)}, f32[3,104,128]{2,1,0:T(8,128)S(1)}, u32[]{:S(2)}, u32[]{:S(2)}) collective-permute-start(f32[3,104,128]{2,1,0:T(8,128)S(1)} %get-tuple-element.38), channel_id=1, source_target_pairs={{0,8},{8,0},{1,9},{9,1},{2,10},{10,2},{3,11},{11,3},{4,12},{12,4},... | collective-permute-start | bytes 479240 | tf_op jit(solution)/shard_map/ppermute | solution.py:629
  20.1 0.0 all-to-all-done
  20.1 1.0 %shard_map.76 = f32[256,128]{1,0:T(8,128)} custom-call(f32[256,128]{1,0:T(8,128)S(1)} %bitcast.20, f32[32,128]{1,0:T(8,128)S(1)} %get-tuple-element.45.base, f32[32,128]{1,0:T(8,128)S(1)} %get-tuple-element.46.scale, f32[4,32,128]{2,1,0:T(8,128)S(1)} %get-tuple-element.33.refs_4_.cols, f32[128,128]{1,0:T(8,128)S(1)} %get-tuple-element.47.pcat), custom_call_target="tpu_custom_call" | custom-call | flops 4000000000 | bytes 4194304 | tf_op jit(solution)/shard_map/pallas_call | solution.py:564
  21.1 2.6 %all-to-all-start.1 = ((f32[32,8,128]{2,1,0:T(8,128)}), f32[32,8,128]{2,1,0:T(8,128)S(1)}, u32[]{:S(2)}, u32[]{:S(2)}) async-start(f32[32,8,128]{2,1,0:T(8,128)} %bitcast.10), calls=%async_computation.1 | async-start | bytes 262144 | tf_op jit(solution)/shard_map/all_to_all | solution.py:605
  23.7 0.0 collective-permute-done.4.refs_6_
  23.7 0.0 collective-permute-done.5.refs_7_
  23.7 0.2 collective-permute-done.3.refs_5_
  23.9 2.9 %shard_map.75 = (f32[3,800,128]{2,1,0:T(8,128)S(1)}, f32[3,800,128]{2,1,0:T(8,128)S(1)}, f32[32,128]{1,0:T(8,128)S(1)}, f32[3,104,128]{2,1,0:T(8,128)S(1)}, f32[3,2,8,128]{3,2,1,0:T(8,128)S(1)}) custom-call(f32[3,800,128]{2,1,0:T(8,128)S(1)} %get-tuple-element.36.refs_0_, ...), custom_call_target="tpu_custom_call", output_to_operand_aliasing={{0}: (0, {}), {1}: (1, {})} | custom-call | flops 64000000000 | bytes 67108864 | tf_op jit(solution)/shard_map/pallas_call | solution.py:564
  26.8 0.1 collective-permute-start.7
  26.8 3.6 %collective-permute-start.8 = (f32[3,2,8,128]{3,2,1,0:T(8,128)S(1)}, f32[3,2,8,128]{3,2,1,0:T(8,128)S(1)}, u32[]{:S(2)}, u32[]{:S(2)}) collective-permute-start(f32[3,2,8,128]{3,2,1,0:T(8,128)S(1)} %get-tuple-element.44.refs_8_), channel_id=1, source_target_pairs={{0,7},{1,2},{2,1},{3,4},{4,3},{5,6},{6,5},{7,0},{8,15},{9,10},{10,... | collective-permute-start | bytes 73736 | tf_op jit(solution)/shard_map/ppermute | solution.py:631
  30.4 1.5 %collective-permute-start.6 = (f32[3,104,128]{2,1,0:T(8,128)S(1)}, f32[3,104,128]{2,1,0:T(8,128)S(1)}, u32[]{:S(2)}, u32[]{:S(2)}) collective-permute-start(f32[3,104,128]{2,1,0:T(8,128)S(1)} %get-tuple-element.43), channel_id=1, source_target_pairs={{0,8},{8,0},{1,9},{9,1},{2,10},{10,2},{3,11},{11,3},{4,12},{12,4},... | collective-permute-start | bytes 479240 | tf_op jit(solution)/shard_map/ppermute | solution.py:629
  31.9 0.0 all-to-all-done.1
  31.9 1.0 %shard_map.78 = f32[256,128]{1,0:T(8,128)} custom-call(f32[256,128]{1,0:T(8,128)S(1)} %bitcast.22, f32[32,128]{1,0:T(8,128)S(1)} %get-tuple-element.52.base, f32[32,128]{1,0:T(8,128)S(1)} %get-tuple-element.46.scale, f32[4,32,128]{2,1,0:T(8,128)S(1)} %get-tuple-element.33.refs_4_.cols, f32[128,128]{1,0:T(8,128)S(1)} %get-tuple-element.47.pcat), custom_call_target="tpu_custom_call" | custom-call | flops 4000000000 | bytes 4194304 | tf_op jit(solution)/shard_map/pallas_call | solution.py:564
  32.9 2.6 %all-to-all-start.2 = ((f32[32,8,128]{2,1,0:T(8,128)}), f32[32,8,128]{2,1,0:T(8,128)S(1)}, u32[]{:S(2)}, u32[]{:S(2)}) async-start(f32[32,8,128]{2,1,0:T(8,128)} %bitcast.12), calls=%async_computation.2 | async-start | bytes 262144 | tf_op jit(solution)/shard_map/all_to_all | solution.py:605
  35.5 0.0 collective-permute-done.7.refs_6_
  35.5 0.0 collective-permute-done.8.refs_7_
  35.6 0.2 collective-permute-done.6.refs_5_
  35.7 2.9 %shard_map.77 = (f32[3,800,128]{2,1,0:T(8,128)S(1)}, f32[3,800,128]{2,1,0:T(8,128)S(1)}, f32[32,128]{1,0:T(8,128)S(1)}, f32[3,104,128]{2,1,0:T(8,128)S(1)}, f32[3,2,8,128]{3,2,1,0:T(8,128)S(1)}) custom-call(f32[3,800,128]{2,1,0:T(8,128)S(1)} %get-tuple-element.41.refs_0_, ...), custom_call_target="tpu_custom_call", output_to_operand_aliasing={{0}: (0, {}), {1}: (1, {})} | custom-call | flops 64000000000 | bytes 67108864 | tf_op jit(solution)/shard_map/pallas_call | solution.py:564
  38.6 0.1 collective-permute-start.10
  38.7 3.6 %collective-permute-start.11 = (f32[3,2,8,128]{3,2,1,0:T(8,128)S(1)}, f32[3,2,8,128]{3,2,1,0:T(8,128)S(1)}, u32[]{:S(2)}, u32[]{:S(2)}) collective-permute-start(f32[3,2,8,128]{3,2,1,0:T(8,128)S(1)} %get-tuple-element.51.refs_8_), channel_id=1, source_target_pairs={{0,7},{1,2},{2,1},{3,4},{4,3},{5,6},{6,5},{7,0},{8,15},{9,10},{10,... | collective-permute-start | bytes 73736 | tf_op jit(solution)/shard_map/ppermute | solution.py:631
  42.3 1.5 %collective-permute-start.9 = (f32[3,104,128]{2,1,0:T(8,128)S(1)}, f32[3,104,128]{2,1,0:T(8,128)S(1)}, u32[]{:S(2)}, u32[]{:S(2)}) collective-permute-start(f32[3,104,128]{2,1,0:T(8,128)S(1)} %get-tuple-element.50), channel_id=1, source_target_pairs={{0,8},{8,0},{1,9},{9,1},{2,10},{10,2},{3,11},{11,3},{4,12},{12,4},... | collective-permute-start | bytes 479240 | tf_op jit(solution)/shard_map/ppermute | solution.py:629
  43.8 0.0 all-to-all-done.2
  43.8 0.0 copy-done
  43.8 1.0 %shard_map.80 = f32[256,128]{1,0:T(8,128)} custom-call(f32[256,128]{1,0:T(8,128)S(1)} %bitcast.18, f32[32,128]{1,0:T(8,128)S(1)} %get-tuple-element.56.base, f32[32,128]{1,0:T(8,128)S(1)} %get-tuple-element.46.scale, f32[4,32,128]{2,1,0:T(8,128)S(1)} %get-tuple-element.33.refs_4_.cols, f32[128,128]{1,0:T(8,128)S(1)} %get-tuple-element.47.pcat), custom_call_target="tpu_custom_call" | custom-call | flops 4000000000 | bytes 4194304 | tf_op jit(solution)/shard_map/pallas_call | solution.py:564
  44.8 2.6 %all-to-all-start.3 = ((f32[32,8,128]{2,1,0:T(8,128)}), f32[32,8,128]{2,1,0:T(8,128)S(1)}, u32[]{:S(2)}, u32[]{:S(2)}) async-start(f32[32,8,128]{2,1,0:T(8,128)} %bitcast.14), calls=%async_computation.3 | async-start | bytes 262144 | tf_op jit(solution)/shard_map/all_to_all | solution.py:605
  47.4 0.0 collective-permute-done.10.refs_6_
  47.4 0.0 collective-permute-done.11.refs_7_
  47.4 0.2 collective-permute-done.9.refs_5_
  47.6 0.0 copy-start.1
  47.6 0.8 %copy-done.1 = f32[4,32,128]{2,1,0:T(8,128)S(1)} copy-done((f32[4,32,128]{2,1,0:T(8,128)S(1)}, f32[4,32,128]{2,1,0:T(8,128)}, u32[]{:S(2)}) %copy-start.1) | copy-done | bytes 65560
  48.4 3.3 %shard_map.79 = (f32[3,800,128]{2,1,0:T(8,128)S(1)}, f32[3,800,128]{2,1,0:T(8,128)S(1)}, f32[3,800,128]{2,1,0:T(8,128)}, s32[800,128]{1,0:T(8,128)S(1)}) custom-call(f32[3,800,128]{2,1,0:T(8,128)S(1)} %get-tuple-element.48.refs_0_, f32[3,800,128]{2,1,0:T(8,128)S(1)} %get-tuple-element.49.refs_1_, ...), custom_call_target="tpu_custom_call", output_to_operand_aliasing={{0}: (0, {}), {1}: (1, {})} | custom-call | flops 64000000000 | bytes 67108864 | tf_op jit(solution)/shard_map/pallas_call | solution.py:564
  51.7 3.8 %all-to-all-done.3 = f32[32,8,128]{2,1,0:T(8,128)S(1)} async-done(((f32[32,8,128]{2,1,0:T(8,128)}), f32[32,8,128]{2,1,0:T(8,128)S(1)}, u32[]{:S(2)}, u32[]{:S(2)}) %all-to-all-start.3) | async-done | bytes 131104 | tf_op jit(solution)/shard_map/all_to_all | solution.py:605
  55.5 0.8 %shard_map.81 = f32[3,800,128]{2,1,0:T(8,128)} custom-call(f32[3,800,128]{2,1,0:T(8,128)} %get-tuple-element.53.final_in, f32[3,800,128]{2,1,0:T(8,128)S(1)} %get-tuple-element.54.fields, s32[800,128]{1,0:T(8,128)S(1)} %get-tuple-element.55.wet, f32[256,128]{1,0:T(8,128)S(1)} %bitcast.24), custom_call_target="tpu_custom_call", output_to_operand_aliasing={{}: (0, {})} | custom-call | flops 4000000000 | bytes 4194304 | tf_op jit(solution)/shard_map/pallas_call | solution.py:564
Async XLA Ops:
  2.5 41.2 %copy-start = (f32[4,32,128]{2,1,0:T(8,128)}, f32[4,32,128]{2,1,0:T(8,128)S(1)}, u32[]{:S(2)}) copy-start(f32[4,32,128]{2,1,0:T(8,128)S(1)} %get-tuple-element.33.refs_4_.cols) | copy-start | bytes 196612
  2.5 9.3 %collective-permute-start = (f32[3,104,128]{2,1,0:T(8,128)S(1)}, f32[3,104,128]{2,1,0:T(8,128)S(1)}, u32[]{:S(2)}, u32[]{:S(2)}) collective-permute-start(f32[3,104,128]{2,1,0:T(8,128)S(1)} %get-tuple-element.34), channel_id=1, source_target_pairs={{0,8},{8,0},{1,9},{9,1},{2,10},{10,2},{3,11},{11,3},{4,12},{12,4},... | collective-permute-start | bytes 479240 | tf_op jit(solution)/shard_map/ppermute | solution.py:629
  5.5 6.3 %collective-permute-start.1 = (f32[3,2,8,128]{3,2,1,0:T(8,128)S(1)}, f32[3,2,8,128]{3,2,1,0:T(8,128)S(1)}, u32[]{:S(2)}, u32[]{:S(2)}) collective-permute-start(f32[3,2,8,128]{3,2,1,0:T(8,128)S(1)} %get-tuple-element.35.refs_8_), channel_id=1, source_target_pairs={{0,1},{1,0},{2,3},{3,2},{4,5},{5,4},{6,7},{7,6},{8,9},{9,8},{10,11... | collective-permute-start | bytes 73736 | tf_op jit(solution)/shard_map/ppermute | solution.py:630
  5.5 6.3 %collective-permute-start.2 = (f32[3,2,8,128]{3,2,1,0:T(8,128)S(1)}, f32[3,2,8,128]{3,2,1,0:T(8,128)S(1)}, u32[]{:S(2)}, u32[]{:S(2)}) collective-permute-start(f32[3,2,8,128]{3,2,1,0:T(8,128)S(1)} %get-tuple-element.35.refs_8_), channel_id=1, source_target_pairs={{0,7},{1,2},{2,1},{3,4},{4,3},{5,6},{6,5},{7,0},{8,15},{9,10},{10,... | collective-permute-start | bytes 73736 | tf_op jit(solution)/shard_map/ppermute | solution.py:631
  9.2 10.8 %all-to-all-start = ((f32[32,8,128]{2,1,0:T(8,128)}), f32[32,8,128]{2,1,0:T(8,128)S(1)}, u32[]{:S(2)}, u32[]{:S(2)}) async-start(f32[32,8,128]{2,1,0:T(8,128)} %bitcast.8), calls=%async_computation | async-start | bytes 262144 | tf_op jit(solution)/shard_map/all_to_all | solution.py:605
  14.8 8.9 %collective-permute-start.4 = (f32[3,2,8,128]{3,2,1,0:T(8,128)S(1)}, f32[3,2,8,128]{3,2,1,0:T(8,128)S(1)}, u32[]{:S(2)}, u32[]{:S(2)}) collective-permute-start(f32[3,2,8,128]{3,2,1,0:T(8,128)S(1)} %get-tuple-element.39.refs_8_), channel_id=1, source_target_pairs={{0,1},{1,0},{2,3},{3,2},{4,5},{5,4},{6,7},{7,6},{8,9},{9,8},{10,11... | collective-permute-start | bytes 73736 | tf_op jit(solution)/shard_map/ppermute | solution.py:630
  15.0 8.7 %collective-permute-start.5 = (f32[3,2,8,128]{3,2,1,0:T(8,128)S(1)}, f32[3,2,8,128]{3,2,1,0:T(8,128)S(1)}, u32[]{:S(2)}, u32[]{:S(2)}) collective-permute-start(f32[3,2,8,128]{3,2,1,0:T(8,128)S(1)} %get-tuple-element.39.refs_8_), channel_id=1, source_target_pairs={{0,7},{1,2},{2,1},{3,4},{4,3},{5,6},{6,5},{7,0},{8,15},{9,10},{10,... | collective-permute-start | bytes 73736 | tf_op jit(solution)/shard_map/ppermute | solution.py:631
  18.6 5.3 %collective-permute-start.3 = (f32[3,104,128]{2,1,0:T(8,128)S(1)}, f32[3,104,128]{2,1,0:T(8,128)S(1)}, u32[]{:S(2)}, u32[]{:S(2)}) collective-permute-start(f32[3,104,128]{2,1,0:T(8,128)S(1)} %get-tuple-element.38), channel_id=1, source_target_pairs={{0,8},{8,0},{1,9},{9,1},{2,10},{10,2},{3,11},{11,3},{4,12},{12,4},... | collective-permute-start | bytes 479240 | tf_op jit(solution)/shard_map/ppermute | solution.py:629
  21.1 10.8 %all-to-all-start.1 = ((f32[32,8,128]{2,1,0:T(8,128)}), f32[32,8,128]{2,1,0:T(8,128)S(1)}, u32[]{:S(2)}, u32[]{:S(2)}) async-start(f32[32,8,128]{2,1,0:T(8,128)} %bitcast.10), calls=%async_computation.1 | async-start | bytes 262144 | tf_op jit(solution)/shard_map/all_to_all | solution.py:605
  26.8 8.8 %collective-permute-start.7 = (f32[3,2,8,128]{3,2,1,0:T(8,128)S(1)}, f32[3,2,8,128]{3,2,1,0:T(8,128)S(1)}, u32[]{:S(2)}, u32[]{:S(2)}) collective-permute-start(f32[3,2,8,128]{3,2,1,0:T(8,128)S(1)} %get-tuple-element.44.refs_8_), channel_id=1, source_target_pairs={{0,1},{1,0},{2,3},{3,2},{4,5},{5,4},{6,7},{7,6},{8,9},{9,8},{10,11... | collective-permute-start | bytes 73736 | tf_op jit(solution)/shard_map/ppermute | solution.py:630
  26.8 8.7 %collective-permute-start.8 = (f32[3,2,8,128]{3,2,1,0:T(8,128)S(1)}, f32[3,2,8,128]{3,2,1,0:T(8,128)S(1)}, u32[]{:S(2)}, u32[]{:S(2)}) collective-permute-start(f32[3,2,8,128]{3,2,1,0:T(8,128)S(1)} %get-tuple-element.44.refs_8_), channel_id=1, source_target_pairs={{0,7},{1,2},{2,1},{3,4},{4,3},{5,6},{6,5},{7,0},{8,15},{9,10},{10,... | collective-permute-start | bytes 73736 | tf_op jit(solution)/shard_map/ppermute | solution.py:631
  30.4 5.3 %collective-permute-start.6 = (f32[3,104,128]{2,1,0:T(8,128)S(1)}, f32[3,104,128]{2,1,0:T(8,128)S(1)}, u32[]{:S(2)}, u32[]{:S(2)}) collective-permute-start(f32[3,104,128]{2,1,0:T(8,128)S(1)} %get-tuple-element.43), channel_id=1, source_target_pairs={{0,8},{8,0},{1,9},{9,1},{2,10},{10,2},{3,11},{11,3},{4,12},{12,4},... | collective-permute-start | bytes 479240 | tf_op jit(solution)/shard_map/ppermute | solution.py:629
  32.9 10.8 %all-to-all-start.2 = ((f32[32,8,128]{2,1,0:T(8,128)}), f32[32,8,128]{2,1,0:T(8,128)S(1)}, u32[]{:S(2)}, u32[]{:S(2)}) async-start(f32[32,8,128]{2,1,0:T(8,128)} %bitcast.12), calls=%async_computation.2 | async-start | bytes 262144 | tf_op jit(solution)/shard_map/all_to_all | solution.py:605
  38.6 8.8 %collective-permute-start.10 = (f32[3,2,8,128]{3,2,1,0:T(8,128)S(1)}, f32[3,2,8,128]{3,2,1,0:T(8,128)S(1)}, u32[]{:S(2)}, u32[]{:S(2)}) collective-permute-start(f32[3,2,8,128]{3,2,1,0:T(8,128)S(1)} %get-tuple-element.51.refs_8_), channel_id=1, source_target_pairs={{0,1},{1,0},{2,3},{3,2},{4,5},{5,4},{6,7},{7,6},{8,9},{9,8},{10,11... | collective-permute-start | bytes 73736 | tf_op jit(solution)/shard_map/ppermute | solution.py:630
  38.7 8.7 %collective-permute-start.11 = (f32[3,2,8,128]{3,2,1,0:T(8,128)S(1)}, f32[3,2,8,128]{3,2,1,0:T(8,128)S(1)}, u32[]{:S(2)}, u32[]{:S(2)}) collective-permute-start(f32[3,2,8,128]{3,2,1,0:T(8,128)S(1)} %get-tuple-element.51.refs_8_), channel_id=1, source_target_pairs={{0,7},{1,2},{2,1},{3,4},{4,3},{5,6},{6,5},{7,0},{8,15},{9,10},{10,... | collective-permute-start | bytes 73736 | tf_op jit(solution)/shard_map/ppermute | solution.py:631
  42.3 5.3 %collective-permute-start.9 = (f32[3,104,128]{2,1,0:T(8,128)S(1)}, f32[3,104,128]{2,1,0:T(8,128)S(1)}, u32[]{:S(2)}, u32[]{:S(2)}) collective-permute-start(f32[3,104,128]{2,1,0:T(8,128)S(1)} %get-tuple-element.50), channel_id=1, source_target_pairs={{0,8},{8,0},{1,9},{9,1},{2,10},{10,2},{3,11},{11,3},{4,12},{12,4},... | collective-permute-start | bytes 479240 | tf_op jit(solution)/shard_map/ppermute | solution.py:629
  44.8 10.8 %all-to-all-start.3 = ((f32[32,8,128]{2,1,0:T(8,128)}), f32[32,8,128]{2,1,0:T(8,128)S(1)}, u32[]{:S(2)}, u32[]{:S(2)}) async-start(f32[32,8,128]{2,1,0:T(8,128)} %bitcast.14), calls=%async_computation.3 | async-start | bytes 262144 | tf_op jit(solution)/shard_map/all_to_all | solution.py:605
  47.6 0.8 %copy-start.1 = (f32[4,32,128]{2,1,0:T(8,128)S(1)}, f32[4,32,128]{2,1,0:T(8,128)}, u32[]{:S(2)}) copy-start(f32[4,32,128]{2,1,0:T(8,128)} %copy-done) | copy-start | bytes 196612

commit v5 on v4

--- a/solution.py
+++ b/solution.py
@@ -18,8 +18,8 @@
 FIRST = 104
 TOTAL = FIRST + ROWS + FIRST
 SLOTS = 8
-BLOCKS = 20
-BATCH = 4
+BLOCKS = 25
+BATCH = 5
 GROUP = 8 * BLOCKS
 HALF = ROWS // 16
 F32 = jnp.float32
@@ -512,10 +512,11 @@
 
 def fine_addend(addend):
     lane = iota((8, CY), 1)
+    sources = [((lane + k * CY) * 6554) >> 16 for k in range(REFINE)]
     for m in range(FINE // 8):
         rows = addend[8 * m : 8 * m + 8]
         for k in range(REFINE):
-            fine = jnp.take_along_axis(rows, ((lane + k * CY) * 6554) >> 16, axis=1)
+            fine = jnp.take_along_axis(rows, sources[k], axis=1)
             yield 8 * REFINE * m + k, fine
 
 

time: 56.9 us -> 56.7 us (level)
  transfers between devices with their start and end apart: 16 -> 16, of which waited for: 4 -> 4; matrix products, arithmetic and copies ran while one was open for 0% -> 0% of each run, Pallas kernels for 27% -> 26%
where the time goes in v5:
time: 56.7 us; the launch traced here: 56.2 us
  starting transfers between devices  32.6 us (57%)
  Pallas kernels  18.2 us (32%)
  waiting for transfers between devices  4.37 us (8%)
  local copies, waits for them, and re-layouts  0.84 us (1%)
    pallas_call x9, Pallas kernels, call(): pl.pallas_call(kernel, out_shape=[(pltpu.VMEM if kept else jax.ShapeDtype...  18.2 us
    ppermute x4, starting transfers between devices, on_device(): yrb = lax.ppermute(sides, 'gy', outer)  14.5 us
    all_to_all x4, starting transfers between devices, exchange(): payload = lax.all_to_all(payload, ('sec', 'gx', 'gy'), 0, 0, tiled=True)  10.3 us
    ppermute x4, starting transfers between devices, on_device(): xr = lax.ppermute(xs, 'gx', swap)  7.44 us
    all_to_all x4, waiting for transfers between devices, exchange(): payload = lax.all_to_all(payload, ('sec', 'gx', 'gy'), 0, 0, tiled=True)  3.89 us
  transfers between devices with their start and end apart: 16, of which 4 were waited for; matrix products, arithmetic and copies ran while one was open for 0% of the time, Pallas kernels for 26%

profile of v5, /device:TPU:0, one launch (start us, length us, event | category | flops | bytes accessed | tf_op | source)
XLA Modules:
  0.0 56.2 jit_solution(13246524249074424759)
XLA Ops:
  0.0 2.5 %shard_map.73 = (f32[256,128]{1,0:T(8,128)}, f32[4,32,128]{2,1,0:T(8,128)S(1)}, f32[128,128]{1,0:T(8,128)S(1)}, f32[3,800,128]{2,1,0:T(8,128)S(1)}, f32[3,800,12...) custom-call(f32[3,800,128]{2,1,0:T(8,128)} %bitcast.25, f32[3,800,128]{2,1,0:T(8,128)} %bitcast.26, ...), custom_call_target="tpu_custom_call" | custom-call | flops 4000000000 | bytes 4194304 | tf_op jit(solution)/shard_map/pallas_call | solution.py:565
  2.5 0.0 copy-start
  2.5 3.0 %collective-permute-start = (f32[3,104,128]{2,1,0:T(8,128)S(1)}, f32[3,104,128]{2,1,0:T(8,128)S(1)}, u32[]{:S(2)}, u32[]{:S(2)}) collective-permute-start(f32[3,104,128]{2,1,0:T(8,128)S(1)} %get-tuple-element.34), channel_id=1, source_target_pairs={{0,8},{8,0},{1,9},{9,1},{2,10},{10,2},{3,11},{11,3},{4,12},{12,4},... | collective-permute-start | bytes 479240 | tf_op jit(solution)/shard_map/ppermute | solution.py:630
  5.5 0.0 collective-permute-start.1
  5.5 3.7 %collective-permute-start.2 = (f32[3,2,8,128]{3,2,1,0:T(8,128)S(1)}, f32[3,2,8,128]{3,2,1,0:T(8,128)S(1)}, u32[]{:S(2)}, u32[]{:S(2)}) collective-permute-start(f32[3,2,8,128]{3,2,1,0:T(8,128)S(1)} %get-tuple-element.35.refs_8_), channel_id=1, source_target_pairs={{0,7},{1,2},{2,1},{3,4},{4,3},{5,6},{6,5},{7,0},{8,15},{9,10},{10,... | collective-permute-start | bytes 73736 | tf_op jit(solution)/shard_map/ppermute | solution.py:632
  9.2 2.6 %all-to-all-start = ((f32[32,8,128]{2,1,0:T(8,128)}), f32[32,8,128]{2,1,0:T(8,128)S(1)}, u32[]{:S(2)}, u32[]{:S(2)}) async-start(f32[32,8,128]{2,1,0:T(8,128)} %bitcast.8), calls=%async_computation | async-start | bytes 262144 | tf_op jit(solution)/shard_map/all_to_all | solution.py:606
  11.8 0.0 collective-permute-done.1.refs_6_
  11.8 0.0 collective-permute-done.2.refs_7_
  11.9 0.0 collective-permute-done.refs_5_
  11.9 2.9 %shard_map.74 = (f32[3,800,128]{2,1,0:T(8,128)S(1)}, f32[3,800,128]{2,1,0:T(8,128)S(1)}, f32[32,128]{1,0:T(8,128)S(1)}, f32[3,104,128]{2,1,0:T(8,128)S(1)}, f32[...) custom-call(f32[3,800,128]{2,1,0:T(8,128)S(1)} %get-tuple-element.31.refs_0_, ...), custom_call_target="tpu_custom_call", output_to_operand_aliasing={{0}: (0, {}), {1}: (1, {})} | custom-call | flops 64000000000 | bytes 67108864 | tf_op jit(solution)/shard_map/pallas_call | solution.py:565
  14.7 0.2 collective-permute-start.4
  14.9 3.6 %collective-permute-start.5 = (f32[3,2,8,128]{3,2,1,0:T(8,128)S(1)}, f32[3,2,8,128]{3,2,1,0:T(8,128)S(1)}, u32[]{:S(2)}, u32[]{:S(2)}) collective-permute-start(f32[3,2,8,128]{3,2,1,0:T(8,128)S(1)} %get-tuple-element.39.refs_8_), channel_id=1, source_target_pairs={{0,7},{1,2},{2,1},{3,4},{4,3},{5,6},{6,5},{7,0},{8,15},{9,10},{10,... | collective-permute-start | bytes 73736 | tf_op jit(solution)/shard_map/ppermute | solution.py:632
  18.5 1.5 %collective-permute-start.3 = (f32[3,104,128]{2,1,0:T(8,128)S(1)}, f32[3,104,128]{2,1,0:T(8,128)S(1)}, u32[]{:S(2)}, u32[]{:S(2)}) collective-permute-start(f32[3,104,128]{2,1,0:T(8,128)S(1)} %get-tuple-element.38), channel_id=1, source_target_pairs={{0,8},{8,0},{1,9},{9,1},{2,10},{10,2},{3,11},{11,3},{4,12},{12,4},... | collective-permute-start | bytes 479240 | tf_op jit(solution)/shard_map/ppermute | solution.py:630
  20.0 0.0 all-to-all-done
  20.0 1.0 %shard_map.76 = f32[256,128]{1,0:T(8,128)} custom-call(f32[256,128]{1,0:T(8,128)S(1)} %bitcast.20, f32[32,128]{1,0:T(8,128)S(1)} %get-tuple-element.45.base, f32[32,128]{1,0:T(8,128)S(1)} %get-tuple-element.46.scale, f32[4,32,128]{2,1,0:T(8,128)S(1)} %get-tuple-element.33.refs_4_.cols, f32[128,128]{1,0:T(8,128)S(1)} %get-tuple-element.47.pcat), custom_call_target="tpu_custom_call" | custom-call | flops 4000000000 | bytes 4194304 | tf_op jit(solution)/shard_map/pallas_call | solution.py:565
  21.0 2.6 %all-to-all-start.1 = ((f32[32,8,128]{2,1,0:T(8,128)}), f32[32,8,128]{2,1,0:T(8,128)S(1)}, u32[]{:S(2)}, u32[]{:S(2)}) async-start(f32[32,8,128]{2,1,0:T(8,128)} %bitcast.10), calls=%async_computation.1 | async-start | bytes 262144 | tf_op jit(solution)/shard_map/all_to_all | solution.py:606
  23.6 0.0 collective-permute-done.4.refs_6_
  23.6 0.0 collective-permute-done.5.refs_7_
  23.7 0.2 collective-permute-done.3.refs_5_
  23.8 2.8 %shard_map.75 = (f32[3,800,128]{2,1,0:T(8,128)S(1)}, f32[3,800,128]{2,1,0:T(8,128)S(1)}, f32[32,128]{1,0:T(8,128)S(1)}, f32[3,104,128]{2,1,0:T(8,128)S(1)}, f32[3,2,8,128]{3,2,1,0:T(8,128)S(1)}) custom-call(f32[3,800,128]{2,1,0:T(8,128)S(1)} %get-tuple-element.36.refs_0_, ...), custom_call_target="tpu_custom_call", output_to_operand_aliasing={{0}: (0, {}), {1}: (1, {})} | custom-call | flops 64000000000 | bytes 67108864 | tf_op jit(solution)/shard_map/pallas_call | solution.py:565
  26.7 0.1 collective-permute-start.7
  26.7 3.6 %collective-permute-start.8 = (f32[3,2,8,128]{3,2,1,0:T(8,128)S(1)}, f32[3,2,8,128]{3,2,1,0:T(8,128)S(1)}, u32[]{:S(2)}, u32[]{:S(2)}) collective-permute-start(f32[3,2,8,128]{3,2,1,0:T(8,128)S(1)} %get-tuple-element.44.refs_8_), channel_id=1, source_target_pairs={{0,7},{1,2},{2,1},{3,4},{4,3},{5,6},{6,5},{7,0},{8,15},{9,10},{10,... | collective-permute-start | bytes 73736 | tf_op jit(solution)/shard_map/ppermute | solution.py:632
  30.3 1.5 %collective-permute-start.6 = (f32[3,104,128]{2,1,0:T(8,128)S(1)}, f32[3,104,128]{2,1,0:T(8,128)S(1)}, u32[]{:S(2)}, u32[]{:S(2)}) collective-permute-start(f32[3,104,128]{2,1,0:T(8,128)S(1)} %get-tuple-element.43), channel_id=1, source_target_pairs={{0,8},{8,0},{1,9},{9,1},{2,10},{10,2},{3,11},{11,3},{4,12},{12,4},... | collective-permute-start | bytes 479240 | tf_op jit(solution)/shard_map/ppermute | solution.py:630
  31.8 0.0 all-to-all-done.1
  31.8 1.0 %shard_map.78 = f32[256,128]{1,0:T(8,128)} custom-call(f32[256,128]{1,0:T(8,128)S(1)} %bitcast.22, f32[32,128]{1,0:T(8,128)S(1)} %get-tuple-element.52.base, f32[32,128]{1,0:T(8,128)S(1)} %get-tuple-element.46.scale, f32[4,32,128]{2,1,0:T(8,128)S(1)} %get-tuple-element.33.refs_4_.cols, f32[128,128]{1,0:T(8,128)S(1)} %get-tuple-element.47.pcat), custom_call_target="tpu_custom_call" | custom-call | flops 4000000000 | bytes 4194304 | tf_op jit(solution)/shard_map/pallas_call | solution.py:565
  32.8 2.6 %all-to-all-start.2 = ((f32[32,8,128]{2,1,0:T(8,128)}), f32[32,8,128]{2,1,0:T(8,128)S(1)}, u32[]{:S(2)}, u32[]{:S(2)}) async-start(f32[32,8,128]{2,1,0:T(8,128)} %bitcast.12), calls=%async_computation.2 | async-start | bytes 262144 | tf_op jit(solution)/shard_map/all_to_all | solution.py:606
  35.4 0.0 collective-permute-done.7.refs_6_
  35.4 0.0 collective-permute-done.8.refs_7_
  35.5 0.2 collective-permute-done.6.refs_5_
  35.6 2.8 %shard_map.77 = (f32[3,800,128]{2,1,0:T(8,128)S(1)}, f32[3,800,128]{2,1,0:T(8,128)S(1)}, f32[32,128]{1,0:T(8,128)S(1)}, f32[3,104,128]{2,1,0:T(8,128)S(1)}, f32[3,2,8,128]{3,2,1,0:T(8,128)S(1)}) custom-call(f32[3,800,128]{2,1,0:T(8,128)S(1)} %get-tuple-element.41.refs_0_, ...), custom_call_target="tpu_custom_call", output_to_operand_aliasing={{0}: (0, {}), {1}: (1, {})} | custom-call | flops 64000000000 | bytes 67108864 | tf_op jit(solution)/shard_map/pallas_call | solution.py:565
  38.4 0.1 collective-permute-start.10
  38.5 3.6 %collective-permute-start.11 = (f32[3,2,8,128]{3,2,1,0:T(8,128)S(1)}, f32[3,2,8,128]{3,2,1,0:T(8,128)S(1)}, u32[]{:S(2)}, u32[]{:S(2)}) collective-permute-start(f32[3,2,8,128]{3,2,1,0:T(8,128)S(1)} %get-tuple-element.51.refs_8_), channel_id=1, source_target_pairs={{0,7},{1,2},{2,1},{3,4},{4,3},{5,6},{6,5},{7,0},{8,15},{9,10},{10,... | collective-permute-start | bytes 73736 | tf_op jit(solution)/shard_map/ppermute | solution.py:632
  42.1 1.5 %collective-permute-start.9 = (f32[3,104,128]{2,1,0:T(8,128)S(1)}, f32[3,104,128]{2,1,0:T(8,128)S(1)}, u32[]{:S(2)}, u32[]{:S(2)}) collective-permute-start(f32[3,104,128]{2,1,0:T(8,128)S(1)} %get-tuple-element.50), channel_id=1, source_target_pairs={{0,8},{8,0},{1,9},{9,1},{2,10},{10,2},{3,11},{11,3},{4,12},{12,4},... | collective-permute-start | bytes 479240 | tf_op jit(solution)/shard_map/ppermute | solution.py:630
  43.6 0.0 all-to-all-done.2
  43.6 0.0 copy-done
  43.6 1.0 %shard_map.80 = f32[256,128]{1,0:T(8,128)} custom-call(f32[256,128]{1,0:T(8,128)S(1)} %bitcast.18, f32[32,128]{1,0:T(8,128)S(1)} %get-tuple-element.56.base, f32[32,128]{1,0:T(8,128)S(1)} %get-tuple-element.46.scale, f32[4,32,128]{2,1,0:T(8,128)S(1)} %get-tuple-element.33.refs_4_.cols, f32[128,128]{1,0:T(8,128)S(1)} %get-tuple-element.47.pcat), custom_call_target="tpu_custom_call" | custom-call | flops 4000000000 | bytes 4194304 | tf_op jit(solution)/shard_map/pallas_call | solution.py:565
  44.6 2.6 %all-to-all-start.3 = ((f32[32,8,128]{2,1,0:T(8,128)}), f32[32,8,128]{2,1,0:T(8,128)S(1)}, u32[]{:S(2)}, u32[]{:S(2)}) async-start(f32[32,8,128]{2,1,0:T(8,128)} %bitcast.14), calls=%async_computation.3 | async-start | bytes 262144 | tf_op jit(solution)/shard_map/all_to_all | solution.py:606
  47.2 0.0 collective-permute-done.10.refs_6_
  47.2 0.0 collective-permute-done.11.refs_7_
  47.2 0.2 collective-permute-done.9.refs_5_
  47.4 0.0 copy-start.1
  47.4 0.8 %copy-done.1 = f32[4,32,128]{2,1,0:T(8,128)S(1)} copy-done((f32[4,32,128]{2,1,0:T(8,128)S(1)}, f32[4,32,128]{2,1,0:T(8,128)}, u32[]{:S(2)}) %copy-start.1) | copy-done | bytes 65560
  48.2 3.3 %shard_map.79 = (f32[3,800,128]{2,1,0:T(8,128)S(1)}, f32[3,800,128]{2,1,0:T(8,128)S(1)}, f32[3,800,128]{2,1,0:T(8,128)}, s32[800,128]{1,0:T(8,128)S(1)}) custom-call(f32[3,800,128]{2,1,0:T(8,128)S(1)} %get-tuple-element.48.refs_0_, f32[3,800,128]{2,1,0:T(8,128)S(1)} %get-tuple-element.49.refs_1_, ...), custom_call_target="tpu_custom_call", output_to_operand_aliasing={{0}: (0, {}), {1}: (1, {})} | custom-call | flops 64000000000 | bytes 67108864 | tf_op jit(solution)/shard_map/pallas_call | solution.py:565
  51.5 3.9 %all-to-all-done.3 = f32[32,8,128]{2,1,0:T(8,128)S(1)} async-done(((f32[32,8,128]{2,1,0:T(8,128)}), f32[32,8,128]{2,1,0:T(8,128)S(1)}, u32[]{:S(2)}, u32[]{:S(2)}) %all-to-all-start.3) | async-done | bytes 131104 | tf_op jit(solution)/shard_map/all_to_all | solution.py:606
  55.4 0.8 %shard_map.81 = f32[3,800,128]{2,1,0:T(8,128)} custom-call(f32[3,800,128]{2,1,0:T(8,128)} %get-tuple-element.53.final_in, f32[3,800,128]{2,1,0:T(8,128)S(1)} %get-tuple-element.54.fields, s32[800,128]{1,0:T(8,128)S(1)} %get-tuple-element.55.wet, f32[256,128]{1,0:T(8,128)S(1)} %bitcast.24), custom_call_target="tpu_custom_call", output_to_operand_aliasing={{}: (0, {})} | custom-call | flops 4000000000 | bytes 4194304 | tf_op jit(solution)/shard_map/pallas_call | solution.py:565
Async XLA Ops:
  2.5 41.1 %copy-start = (f32[4,32,128]{2,1,0:T(8,128)}, f32[4,32,128]{2,1,0:T(8,128)S(1)}, u32[]{:S(2)}) copy-start(f32[4,32,128]{2,1,0:T(8,128)S(1)} %get-tuple-element.33.refs_4_.cols) | copy-start | bytes 196612
  2.5 9.3 %collective-permute-start = (f32[3,104,128]{2,1,0:T(8,128)S(1)}, f32[3,104,128]{2,1,0:T(8,128)S(1)}, u32[]{:S(2)}, u32[]{:S(2)}) collective-permute-start(f32[3,104,128]{2,1,0:T(8,128)S(1)} %get-tuple-element.34), channel_id=1, source_target_pairs={{0,8},{8,0},{1,9},{9,1},{2,10},{10,2},{3,11},{11,3},{4,12},{12,4},... | collective-permute-start | bytes 479240 | tf_op jit(solution)/shard_map/ppermute | solution.py:630
  5.5 6.3 %collective-permute-start.1 = (f32[3,2,8,128]{3,2,1,0:T(8,128)S(1)}, f32[3,2,8,128]{3,2,1,0:T(8,128)S(1)}, u32[]{:S(2)}, u32[]{:S(2)}) collective-permute-start(f32[3,2,8,128]{3,2,1,0:T(8,128)S(1)} %get-tuple-element.35.refs_8_), channel_id=1, source_target_pairs={{0,1},{1,0},{2,3},{3,2},{4,5},{5,4},{6,7},{7,6},{8,9},{9,8},{10,11... | collective-permute-start | bytes 73736 | tf_op jit(solution)/shard_map/ppermute | solution.py:631
  5.5 6.3 %collective-permute-start.2 = (f32[3,2,8,128]{3,2,1,0:T(8,128)S(1)}, f32[3,2,8,128]{3,2,1,0:T(8,128)S(1)}, u32[]{:S(2)}, u32[]{:S(2)}) collective-permute-start(f32[3,2,8,128]{3,2,1,0:T(8,128)S(1)} %get-tuple-element.35.refs_8_), channel_id=1, source_target_pairs={{0,7},{1,2},{2,1},{3,4},{4,3},{5,6},{6,5},{7,0},{8,15},{9,10},{10,... | collective-permute-start | bytes 73736 | tf_op jit(solution)/shard_map/ppermute | solution.py:632
  9.2 10.8 %all-to-all-start = ((f32[32,8,128]{2,1,0:T(8,128)}), f32[32,8,128]{2,1,0:T(8,128)S(1)}, u32[]{:S(2)}, u32[]{:S(2)}) async-start(f32[32,8,128]{2,1,0:T(8,128)} %bitcast.8), calls=%async_computation | async-start | bytes 262144 | tf_op jit(solution)/shard_map/all_to_all | solution.py:606
  14.7 8.9 %collective-permute-start.4 = (f32[3,2,8,128]{3,2,1,0:T(8,128)S(1)}, f32[3,2,8,128]{3,2,1,0:T(8,128)S(1)}, u32[]{:S(2)}, u32[]{:S(2)}) collective-permute-start(f32[3,2,8,128]{3,2,1,0:T(8,128)S(1)} %get-tuple-element.39.refs_8_), channel_id=1, source_target_pairs={{0,1},{1,0},{2,3},{3,2},{4,5},{5,4},{6,7},{7,6},{8,9},{9,8},{10,11... | collective-permute-start | bytes 73736 | tf_op jit(solution)/shard_map/ppermute | solution.py:631
  14.9 8.7 %collective-permute-start.5 = (f32[3,2,8,128]{3,2,1,0:T(8,128)S(1)}, f32[3,2,8,128]{3,2,1,0:T(8,128)S(1)}, u32[]{:S(2)}, u32[]{:S(2)}) collective-permute-start(f32[3,2,8,128]{3,2,1,0:T(8,128)S(1)} %get-tuple-element.39.refs_8_), channel_id=1, source_target_pairs={{0,7},{1,2},{2,1},{3,4},{4,3},{5,6},{6,5},{7,0},{8,15},{9,10},{10,... | collective-permute-start | bytes 73736 | tf_op jit(solution)/shard_map/ppermute | solution.py:632
  18.5 5.3 %collective-permute-start.3 = (f32[3,104,128]{2,1,0:T(8,128)S(1)}, f32[3,104,128]{2,1,0:T(8,128)S(1)}, u32[]{:S(2)}, u32[]{:S(2)}) collective-permute-start(f32[3,104,128]{2,1,0:T(8,128)S(1)} %get-tuple-element.38), channel_id=1, source_target_pairs={{0,8},{8,0},{1,9},{9,1},{2,10},{10,2},{3,11},{11,3},{4,12},{12,4},... | collective-permute-start | bytes 479240 | tf_op jit(solution)/shard_map/ppermute | solution.py:630
  21.0 10.8 %all-to-all-start.1 = ((f32[32,8,128]{2,1,0:T(8,128)}), f32[32,8,128]{2,1,0:T(8,128)S(1)}, u32[]{:S(2)}, u32[]{:S(2)}) async-start(f32[32,8,128]{2,1,0:T(8,128)} %bitcast.10), calls=%async_computation.1 | async-start | bytes 262144 | tf_op jit(solution)/shard_map/all_to_all | solution.py:606
  26.7 8.8 %collective-permute-start.7 = (f32[3,2,8,128]{3,2,1,0:T(8,128)S(1)}, f32[3,2,8,128]{3,2,1,0:T(8,128)S(1)}, u32[]{:S(2)}, u32[]{:S(2)}) collective-permute-start(f32[3,2,8,128]{3,2,1,0:T(8,128)S(1)} %get-tuple-element.44.refs_8_), channel_id=1, source_target_pairs={{0,1},{1,0},{2,3},{3,2},{4,5},{5,4},{6,7},{7,6},{8,9},{9,8},{10,11... | collective-permute-start | bytes 73736 | tf_op jit(solution)/shard_map/ppermute | solution.py:631
  26.7 8.7 %collective-permute-start.8 = (f32[3,2,8,128]{3,2,1,0:T(8,128)S(1)}, f32[3,2,8,128]{3,2,1,0:T(8,128)S(1)}, u32[]{:S(2)}, u32[]{:S(2)}) collective-permute-start(f32[3,2,8,128]{3,2,1,0:T(8,128)S(1)} %get-tuple-element.44.refs_8_), channel_id=1, source_target_pairs={{0,7},{1,2},{2,1},{3,4},{4,3},{5,6},{6,5},{7,0},{8,15},{9,10},{10,... | collective-permute-start | bytes 73736 | tf_op jit(solution)/shard_map/ppermute | solution.py:632
  30.3 5.3 %collective-permute-start.6 = (f32[3,104,128]{2,1,0:T(8,128)S(1)}, f32[3,104,128]{2,1,0:T(8,128)S(1)}, u32[]{:S(2)}, u32[]{:S(2)}) collective-permute-start(f32[3,104,128]{2,1,0:T(8,128)S(1)} %get-tuple-element.43), channel_id=1, source_target_pairs={{0,8},{8,0},{1,9},{9,1},{2,10},{10,2},{3,11},{11,3},{4,12},{12,4},... | collective-permute-start | bytes 479240 | tf_op jit(solution)/shard_map/ppermute | solution.py:630
  32.8 10.8 %all-to-all-start.2 = ((f32[32,8,128]{2,1,0:T(8,128)}), f32[32,8,128]{2,1,0:T(8,128)S(1)}, u32[]{:S(2)}, u32[]{:S(2)}) async-start(f32[32,8,128]{2,1,0:T(8,128)} %bitcast.12), calls=%async_computation.2 | async-start | bytes 262144 | tf_op jit(solution)/shard_map/all_to_all | solution.py:606
  38.4 8.8 %collective-permute-start.10 = (f32[3,2,8,128]{3,2,1,0:T(8,128)S(1)}, f32[3,2,8,128]{3,2,1,0:T(8,128)S(1)}, u32[]{:S(2)}, u32[]{:S(2)}) collective-permute-start(f32[3,2,8,128]{3,2,1,0:T(8,128)S(1)} %get-tuple-element.51.refs_8_), channel_id=1, source_target_pairs={{0,1},{1,0},{2,3},{3,2},{4,5},{5,4},{6,7},{7,6},{8,9},{9,8},{10,11... | collective-permute-start | bytes 73736 | tf_op jit(solution)/shard_map/ppermute | solution.py:631
  38.5 8.7 %collective-permute-start.11 = (f32[3,2,8,128]{3,2,1,0:T(8,128)S(1)}, f32[3,2,8,128]{3,2,1,0:T(8,128)S(1)}, u32[]{:S(2)}, u32[]{:S(2)}) collective-permute-start(f32[3,2,8,128]{3,2,1,0:T(8,128)S(1)} %get-tuple-element.51.refs_8_), channel_id=1, source_target_pairs={{0,7},{1,2},{2,1},{3,4},{4,3},{5,6},{6,5},{7,0},{8,15},{9,10},{10,... | collective-permute-start | bytes 73736 | tf_op jit(solution)/shard_map/ppermute | solution.py:632
  42.1 5.3 %collective-permute-start.9 = (f32[3,104,128]{2,1,0:T(8,128)S(1)}, f32[3,104,128]{2,1,0:T(8,128)S(1)}, u32[]{:S(2)}, u32[]{:S(2)}) collective-permute-start(f32[3,104,128]{2,1,0:T(8,128)S(1)} %get-tuple-element.50), channel_id=1, source_target_pairs={{0,8},{8,0},{1,9},{9,1},{2,10},{10,2},{3,11},{11,3},{4,12},{12,4},... | collective-permute-start | bytes 479240 | tf_op jit(solution)/shard_map/ppermute | solution.py:630
  44.6 10.8 %all-to-all-start.3 = ((f32[32,8,128]{2,1,0:T(8,128)}), f32[32,8,128]{2,1,0:T(8,128)S(1)}, u32[]{:S(2)}, u32[]{:S(2)}) async-start(f32[32,8,128]{2,1,0:T(8,128)} %bitcast.14), calls=%async_computation.3 | async-start | bytes 262144 | tf_op jit(solution)/shard_map/all_to_all | solution.py:606
  47.4 0.8 %copy-start.1 = (f32[4,32,128]{2,1,0:T(8,128)S(1)}, f32[4,32,128]{2,1,0:T(8,128)}, u32[]{:S(2)}) copy-start(f32[4,32,128]{2,1,0:T(8,128)} %copy-done) | copy-start | bytes 196612
